TPU v7x, 256 devices: a whole 4x4x8 slice. The times are simulated.
256 devices in a mesh: head: 4 (over y_lo, core), space: 16 (over y_hi, z), tm: 4 (over x).
Axes of the slice: x: 4, y: 4 (y_hi: 2, y_lo: 2; y = y_hi * 2 + y_lo), z: 8, core: 2. Of those that a mesh axis runs over, the one named last changes fastest.
Arguments:
- query: bfloat16 [16384, 2560], P(('space', 'tm'), 'head'), may hold values from -6 to 6
- key: bfloat16 [16384, 2560], P(('space', 'tm'), 'head'), may hold values from -6 to 6
- value: bfloat16 [16384, 2560], P(('space', 'tm'), 'head'), may hold values from -6 to 6
- tile_coords: int32 [3, 256], replicated, may hold values from 0 to 15, as said below
- windows: int32 [3, 20], P(None, 'head'), may hold values from 0 to 2, as said below
Outputs:
- attended: bfloat16 [16384, 2560], P(('space', 'tm'), 'head')
Inputs may be any that keep to these rules, and one draw needn't show every extreme that they name: `tile_coords`: the device at position (s, t) of space and tm holds the tiles with frame coordinates t * 2 to (t + 1) * 2 - 1, all 2 height coordinates, and the single column (offset + sign * s) mod 16, for one offset and one sign of +1 or -1; its 4 tiles are stored in any order. windows[0, h] <= 2, windows[1, h] <= 1 and windows[2, h] <= 1 for every head; each of the three bounds is reached by some head.
All inputs are finite; a program needn't handle non-finite values.
Results may differ from a plain program's by a relative error of at most 0.007.
Values may be sent and summed in bfloat16 or wider, within the bound.
No kernel may reach another device: no remote copies, remote signals or barrier semaphores. Data moves between devices by JAX's collectives and lax.ppermute only.
A program may use at most 64 MiB of HBM per device.

v0:
```python
import functools

import jax
import jax.numpy as jnp
from jax import lax
from jax.experimental import pallas as pl
from jax.experimental.pallas import tpu as pltpu
from jax.sharding import PartitionSpec as P

TILE = 64
HEAD = 128
MASKED = -1e30
FLOOR = -1e29
FACTOR = 1.4426950408889634 * HEAD**-0.5
PARTS = 3
SPARE = 16
NEAR, FAR = 0, 1


def partner(index, side, count):
    step = 1 - 2 * (index % 2)
    return (index + (step if side == NEAR else -step)) % count


def exchange(block, axis, side):
    count = lax.axis_size(axis)
    return lax.ppermute(block, axis, [(i, partner(i, side, count)) for i in range(count)])


def shift(block, axis, distance):
    count = lax.axis_size(axis)
    return lax.ppermute(block, axis, [(i, (i + distance) % count) for i in range(count)])


def call(kernel, out_shape, flops, *operands, exps=0, moved=1 << 20):
    return pl.pallas_call(
        kernel,
        out_shape=out_shape,
        compiler_params=pltpu.CompilerParams(vmem_limit_bytes=40 * 1024 * 1024),
        cost_estimate=pl.CostEstimate(flops=flops, bytes_accessed=moved, transcendentals=exps),
    )(*operands)


def turn_kernel(v, out):
    for h in range(v.shape[1] // HEAD):
        lanes = slice(h * HEAD, (h + 1) * HEAD)
        out[lanes, :] = v[:, lanes].astype(jnp.float32).T.astype(jnp.bfloat16)


def weigh_kernel(heads, q, key, key_near, key_far, bias, weights_out, stats_out):
    stats_out[...] = jnp.zeros(stats_out.shape, jnp.float32)
    tiles = key.shape[0] // TILE
    for h in range(heads):
        lanes = slice(h * HEAD, (h + 1) * HEAD)
        blocks, peak = [], None
        for j, keys in enumerate((key, key_near, key_far)):
            raw = lax.dot_general(
                keys[:, lanes], q[:, lanes], (((1,), (1,)), ((), ())),
                preferred_element_type=jnp.float32,
            )
            for i in range(tiles):
                row = (h * 3 + j) * tiles + i
                block = raw[i * TILE : (i + 1) * TILE] + bias[row : row + 1, :]
                blocks.append(block)
                peak = block if peak is None else jnp.maximum(peak, block)
        peak = jnp.maximum(jnp.max(peak, axis=0, keepdims=True), FLOOR)
        total = None
        for i, block in enumerate(blocks):
            weights = jnp.exp2((block - peak) * FACTOR)
            weights_out[h, i * TILE : (i + 1) * TILE, :] = weights.astype(jnp.bfloat16)
            total = weights if total is None else total + weights
        total = jnp.maximum(jnp.sum(total, axis=0, keepdims=True), 0.5)
        stats_out[h : h + 1, :] = 1.0 / total
        stats_out[8 + h : 9 + h, :] = peak * FACTOR + jnp.log2(total)


def weighted(h, weights, stats, values):
    rows = slice(h * HEAD, (h + 1) * HEAD)
    width = values[0].shape[1]
    summed = None
    for j, turned in enumerate(values):
        part = jnp.dot(
            turned[rows, :], weights[h, j * width : (j + 1) * width, :],
            preferred_element_type=jnp.float32,
        )
        summed = part if summed is None else summed + part
    return summed * stats[h : h + 1, :]


def visitors_kernel(heads, weights, stats, v, v_near, v_far, out):
    end = heads * HEAD
    for h in range(heads):
        out[h * HEAD : (h + 1) * HEAD, :] = weighted(
            h, weights, stats, (v, v_near, v_far)
        ).astype(jnp.bfloat16)
    rest = stats[8:16, :]
    pieces = []
    for part in range(PARTS):
        piece = rest.astype(jnp.bfloat16).astype(jnp.float32)
        rest = rest - piece
        pieces.append(piece[0:heads])
    pieces.append(jnp.zeros((SPARE - PARTS * heads, rest.shape[1]), jnp.float32))
    out[end : end + SPARE, :] = jnp.concatenate(pieces, axis=0).astype(jnp.bfloat16)


def home_kernel(heads, weights, stats, v, v_near, v_far, out):
    for h in range(heads):
        out[h * HEAD : (h + 1) * HEAD, :] = weighted(h, weights, stats, (v, v_near, v_far))


def combine_kernel(heads, own, stats, last, next_, out):
    end = heads * HEAD
    own_level = stats[8 : 8 + heads, :]

    def level(ref):
        spare = ref[end : end + SPARE, :].astype(jnp.float32)
        return spare[0:heads] + spare[heads : 2 * heads] + spare[2 * heads : 3 * heads]

    last_level, next_level = level(last), level(next_)
    top = jnp.maximum(own_level, jnp.maximum(last_level, next_level))
    parts = [jnp.exp2(x - top) for x in (own_level, last_level, next_level)]
    scale = 1.0 / (parts[0] + parts[1] + parts[2])
    parts = [part * scale for part in parts]
    for h in range(heads):
        rows = slice(h * HEAD, (h + 1) * HEAD)
        result = own[rows, :] * parts[0][h : h + 1]
        result = result + last[rows, :].astype(jnp.float32) * parts[1][h : h + 1]
        result = result + next_[rows, :].astype(jnp.float32) * parts[2][h : h + 1]
        out[:, rows] = result.T.astype(jnp.bfloat16)


def tile_bias(tile_coords, windows, per_device):
    space_count, tm_count = lax.axis_size("space"), lax.axis_size("tm")
    s, t = lax.axis_index("space"), lax.axis_index("tm")

    def tiles(column, slab):
        device = column * tm_count + slab
        return lax.dynamic_slice_in_dim(tile_coords, device * per_device, per_device, 1)

    slabs = [t, partner(t, NEAR, tm_count), partner(t, FAR, tm_count)]
    columns = [s, (s + 1) % space_count, (s - 1) % space_count]
    key_tiles = jnp.concatenate([tiles(s, slab) for slab in slabs], axis=1)
    queries = jnp.stack([tiles(column, t) for column in columns], axis=1)
    queries = jnp.repeat(queries, TILE, axis=2)
    gap = jnp.abs(key_tiles[:, None, :, None] - queries[:, :, None, :])
    allowed = jnp.all(gap[:, :, None] <= windows[:, None, :, None, None], axis=0)
    bias = jnp.where(allowed, 0.0, MASKED).astype(jnp.float32)
    return [bias[i].reshape(-1, bias.shape[-1]) for i in range(3)]


def shards(query, key, value, tile_coords, windows):
    heads = windows.shape[1]
    rows = query.shape[0]
    width = heads * HEAD
    f32, bf16 = jnp.float32, jnp.bfloat16
    pair = 2 * rows * HEAD * rows

    k_near = exchange(key, "tm", NEAR)
    k_far = exchange(key, "tm", FAR)
    turned = call(turn_kernel, jax.ShapeDtypeStruct((width, rows), bf16), 0, value)
    v_near = exchange(turned, "tm", NEAR)
    v_far = exchange(turned, "tm", FAR)
    q_next = shift(query, "space", -1)
    late, _ = lax.optimization_barrier((query, k_near))
    q_last = shift(late, "space", 1)
    bias = tile_bias(tile_coords, windows, rows // TILE)

    def weigh(q, table):
        return call(
            functools.partial(weigh_kernel, heads),
            (
                jax.ShapeDtypeStruct((heads, 3 * rows, rows), bf16),
                jax.ShapeDtypeStruct((16, rows), f32),
            ),
            heads * 3 * pair, q, key, k_near, k_far, table, exps=heads * 3 * rows * rows,
        )

    def visitors(weights, stats):
        return call(
            functools.partial(visitors_kernel, heads),
            jax.ShapeDtypeStruct((width + SPARE, rows), bf16), heads * 3 * pair,
            weights, stats, turned, v_near, v_far,
        )

    next_weights = weigh(q_next, bias[1])
    last_weights = weigh(q_last, bias[2])
    own_weights, own_stats = weigh(query, bias[0])
    from_last = shift(visitors(*next_weights), "space", 1)
    from_next = shift(visitors(*last_weights), "space", -1)
    own = call(
        functools.partial(home_kernel, heads), jax.ShapeDtypeStruct((width, rows), f32),
        heads * 3 * pair, own_weights, own_stats, turned, v_near, v_far,
    )
    return call(
        functools.partial(combine_kernel, heads), jax.ShapeDtypeStruct((rows, width), bf16), 0,
        own, own_stats, from_last, from_next,
    )


def solution(mesh):
    placed = (
        P(("space", "tm"), "head"),
        P(("space", "tm"), "head"),
        P(("space", "tm"), "head"),
        P(),
        P(None, "head"),
    )
    return jax.shard_map(
        shards, mesh=mesh, in_specs=placed, out_specs=P(("space", "tm"), "head"), check_vma=False
    )
```

profile of v0, /device:TPU:6, one launch (start us, length us, event | category | flops | bytes accessed | tf_op | source)
XLA Modules:
  0.0 39.8 jit_solution(6259659501893322769)
XLA Ops:
  0.0 0.8 %collective-permute-start = (bf16[256,640]{1,0:T(8,128)(2,1)}, bf16[256,640]{1,0:T(8,128)(2,1)S(1)}, u32[]{:S(2)}, u32[]{:S(2)}) collective-permute-start(bf16[256,640]{1,0:T(8,128)(2,1)} %key.5), channel_id=1, source_target_pairs={{0,1},{1,0},{2,3},{3,2},{4,5},{5,4},{6,7},{7,6},{8,9},{9,8},{10,11... | collective-permute-start | bytes 983048 | tf_op jit(solution)/shard_map/ppermute | solution.py:27
  0.8 1.4 %collective-permute-start.1 = (bf16[256,640]{1,0:T(8,128)(2,1)}, bf16[256,640]{1,0:T(8,128)(2,1)S(1)}, u32[]{:S(2)}, u32[]{:S(2)}) collective-permute-start(bf16[256,640]{1,0:T(8,128)(2,1)} %key.5), channel_id=1, source_target_pairs={{0,3},{1,2},{2,1},{3,0},{4,7},{5,6},{6,5},{7,4},{8,11},{9,10},{10,... | collective-permute-start | bytes 983048 | tf_op jit(solution)/shard_map/ppermute | solution.py:27
  2.2 0.0 copy-start
  2.2 1.0 %copy-done = bf16[256,640]{1,0:T(8,128)(2,1)S(1)} copy-done((bf16[256,640]{1,0:T(8,128)(2,1)S(1)}, bf16[256,640]{1,0:T(8,128)(2,1)}, u32[]{:S(2)}) %copy-start) | copy-done | bytes 327704
  3.2 0.0 copy-start.2
  3.2 0.2 shard_map.56.v
  3.4 1.5 %collective-permute-start.2 = (bf16[640,256]{1,0:T(8,128)(2,1)S(1)}, bf16[640,256]{1,0:T(8,128)(2,1)S(1)}, u32[]{:S(2)}, u32[]{:S(2)}) collective-permute-start(bf16[640,256]{1,0:T(8,128)(2,1)S(1)} %shard_map.56.v), channel_id=1, source_target_pairs={{0,1},{1,0},{2,3},{3,2},{4,5},{5,4},{6,7},{7,6},{8,9},{9,8},{10,11... | collective-permute-start | bytes 983048 | tf_op jit(solution)/shard_map/ppermute | solution.py:27
  4.9 1.0 %collective-permute-start.3 = (bf16[640,256]{1,0:T(8,128)(2,1)S(1)}, bf16[640,256]{1,0:T(8,128)(2,1)S(1)}, u32[]{:S(2)}, u32[]{:S(2)}) collective-permute-start(bf16[640,256]{1,0:T(8,128)(2,1)S(1)} %shard_map.56.v), channel_id=1, source_target_pairs={{0,3},{1,2},{2,1},{3,0},{4,7},{5,6},{6,5},{7,4},{8,11},{9,10},{10,... | collective-permute-start | bytes 983048 | tf_op jit(solution)/shard_map/ppermute | solution.py:27
  5.9 8.5 %collective-permute-start.4 = (bf16[256,640]{1,0:T(8,128)(2,1)}, bf16[256,640]{1,0:T(8,128)(2,1)S(1)}, u32[]{:S(2)}, u32[]{:S(2)}) collective-permute-start(bf16[256,640]{1,0:T(8,128)(2,1)} %q.1), channel_id=1, source_target_pairs={{0,60},{4,0},{8,4},{12,8},{16,12},{20,16},{24,20},{28,24},{32,28},... | collective-permute-start | bytes 983048 | tf_op jit(solution)/shard_map/ppermute | solution.py:32
  14.4 0.9 %constant_dynamic-slice_fusion.1 = (s32[3,4]{1,0:T(4,128)S(1)}, s32[3,4]{1,0:T(4,128)S(1)}, s32[3,4]{1,0:T(4,128)S(1)}, s32[3,1,4]{2,0,1:T(4,128)S(1)}, s32[3,1,4]{2,0,1:T(4,128)S(1)}) fusion(s32[3,256]{1,0:T(4,128)} %param.8, s32[]{:T(128)S(6)} %select_n.48, s32[]{:T(128)S(6)} %select_n.50, s32[]{:T(128)S(6)} %select_n.45, s32[]{:T(128)S(6)} %select_n.54, ...), kind=kLoop, calls=%fused_computation.8 | loop fusion | bytes 500 | tf_op jit(solution)/shard_map/dynamic_slice | solution.py:138
  15.3 0.1 broadcast_in_dim.14
  15.4 0.1 sub.29
  15.5 0.1 pad_add_fusion.1
  15.5 0.1 subtract_abs_fusion
  15.6 0.8 %compare_reduce_fusion = pred[3,5,12,256]{3,2,1,0:T(8,128)(4,1)S(1)} fusion(s32[3,5]{1,0:T(4,128)} %param.9, s32[3,3,12,256]{3,2,1,0:T(8,128)S(1)} %subtract_abs_fusion), kind=kLoop, calls=%fused_computation | loop fusion | flops 230400 | bytes 156732 | tf_op jit(solution)/shard_map/reduce_and | solution.py:146
  16.5 0.0 collective-permute-done.key_near
  16.5 0.1 collective-permute-start.6
  16.7 0.0 collective-permute-done.1.key_far
  16.7 0.0 copy-start.3
  16.7 3.8 %collective-permute-done.4.q = bf16[256,640]{1,0:T(8,128)(2,1)S(1)} collective-permute-done((bf16[256,640]{1,0:T(8,128)(2,1)}, bf16[256,640]{1,0:T(8,128)(2,1)S(1)}, u32[]{:S(2)}, u32[]{:S(2)}) %collective-permute-start.4) | collective-permute-done | bytes 327712 | tf_op jit(solution)/shard_map/ppermute | solution.py:32
  20.5 0.0 copy-done.2
  20.5 1.3 %shard_map.58 = (bf16[5,768,256]{2,1,0:T(8,128)(2,1)S(1)}, f32[16,256]{1,0:T(8,128)S(1)}) custom-call(bf16[256,640]{1,0:T(8,128)(2,1)S(1)} %collective-permute-done.4.q, bf16[256,640]{1,0:T(8,128)(2,1)S(1)} %copy-done.2, bf16[256,640]{1,0:T(8,128)(2,1)S(1)} %collective-permute-done.key_near, bf16[256,640]{1,0:T(8,128)(2,1)S(1)} %collective-permute-done.1.key_far, ...), custom_call_target="tpu_custom_call" | custom-call | flops 251658240 | bytes 1048576 | tf_op jit(solution)/shard_map/pallas_call | solution.py:36
  21.9 0.0 collective-permute-done.2.v_near
  21.9 0.0 collective-permute-done.3.v_far
  21.9 0.4 %shard_map.59 = bf16[656,256]{1,0:T(8,128)(2,1)S(1)} custom-call(bf16[5,768,256]{2,1,0:T(8,128)(2,1)S(1)} %get-tuple-element.14.weights, f32[16,256]{1,0:T(8,128)S(1)} %get-tuple-element.15.stats, bf16[640,256]{1,0:T(8,128)(2,1)S(1)} %shard_map.56.v, bf16[640,256]{1,0:T(8,128)(2,1)S(1)} %collective-permute-done.2.v_near, ...), custom_call_target="tpu_custom_call" | custom-call | flops 251658240 | bytes 1048576 | tf_op jit(solution)/shard_map/pallas_call | solution.py:36
  22.4 0.1 collective-permute-start.5
  22.5 7.3 %collective-permute-done.6.q = bf16[256,640]{1,0:T(8,128)(2,1)S(1)} collective-permute-done((bf16[256,640]{1,0:T(8,128)(2,1)}, bf16[256,640]{1,0:T(8,128)(2,1)S(1)}, u32[]{:S(2)}, u32[]{:S(2)}) %collective-permute-start.6) | collective-permute-done | bytes 327712 | tf_op jit(solution)/shard_map/ppermute | solution.py:32
  29.8 0.0 copy-done.3
  29.8 1.3 %shard_map.60 = (bf16[5,768,256]{2,1,0:T(8,128)(2,1)S(1)}, f32[16,256]{1,0:T(8,128)S(1)}) custom-call(bf16[256,640]{1,0:T(8,128)(2,1)S(1)} %collective-permute-done.6.q, bf16[256,640]{1,0:T(8,128)(2,1)S(1)} %copy-done.2, bf16[256,640]{1,0:T(8,128)(2,1)S(1)} %collective-permute-done.key_near, bf16[256,640]{1,0:T(8,128)(2,1)S(1)} %collective-permute-done.1.key_far, ...), custom_call_target="tpu_custom_call" | custom-call | flops 251658240 | bytes 1048576 | tf_op jit(solution)/shard_map/pallas_call | solution.py:36
  31.1 0.0 copy-start.1
  31.1 0.4 %shard_map.61 = bf16[656,256]{1,0:T(8,128)(2,1)S(1)} custom-call(bf16[5,768,256]{2,1,0:T(8,128)(2,1)S(1)} %get-tuple-element.17.weights, f32[16,256]{1,0:T(8,128)S(1)} %get-tuple-element.18.stats, bf16[640,256]{1,0:T(8,128)(2,1)S(1)} %shard_map.56.v, bf16[640,256]{1,0:T(8,128)(2,1)S(1)} %collective-permute-done.2.v_near, ...), custom_call_target="tpu_custom_call" | custom-call | flops 251658240 | bytes 1048576 | tf_op jit(solution)/shard_map/pallas_call | solution.py:36
  31.6 0.1 collective-permute-start.7
  31.7 0.4 %copy-done.1 = bf16[256,640]{1,0:T(8,128)(2,1)S(1)} copy-done((bf16[256,640]{1,0:T(8,128)(2,1)S(1)}, bf16[256,640]{1,0:T(8,128)(2,1)}, u32[]{:S(2)}) %copy-start.1) | copy-done | bytes 327704
  32.1 0.0 copy-start.4
  32.1 1.0 %copy-done.4 = bf16[256,640]{1,0:T(8,128)(2,1)S(1)} copy-done((bf16[256,640]{1,0:T(8,128)(2,1)S(1)}, bf16[256,640]{1,0:T(8,128)(2,1)}, u32[]{:S(2)}) %copy-start.4) | copy-done | bytes 327704
  33.1 1.3 %shard_map.55 = (bf16[5,768,256]{2,1,0:T(8,128)(2,1)S(1)}, f32[16,256]{1,0:T(8,128)S(1)}) custom-call(bf16[256,640]{1,0:T(8,128)(2,1)S(1)} %copy-done.1, bf16[256,640]{1,0:T(8,128)(2,1)S(1)} %copy-done.2, bf16[256,640]{1,0:T(8,128)(2,1)S(1)} %collective-permute-done.key_near, bf16[256,640]{1,0:T(8,128)(2,1)S(1)} %copy-done.4, f32[60,256]{1,0:T(8,128)S(1)} %reshape_squeeze.9.bias), custom_call_target="tpu_custom_call" | custom-call | flops 251658240 | bytes 1048576 | tf_op jit(solution)/shard_map/pallas_call | solution.py:36
  34.4 0.4 %shard_map.57.own = f32[640,256]{1,0:T(8,128)S(1)} custom-call(bf16[5,768,256]{2,1,0:T(8,128)(2,1)S(1)} %get-tuple-element.12.weights, f32[16,256]{1,0:T(8,128)S(1)} %get-tuple-element.13.stats, bf16[640,256]{1,0:T(8,128)(2,1)S(1)} %shard_map.56.v, bf16[640,256]{1,0:T(8,128)(2,1)S(1)} %collective-permute-done.2.v_near, ...), custom_call_target="tpu_custom_call" | custom-call | flops 251658240 | bytes 1048576 | tf_op jit(solution)/shard_map/pallas_call | solution.py:36
  34.9 0.8 %collective-permute-done.5.last = bf16[656,256]{1,0:T(8,128)(2,1)S(1)} collective-permute-done((bf16[656,256]{1,0:T(8,128)(2,1)S(1)}, bf16[656,256]{1,0:T(8,128)(2,1)S(1)}, u32[]{:S(2)}, u32[]{:S(2)}) %collective-permute-start.5) | collective-permute-done | bytes 335904 | tf_op jit(solution)/shard_map/ppermute | solution.py:32
  35.7 3.2 %collective-permute-done.7.next_ = bf16[656,256]{1,0:T(8,128)(2,1)S(1)} collective-permute-done((bf16[656,256]{1,0:T(8,128)(2,1)S(1)}, bf16[656,256]{1,0:T(8,128)(2,1)S(1)}, u32[]{:S(2)}, u32[]{:S(2)}) %collective-permute-start.7) | collective-permute-done | bytes 335904 | tf_op jit(solution)/shard_map/ppermute | solution.py:32
  38.8 1.0 %shard_map.62 = bf16[256,640]{1,0:T(8,128)(2,1)} custom-call(f32[640,256]{1,0:T(8,128)S(1)} %shard_map.57.own, f32[16,256]{1,0:T(8,128)S(1)} %get-tuple-element.13.stats, bf16[656,256]{1,0:T(8,128)(2,1)S(1)} %collective-permute-done.5.last, bf16[656,256]{1,0:T(8,128)(2,1)S(1)} %collective-permute-done.7.next_), custom_call_target="tpu_custom_call" | custom-call | bytes 1048576 | tf_op jit(solution)/shard_map/pallas_call | solution.py:36
  (7 shorter events, 0.1 us)
Async XLA Ops:
  0.0 16.5 %collective-permute-start = (bf16[256,640]{1,0:T(8,128)(2,1)}, bf16[256,640]{1,0:T(8,128)(2,1)S(1)}, u32[]{:S(2)}, u32[]{:S(2)}) collective-permute-start(bf16[256,640]{1,0:T(8,128)(2,1)} %key.5), channel_id=1, source_target_pairs={{0,1},{1,0},{2,3},{3,2},{4,5},{5,4},{6,7},{7,6},{8,9},{9,8},{10,11... | collective-permute-start | bytes 983048 | tf_op jit(solution)/shard_map/ppermute | solution.py:27
  0.8 15.9 %collective-permute-start.1 = (bf16[256,640]{1,0:T(8,128)(2,1)}, bf16[256,640]{1,0:T(8,128)(2,1)S(1)}, u32[]{:S(2)}, u32[]{:S(2)}) collective-permute-start(bf16[256,640]{1,0:T(8,128)(2,1)} %key.5), channel_id=1, source_target_pairs={{0,3},{1,2},{2,1},{3,0},{4,7},{5,6},{6,5},{7,4},{8,11},{9,10},{10,... | collective-permute-start | bytes 983048 | tf_op jit(solution)/shard_map/ppermute | solution.py:27
  2.2 1.0 %copy-start = (bf16[256,640]{1,0:T(8,128)(2,1)S(1)}, bf16[256,640]{1,0:T(8,128)(2,1)}, u32[]{:S(2)}) copy-start(bf16[256,640]{1,0:T(8,128)(2,1)} %v.1) | copy-start | bytes 983044
  3.2 17.4 %copy-start.2 = (bf16[256,640]{1,0:T(8,128)(2,1)S(1)}, bf16[256,640]{1,0:T(8,128)(2,1)}, u32[]{:S(2)}) copy-start(bf16[256,640]{1,0:T(8,128)(2,1)} %key.5) | copy-start | bytes 983044
  3.4 18.5 %collective-permute-start.2 = (bf16[640,256]{1,0:T(8,128)(2,1)S(1)}, bf16[640,256]{1,0:T(8,128)(2,1)S(1)}, u32[]{:S(2)}, u32[]{:S(2)}) collective-permute-start(bf16[640,256]{1,0:T(8,128)(2,1)S(1)} %shard_map.56.v), channel_id=1, source_target_pairs={{0,1},{1,0},{2,3},{3,2},{4,5},{5,4},{6,7},{7,6},{8,9},{9,8},{10,11... | collective-permute-start | bytes 983048 | tf_op jit(solution)/shard_map/ppermute | solution.py:27
  4.9 17.0 %collective-permute-start.3 = (bf16[640,256]{1,0:T(8,128)(2,1)S(1)}, bf16[640,256]{1,0:T(8,128)(2,1)S(1)}, u32[]{:S(2)}, u32[]{:S(2)}) collective-permute-start(bf16[640,256]{1,0:T(8,128)(2,1)S(1)} %shard_map.56.v), channel_id=1, source_target_pairs={{0,3},{1,2},{2,1},{3,0},{4,7},{5,6},{6,5},{7,4},{8,11},{9,10},{10,... | collective-permute-start | bytes 983048 | tf_op jit(solution)/shard_map/ppermute | solution.py:27
  5.9 14.7 %collective-permute-start.4 = (bf16[256,640]{1,0:T(8,128)(2,1)}, bf16[256,640]{1,0:T(8,128)(2,1)S(1)}, u32[]{:S(2)}, u32[]{:S(2)}) collective-permute-start(bf16[256,640]{1,0:T(8,128)(2,1)} %q.1), channel_id=1, source_target_pairs={{0,60},{4,0},{8,4},{12,8},{16,12},{20,16},{24,20},{28,24},{32,28},... | collective-permute-start | bytes 983048 | tf_op jit(solution)/shard_map/ppermute | solution.py:32
  16.5 13.3 %collective-permute-start.6 = (bf16[256,640]{1,0:T(8,128)(2,1)}, bf16[256,640]{1,0:T(8,128)(2,1)S(1)}, u32[]{:S(2)}, u32[]{:S(2)}) collective-permute-start(bf16[256,640]{1,0:T(8,128)(2,1)} %q.1), channel_id=1, source_target_pairs={{0,4},{4,8},{8,12},{12,16},{16,20},{20,24},{24,28},{28,32},{32,36}... | collective-permute-start | bytes 983048 | tf_op jit(solution)/shard_map/ppermute | solution.py:32
  16.7 13.1 %copy-start.3 = (bf16[256,640]{1,0:T(8,128)(2,1)}, bf16[256,640]{1,0:T(8,128)(2,1)S(1)}, u32[]{:S(2)}) copy-start(bf16[256,640]{1,0:T(8,128)(2,1)S(1)} %collective-permute-done.1.key_far) | copy-start | bytes 983044
  22.4 13.3 %collective-permute-start.5 = (bf16[656,256]{1,0:T(8,128)(2,1)S(1)}, bf16[656,256]{1,0:T(8,128)(2,1)S(1)}, u32[]{:S(2)}, u32[]{:S(2)}) collective-permute-start(bf16[656,256]{1,0:T(8,128)(2,1)S(1)} %shard_map.59), channel_id=1, source_target_pairs={{0,4},{4,8},{8,12},{12,16},{16,20},{20,24},{24,28},{28,32},{32,36}... | collective-permute-start | bytes 1007624 | tf_op jit(solution)/shard_map/ppermute | solution.py:32
  31.1 1.0 %copy-start.1 = (bf16[256,640]{1,0:T(8,128)(2,1)S(1)}, bf16[256,640]{1,0:T(8,128)(2,1)}, u32[]{:S(2)}) copy-start(bf16[256,640]{1,0:T(8,128)(2,1)} %q.1) | copy-start | bytes 983044
  31.6 7.2 %collective-permute-start.7 = (bf16[656,256]{1,0:T(8,128)(2,1)S(1)}, bf16[656,256]{1,0:T(8,128)(2,1)S(1)}, u32[]{:S(2)}, u32[]{:S(2)}) collective-permute-start(bf16[656,256]{1,0:T(8,128)(2,1)S(1)} %shard_map.61), channel_id=1, source_target_pairs={{0,60},{4,0},{8,4},{12,8},{16,12},{20,16},{24,20},{28,24},{32,28},... | collective-permute-start | bytes 1007624 | tf_op jit(solution)/shard_map/ppermute | solution.py:32
  32.1 1.0 %copy-start.4 = (bf16[256,640]{1,0:T(8,128)(2,1)S(1)}, bf16[256,640]{1,0:T(8,128)(2,1)}, u32[]{:S(2)}) copy-start(bf16[256,640]{1,0:T(8,128)(2,1)} %copy-done.3) | copy-start | bytes 983044
where the time goes:
time: 40.1 us; the launch traced here: 39.8 us
  waiting for transfers between devices  15.1 us (38%)
  starting transfers between devices  13.5 us (34%)
  Pallas kernels  6.48 us (16%)
  local copies, waits for them, and re-layouts  3.49 us (9%)
  other arithmetic  1.05 us (3%)
    ppermute x4, waiting for transfers between devices, shift(): lax.ppermute(block, axis, [(i, (i + distance) % count) for i in range(cou...  15.1 us
    ppermute x4, starting transfers between devices, shift(): lax.ppermute(block, axis, [(i, (i + distance) % count) for i in range(cou...  8.74 us
    pallas_call x8, Pallas kernels, call(): pl.pallas_call(kernel, out_shape=out_shape, compiler_params=pltpu.Compile...  6.48 us
    ppermute x4, starting transfers between devices, exchange(): lax.ppermute(block, axis, [(i, partner(i, side, count)) for i in range(co...  4.74 us
    unnamed x10, local copies, waits for them, and re-layouts  2.38 us
    dynamic_slice x1, local copies, waits for them, and re-layouts, tiles(): lax.dynamic_slice_in_dim(tile_coords, device * per_device, per_device, 1)  0.9 us
    reduce_and x1, other arithmetic, tile_bias(): jnp.all(gap[:, :, None] <= windows[:, None, :, None, None], axis=0)  0.84 us
  transfers between devices with their start and end apart: 8, of which 4 were waited for; matrix products, arithmetic and copies ran while one was open for 5% of the time, Pallas kernels for 14%

commit v1 on v0

--- a/solution.py
+++ b/solution.py
@@ -27,9 +27,8 @@
     return lax.ppermute(block, axis, [(i, partner(i, side, count)) for i in range(count)])
 
 
-def shift(block, axis, distance):
-    count = lax.axis_size(axis)
-    return lax.ppermute(block, axis, [(i, (i + distance) % count) for i in range(count)])
+def after(block, other):
+    return lax.optimization_barrier((block, other))[0]
 
 
 def call(kernel, out_shape, flops, *operands, exps=0, moved=1 << 20):
@@ -108,24 +107,35 @@
         out[h * HEAD : (h + 1) * HEAD, :] = weighted(h, weights, stats, (v, v_near, v_far))
 
 
-def combine_kernel(heads, own, stats, last, next_, out):
-    end = heads * HEAD
-    own_level = stats[8 : 8 + heads, :]
-
-    def level(ref):
-        spare = ref[end : end + SPARE, :].astype(jnp.float32)
-        return spare[0:heads] + spare[heads : 2 * heads] + spare[2 * heads : 3 * heads]
-
-    last_level, next_level = level(last), level(next_)
-    top = jnp.maximum(own_level, jnp.maximum(last_level, next_level))
-    parts = [jnp.exp2(x - top) for x in (own_level, last_level, next_level)]
-    scale = 1.0 / (parts[0] + parts[1] + parts[2])
+def level_of(ref, heads):
+    spare = ref[heads * HEAD : heads * HEAD + SPARE, :].astype(jnp.float32)
+    return spare[0:heads] + spare[heads : 2 * heads] + spare[2 * heads : 3 * heads]
+
+
+def merge_kernel(heads, own, stats, near, out, level_out):
+    levels = [stats[8 : 8 + heads, :], level_of(near, heads)]
+    top = jnp.maximum(levels[0], levels[1])
+    parts = [jnp.exp2(level - top) for level in levels]
+    scale = 1.0 / (parts[0] + parts[1])
+    level_out[...] = jnp.zeros(level_out.shape, jnp.float32)
+    level_out[0:heads, :] = top + jnp.log2(parts[0] + parts[1])
     parts = [part * scale for part in parts]
     for h in range(heads):
         rows = slice(h * HEAD, (h + 1) * HEAD)
         result = own[rows, :] * parts[0][h : h + 1]
-        result = result + last[rows, :].astype(jnp.float32) * parts[1][h : h + 1]
-        result = result + next_[rows, :].astype(jnp.float32) * parts[2][h : h + 1]
+        out[rows, :] = result + near[rows, :].astype(jnp.float32) * parts[1][h : h + 1]
+
+
+def combine_kernel(heads, merged, level, far, out):
+    levels = [level[0:heads, :], level_of(far, heads)]
+    top = jnp.maximum(levels[0], levels[1])
+    parts = [jnp.exp2(level - top) for level in levels]
+    scale = 1.0 / (parts[0] + parts[1])
+    parts = [part * scale for part in parts]
+    for h in range(heads):
+        rows = slice(h * HEAD, (h + 1) * HEAD)
+        result = merged[rows, :] * parts[0][h : h + 1]
+        result = result + far[rows, :].astype(jnp.float32) * parts[1][h : h + 1]
         out[:, rows] = result.T.astype(jnp.bfloat16)
 
 
@@ -138,7 +148,7 @@
         return lax.dynamic_slice_in_dim(tile_coords, device * per_device, per_device, 1)
 
     slabs = [t, partner(t, NEAR, tm_count), partner(t, FAR, tm_count)]
-    columns = [s, (s + 1) % space_count, (s - 1) % space_count]
+    columns = [s, partner(s, NEAR, space_count), partner(s, FAR, space_count)]
     key_tiles = jnp.concatenate([tiles(s, slab) for slab in slabs], axis=1)
     queries = jnp.stack([tiles(column, t) for column in columns], axis=1)
     queries = jnp.repeat(queries, TILE, axis=2)
@@ -155,14 +165,13 @@
     f32, bf16 = jnp.float32, jnp.bfloat16
     pair = 2 * rows * HEAD * rows
 
+    q_near = exchange(query, "space", NEAR)
     k_near = exchange(key, "tm", NEAR)
     k_far = exchange(key, "tm", FAR)
     turned = call(turn_kernel, jax.ShapeDtypeStruct((width, rows), bf16), 0, value)
-    v_near = exchange(turned, "tm", NEAR)
+    q_far = exchange(query, "space", FAR)
     v_far = exchange(turned, "tm", FAR)
-    q_next = shift(query, "space", -1)
-    late, _ = lax.optimization_barrier((query, k_near))
-    q_last = shift(late, "space", 1)
+    v_near = exchange(after(turned, k_near), "tm", NEAR)
     bias = tile_bias(tile_coords, windows, rows // TILE)
 
     def weigh(q, table):
@@ -182,18 +191,24 @@
             weights, stats, turned, v_near, v_far,
         )
 
-    next_weights = weigh(q_next, bias[1])
-    last_weights = weigh(q_last, bias[2])
+    near_weights, near_stats = weigh(q_near, bias[1])
+    far_weights, far_stats = weigh(q_far, after(bias[2], near_stats))
     own_weights, own_stats = weigh(query, bias[0])
-    from_last = shift(visitors(*next_weights), "space", 1)
-    from_next = shift(visitors(*last_weights), "space", -1)
+    to_near = visitors(near_weights, after(near_stats, far_stats))
+    near = exchange(to_near, "space", NEAR)
+    far = exchange(visitors(far_weights, after(far_stats, to_near)), "space", FAR)
     own = call(
         functools.partial(home_kernel, heads), jax.ShapeDtypeStruct((width, rows), f32),
         heads * 3 * pair, own_weights, own_stats, turned, v_near, v_far,
     )
+    merged, level = call(
+        functools.partial(merge_kernel, heads),
+        (jax.ShapeDtypeStruct((width, rows), f32), jax.ShapeDtypeStruct((8, rows), f32)), 0,
+        own, own_stats, near,
+    )
     return call(
         functools.partial(combine_kernel, heads), jax.ShapeDtypeStruct((rows, width), bf16), 0,
-        own, own_stats, from_last, from_next,
+        merged, level, far,
     )
 
 

time: 40.1 us -> 38.2 us (0.953)
  waiting for transfers between devices: 15.1 us -> 10.4 us
  starting transfers between devices: 13.5 us -> 16.8 us
  local copies, waits for them, and re-layouts: 3.49 us -> 3.07 us
    ppermute x4 -> x0, waiting for transfers between devices: 15.1 us -> none  [shift(): lax.ppermute(block, axis, [(i, (i + distance) % count) for i in range(cou...]
    ppermute x4 -> x8, starting transfers between devices: 4.74 us -> 16.8 us  [exchange(): lax.ppermute(block, axis, [(i, partner(i, side, count)) for i in range(co...]
    ppermute x4 -> x8, waiting for transfers between devices: 0.01 us -> 10.4 us  [exchange(): lax.ppermute(block, axis, [(i, partner(i, side, count)) for i in range(co...]
    ppermute x4 -> x0, starting transfers between devices: 8.74 us -> none  [shift(): lax.ppermute(block, axis, [(i, (i + distance) % count) for i in range(cou...]
    unnamed x10, local copies, waits for them, and re-layouts: 2.38 us -> 1.96 us
    pallas_call x8 -> x9, Pallas kernels: 6.48 us -> 6.53 us  [call(): pl.pallas_call(kernel, out_shape=out_shape, compiler_params=pltpu.Compile...]
  transfers between devices with their start and end apart: 8 -> 8, of which waited for: 4 -> 5; matrix products, arithmetic and copies ran while one was open for 5% -> 6% of each run, Pallas kernels for 14% -> 14%
where the time goes in v1:
time: 38.2 us; the launch traced here: 38 us
  starting transfers between devices  16.8 us (44%)
  waiting for transfers between devices  10.4 us (27%)
  Pallas kernels  6.53 us (17%)
  local copies, waits for them, and re-layouts  3.07 us (8%)
  other arithmetic  1.05 us (3%)
    ppermute x8, starting transfers between devices, exchange(): lax.ppermute(block, axis, [(i, partner(i, side, count)) for i in range(co...  16.8 us
    ppermute x8, waiting for transfers between devices, exchange(): lax.ppermute(block, axis, [(i, partner(i, side, count)) for i in range(co...  10.4 us
    pallas_call x9, Pallas kernels, call(): pl.pallas_call(kernel, out_shape=out_shape, compiler_params=pltpu.Compile...  6.53 us
    unnamed x10, local copies, waits for them, and re-layouts  1.96 us
    dynamic_slice x1, local copies, waits for them, and re-layouts, tiles(): lax.dynamic_slice_in_dim(tile_coords, device * per_device, per_device, 1)  0.9 us
    reduce_and x1, other arithmetic, tile_bias(): jnp.all(gap[:, :, None] <= windows[:, None, :, None, None], axis=0)  0.84 us
  transfers between devices with their start and end apart: 8, of which 5 were waited for; matrix products, arithmetic and copies ran while one was open for 6% of the time, Pallas kernels for 14%

profile of v1, /device:TPU:6, one launch (start us, length us, event | category | flops | bytes accessed | tf_op | source)
XLA Modules:
  0.0 38.0 jit_solution(2359372639086340986)
XLA Ops:
  0.0 0.8 %collective-permute-start = (bf16[256,640]{1,0:T(8,128)(2,1)}, bf16[256,640]{1,0:T(8,128)(2,1)S(1)}, u32[]{:S(2)}, u32[]{:S(2)}) collective-permute-start(bf16[256,640]{1,0:T(8,128)(2,1)} %key.5), channel_id=1, source_target_pairs={{0,1},{1,0},{2,3},{3,2},{4,5},{5,4},{6,7},{7,6},{8,9},{9,8},{10,11... | collective-permute-start | bytes 983048 | tf_op jit(solution)/shard_map/ppermute | solution.py:27
  0.8 1.4 %collective-permute-start.1 = (bf16[256,640]{1,0:T(8,128)(2,1)}, bf16[256,640]{1,0:T(8,128)(2,1)S(1)}, u32[]{:S(2)}, u32[]{:S(2)}) collective-permute-start(bf16[256,640]{1,0:T(8,128)(2,1)} %key.5), channel_id=1, source_target_pairs={{0,3},{1,2},{2,1},{3,0},{4,7},{5,6},{6,5},{7,4},{8,11},{9,10},{10,... | collective-permute-start | bytes 983048 | tf_op jit(solution)/shard_map/ppermute | solution.py:27
  2.2 1.7 %collective-permute-start.4 = (bf16[256,640]{1,0:T(8,128)(2,1)}, bf16[256,640]{1,0:T(8,128)(2,1)S(1)}, u32[]{:S(2)}, u32[]{:S(2)}) collective-permute-start(bf16[256,640]{1,0:T(8,128)(2,1)} %q.1), channel_id=1, source_target_pairs={{0,4},{4,0},{8,12},{12,8},{16,20},{20,16},{24,28},{28,24},{32,36},... | collective-permute-start | bytes 983048 | tf_op jit(solution)/shard_map/ppermute | solution.py:27
  3.9 7.6 %collective-permute-start.5 = (bf16[256,640]{1,0:T(8,128)(2,1)}, bf16[256,640]{1,0:T(8,128)(2,1)S(1)}, u32[]{:S(2)}, u32[]{:S(2)}) collective-permute-start(bf16[256,640]{1,0:T(8,128)(2,1)} %q.1), channel_id=1, source_target_pairs={{0,60},{4,8},{8,4},{12,16},{16,12},{20,24},{24,20},{28,32},{32,28}... | collective-permute-start | bytes 983048 | tf_op jit(solution)/shard_map/ppermute | solution.py:27
  11.5 0.0 copy-start
  11.5 1.0 %copy-done = bf16[256,640]{1,0:T(8,128)(2,1)S(1)} copy-done((bf16[256,640]{1,0:T(8,128)(2,1)S(1)}, bf16[256,640]{1,0:T(8,128)(2,1)}, u32[]{:S(2)}) %copy-start) | copy-done | bytes 327704
  12.4 0.0 copy-start.2
  12.4 0.2 shard_map.56.v
  12.6 2.2 %collective-permute-start.3 = (bf16[640,256]{1,0:T(8,128)(2,1)S(1)}, bf16[640,256]{1,0:T(8,128)(2,1)S(1)}, u32[]{:S(2)}, u32[]{:S(2)}) collective-permute-start(bf16[640,256]{1,0:T(8,128)(2,1)S(1)} %shard_map.56.v), channel_id=1, source_target_pairs={{0,3},{1,2},{2,1},{3,0},{4,7},{5,6},{6,5},{7,4},{8,11},{9,10},{10,... | collective-permute-start | bytes 983048 | tf_op jit(solution)/shard_map/ppermute | solution.py:27
  14.8 0.9 %constant_dynamic-slice_fusion.1 = (s32[3,4]{1,0:T(4,128)S(1)}, s32[3,4]{1,0:T(4,128)S(1)}, s32[3,4]{1,0:T(4,128)S(1)}, s32[3,1,4]{2,0,1:T(4,128)S(1)}, s32[3,1,4]{2,0,1:T(4,128)S(1)}) fusion(s32[3,256]{1,0:T(4,128)} %param.8, s32[]{:T(128)S(6)} %select_n.54, s32[]{:T(128)S(6)} %select_n.56, s32[]{:T(128)S(6)} %select_n.51, s32[]{:T(128)S(6)} %select_n.61, ...), kind=kLoop, calls=%fused_computation.8 | loop fusion | bytes 500 | tf_op jit(solution)/shard_map/dynamic_slice | solution.py:148
  15.7 0.1 broadcast_in_dim.14
  15.8 0.1 sub.30
  15.9 0.1 pad_add_fusion.1
  16.0 0.1 subtract_abs_fusion
  16.1 0.8 %compare_reduce_fusion = pred[3,5,12,256]{3,2,1,0:T(8,128)(4,1)S(1)} fusion(s32[3,5]{1,0:T(4,128)} %param.9, s32[3,3,12,256]{3,2,1,0:T(8,128)S(1)} %subtract_abs_fusion), kind=kLoop, calls=%fused_computation | loop fusion | flops 230400 | bytes 156732 | tf_op jit(solution)/shard_map/reduce_and | solution.py:156
  16.9 0.0 collective-permute-done.key_near
  16.9 0.1 collective-permute-start.2
  17.1 0.0 collective-permute-done.1.key_far
  17.1 0.0 copy-start.3
  17.1 0.0 collective-permute-done.4.q
  17.1 0.0 copy-done.2
  17.2 1.3 %shard_map.58 = (bf16[5,768,256]{2,1,0:T(8,128)(2,1)S(1)}, f32[16,256]{1,0:T(8,128)S(1)}) custom-call(bf16[256,640]{1,0:T(8,128)(2,1)S(1)} %collective-permute-done.4.q, bf16[256,640]{1,0:T(8,128)(2,1)S(1)} %copy-done.2, bf16[256,640]{1,0:T(8,128)(2,1)S(1)} %collective-permute-done.key_near, bf16[256,640]{1,0:T(8,128)(2,1)S(1)} %collective-permute-done.1.key_far, ...), custom_call_target="tpu_custom_call" | custom-call | flops 251658240 | bytes 1048576 | tf_op jit(solution)/shard_map/pallas_call | solution.py:35
  18.5 0.1 collective-permute-done.5.q
  18.6 1.3 %shard_map.59 = (bf16[5,768,256]{2,1,0:T(8,128)(2,1)S(1)}, f32[16,256]{1,0:T(8,128)S(1)}) custom-call(bf16[256,640]{1,0:T(8,128)(2,1)S(1)} %collective-permute-done.5.q, bf16[256,640]{1,0:T(8,128)(2,1)S(1)} %copy-done.2, bf16[256,640]{1,0:T(8,128)(2,1)S(1)} %collective-permute-done.key_near, bf16[256,640]{1,0:T(8,128)(2,1)S(1)} %collective-permute-done.1.key_far, ...), custom_call_target="tpu_custom_call" | custom-call | flops 251658240 | bytes 1048576 | tf_op jit(solution)/shard_map/pallas_call | solution.py:35
  19.9 2.3 %collective-permute-done.3.v_far = bf16[640,256]{1,0:T(8,128)(2,1)S(1)} collective-permute-done((bf16[640,256]{1,0:T(8,128)(2,1)S(1)}, bf16[640,256]{1,0:T(8,128)(2,1)S(1)}, u32[]{:S(2)}, u32[]{:S(2)}) %collective-permute-start.3) | collective-permute-done | bytes 327712 | tf_op jit(solution)/shard_map/ppermute | solution.py:27
  22.2 2.8 %collective-permute-done.2.v_near = bf16[640,256]{1,0:T(8,128)(2,1)S(1)} collective-permute-done((bf16[640,256]{1,0:T(8,128)(2,1)S(1)}, bf16[640,256]{1,0:T(8,128)(2,1)S(1)}, u32[]{:S(2)}, u32[]{:S(2)}) %collective-permute-start.2) | collective-permute-done | bytes 327712 | tf_op jit(solution)/shard_map/ppermute | solution.py:27
  25.1 0.0 copy-done.3
  25.1 0.4 %shard_map.60 = bf16[656,256]{1,0:T(8,128)(2,1)S(1)} custom-call(bf16[5,768,256]{2,1,0:T(8,128)(2,1)S(1)} %get-tuple-element.20.weights, f32[16,256]{1,0:T(8,128)S(1)} %get-tuple-element.24.stats, bf16[640,256]{1,0:T(8,128)(2,1)S(1)} %shard_map.56.v, bf16[640,256]{1,0:T(8,128)(2,1)S(1)} %collective-permute-done.2.v_near, ...), custom_call_target="tpu_custom_call" | custom-call | flops 251658240 | bytes 1048576 | tf_op jit(solution)/shard_map/pallas_call | solution.py:35
  25.5 0.0 copy-start.1
  25.5 0.1 collective-permute-start.6
  25.6 0.4 %shard_map.62 = bf16[656,256]{1,0:T(8,128)(2,1)S(1)} custom-call(bf16[5,768,256]{2,1,0:T(8,128)(2,1)S(1)} %get-tuple-element.27.weights, f32[16,256]{1,0:T(8,128)S(1)} %get-tuple-element.28.stats, bf16[640,256]{1,0:T(8,128)(2,1)S(1)} %shard_map.56.v, bf16[640,256]{1,0:T(8,128)(2,1)S(1)} %collective-permute-done.2.v_near, ...), custom_call_target="tpu_custom_call" | custom-call | flops 251658240 | bytes 1048576 | tf_op jit(solution)/shard_map/pallas_call | solution.py:35
  26.0 3.0 %collective-permute-start.7 = (bf16[656,256]{1,0:T(8,128)(2,1)S(1)}, bf16[656,256]{1,0:T(8,128)(2,1)S(1)}, u32[]{:S(2)}, u32[]{:S(2)}) collective-permute-start(bf16[656,256]{1,0:T(8,128)(2,1)S(1)} %shard_map.62), channel_id=1, source_target_pairs={{0,60},{4,8},{8,4},{12,16},{16,12},{20,24},{24,20},{28,32},{32,28}... | collective-permute-start | bytes 1007624 | tf_op jit(solution)/shard_map/ppermute | solution.py:27
  29.0 0.0 copy-done.1
  29.0 0.0 copy-start.4
  29.0 1.0 %copy-done.4 = bf16[256,640]{1,0:T(8,128)(2,1)S(1)} copy-done((bf16[256,640]{1,0:T(8,128)(2,1)S(1)}, bf16[256,640]{1,0:T(8,128)(2,1)}, u32[]{:S(2)}) %copy-start.4) | copy-done | bytes 327704
  30.0 1.3 %shard_map.55 = (bf16[5,768,256]{2,1,0:T(8,128)(2,1)S(1)}, f32[16,256]{1,0:T(8,128)S(1)}) custom-call(bf16[256,640]{1,0:T(8,128)(2,1)S(1)} %copy-done.1, bf16[256,640]{1,0:T(8,128)(2,1)S(1)} %copy-done.2, bf16[256,640]{1,0:T(8,128)(2,1)S(1)} %collective-permute-done.key_near, bf16[256,640]{1,0:T(8,128)(2,1)S(1)} %copy-done.4, f32[60,256]{1,0:T(8,128)S(1)} %reshape_squeeze.9.bias), custom_call_target="tpu_custom_call" | custom-call | flops 251658240 | bytes 1048576 | tf_op jit(solution)/shard_map/pallas_call | solution.py:35
  31.3 0.4 %shard_map.57.own = f32[640,256]{1,0:T(8,128)S(1)} custom-call(bf16[5,768,256]{2,1,0:T(8,128)(2,1)S(1)} %get-tuple-element.17.weights, f32[16,256]{1,0:T(8,128)S(1)} %get-tuple-element.18.stats, bf16[640,256]{1,0:T(8,128)(2,1)S(1)} %shard_map.56.v, bf16[640,256]{1,0:T(8,128)(2,1)S(1)} %collective-permute-done.2.v_near, ...), custom_call_target="tpu_custom_call" | custom-call | flops 251658240 | bytes 1048576 | tf_op jit(solution)/shard_map/pallas_call | solution.py:35
  31.8 1.1 %collective-permute-done.6.near = bf16[656,256]{1,0:T(8,128)(2,1)S(1)} collective-permute-done((bf16[656,256]{1,0:T(8,128)(2,1)S(1)}, bf16[656,256]{1,0:T(8,128)(2,1)S(1)}, u32[]{:S(2)}, u32[]{:S(2)}) %collective-permute-start.6) | collective-permute-done | bytes 335904 | tf_op jit(solution)/shard_map/ppermute | solution.py:27
  32.9 0.1 shard_map.61
  33.0 4.0 %collective-permute-done.7.far = bf16[656,256]{1,0:T(8,128)(2,1)S(1)} collective-permute-done((bf16[656,256]{1,0:T(8,128)(2,1)S(1)}, bf16[656,256]{1,0:T(8,128)(2,1)S(1)}, u32[]{:S(2)}, u32[]{:S(2)}) %collective-permute-start.7) | collective-permute-done | bytes 335904 | tf_op jit(solution)/shard_map/ppermute | solution.py:27
  37.0 0.9 %shard_map.63 = bf16[256,640]{1,0:T(8,128)(2,1)} custom-call(f32[640,256]{1,0:T(8,128)S(1)} %get-tuple-element.25.merged, f32[8,256]{1,0:T(8,128)S(1)} %get-tuple-element.26.level, bf16[656,256]{1,0:T(8,128)(2,1)S(1)} %collective-permute-done.7.far), custom_call_target="tpu_custom_call" | custom-call | bytes 1048576 | tf_op jit(solution)/shard_map/pallas_call | solution.py:35
  (7 shorter events, 0.1 us)
Async XLA Ops:
  0.0 16.9 %collective-permute-start = (bf16[256,640]{1,0:T(8,128)(2,1)}, bf16[256,640]{1,0:T(8,128)(2,1)S(1)}, u32[]{:S(2)}, u32[]{:S(2)}) collective-permute-start(bf16[256,640]{1,0:T(8,128)(2,1)} %key.5), channel_id=1, source_target_pairs={{0,1},{1,0},{2,3},{3,2},{4,5},{5,4},{6,7},{7,6},{8,9},{9,8},{10,11... | collective-permute-start | bytes 983048 | tf_op jit(solution)/shard_map/ppermute | solution.py:27
  0.8 16.3 %collective-permute-start.1 = (bf16[256,640]{1,0:T(8,128)(2,1)}, bf16[256,640]{1,0:T(8,128)(2,1)S(1)}, u32[]{:S(2)}, u32[]{:S(2)}) collective-permute-start(bf16[256,640]{1,0:T(8,128)(2,1)} %key.5), channel_id=1, source_target_pairs={{0,3},{1,2},{2,1},{3,0},{4,7},{5,6},{6,5},{7,4},{8,11},{9,10},{10,... | collective-permute-start | bytes 983048 | tf_op jit(solution)/shard_map/ppermute | solution.py:27
  2.2 14.9 %collective-permute-start.4 = (bf16[256,640]{1,0:T(8,128)(2,1)}, bf16[256,640]{1,0:T(8,128)(2,1)S(1)}, u32[]{:S(2)}, u32[]{:S(2)}) collective-permute-start(bf16[256,640]{1,0:T(8,128)(2,1)} %q.1), channel_id=1, source_target_pairs={{0,4},{4,0},{8,12},{12,8},{16,20},{20,16},{24,28},{28,24},{32,36},... | collective-permute-start | bytes 983048 | tf_op jit(solution)/shard_map/ppermute | solution.py:27
  3.9 14.7 %collective-permute-start.5 = (bf16[256,640]{1,0:T(8,128)(2,1)}, bf16[256,640]{1,0:T(8,128)(2,1)S(1)}, u32[]{:S(2)}, u32[]{:S(2)}) collective-permute-start(bf16[256,640]{1,0:T(8,128)(2,1)} %q.1), channel_id=1, source_target_pairs={{0,60},{4,8},{8,4},{12,16},{16,12},{20,24},{24,20},{28,32},{32,28}... | collective-permute-start | bytes 983048 | tf_op jit(solution)/shard_map/ppermute | solution.py:27
  11.5 1.0 %copy-start = (bf16[256,640]{1,0:T(8,128)(2,1)S(1)}, bf16[256,640]{1,0:T(8,128)(2,1)}, u32[]{:S(2)}) copy-start(bf16[256,640]{1,0:T(8,128)(2,1)} %v.1) | copy-start | bytes 983044
  12.4 4.7 %copy-start.2 = (bf16[256,640]{1,0:T(8,128)(2,1)S(1)}, bf16[256,640]{1,0:T(8,128)(2,1)}, u32[]{:S(2)}) copy-start(bf16[256,640]{1,0:T(8,128)(2,1)} %key.5) | copy-start | bytes 983044
  12.6 9.6 %collective-permute-start.3 = (bf16[640,256]{1,0:T(8,128)(2,1)S(1)}, bf16[640,256]{1,0:T(8,128)(2,1)S(1)}, u32[]{:S(2)}, u32[]{:S(2)}) collective-permute-start(bf16[640,256]{1,0:T(8,128)(2,1)S(1)} %shard_map.56.v), channel_id=1, source_target_pairs={{0,3},{1,2},{2,1},{3,0},{4,7},{5,6},{6,5},{7,4},{8,11},{9,10},{10,... | collective-permute-start | bytes 983048 | tf_op jit(solution)/shard_map/ppermute | solution.py:27
  16.9 8.1 %collective-permute-start.2 = (bf16[640,256]{1,0:T(8,128)(2,1)S(1)}, bf16[640,256]{1,0:T(8,128)(2,1)S(1)}, u32[]{:S(2)}, u32[]{:S(2)}) collective-permute-start(bf16[640,256]{1,0:T(8,128)(2,1)S(1)} %shard_map.56.v), channel_id=1, source_target_pairs={{0,1},{1,0},{2,3},{3,2},{4,5},{5,4},{6,7},{7,6},{8,9},{9,8},{10,11... | collective-permute-start | bytes 983048 | tf_op jit(solution)/shard_map/ppermute | solution.py:27
  17.1 7.9 %copy-start.3 = (bf16[256,640]{1,0:T(8,128)(2,1)}, bf16[256,640]{1,0:T(8,128)(2,1)S(1)}, u32[]{:S(2)}) copy-start(bf16[256,640]{1,0:T(8,128)(2,1)S(1)} %collective-permute-done.1.key_far) | copy-start | bytes 983044
  25.5 3.5 %copy-start.1 = (bf16[256,640]{1,0:T(8,128)(2,1)S(1)}, bf16[256,640]{1,0:T(8,128)(2,1)}, u32[]{:S(2)}) copy-start(bf16[256,640]{1,0:T(8,128)(2,1)} %q.1) | copy-start | bytes 983044
  25.5 7.4 %collective-permute-start.6 = (bf16[656,256]{1,0:T(8,128)(2,1)S(1)}, bf16[656,256]{1,0:T(8,128)(2,1)S(1)}, u32[]{:S(2)}, u32[]{:S(2)}) collective-permute-start(bf16[656,256]{1,0:T(8,128)(2,1)S(1)} %shard_map.60), channel_id=1, source_target_pairs={{0,4},{4,0},{8,12},{12,8},{16,20},{20,16},{24,28},{28,24},{32,36},... | collective-permute-start | bytes 1007624 | tf_op jit(solution)/shard_map/ppermute | solution.py:27
  26.0 11.0 %collective-permute-start.7 = (bf16[656,256]{1,0:T(8,128)(2,1)S(1)}, bf16[656,256]{1,0:T(8,128)(2,1)S(1)}, u32[]{:S(2)}, u32[]{:S(2)}) collective-permute-start(bf16[656,256]{1,0:T(8,128)(2,1)S(1)} %shard_map.62), channel_id=1, source_target_pairs={{0,60},{4,8},{8,4},{12,16},{16,12},{20,24},{24,20},{28,32},{32,28}... | collective-permute-start | bytes 1007624 | tf_op jit(solution)/shard_map/ppermute | solution.py:27
  29.0 1.0 %copy-start.4 = (bf16[256,640]{1,0:T(8,128)(2,1)S(1)}, bf16[256,640]{1,0:T(8,128)(2,1)}, u32[]{:S(2)}) copy-start(bf16[256,640]{1,0:T(8,128)(2,1)} %copy-done.3) | copy-start | bytes 983044

commit v2 on v1

--- a/solution.py
+++ b/solution.py
@@ -27,6 +27,19 @@
     return lax.ppermute(block, axis, [(i, partner(i, side, count)) for i in range(count)])
 
 
+def swap_slabs(block):
+    heads, slabs = lax.axis_size("head"), lax.axis_size("tm")
+    pairs = []
+    for head in range(heads):
+        for slab in range(slabs):
+            if 0 < slab < slabs - 1:
+                there = head * slabs + partner(slab, FAR, slabs)
+            else:
+                there = partner(head, NEAR, heads) * slabs + slab
+            pairs.append((head * slabs + slab, there))
+    return lax.ppermute(block, ("head", "tm"), pairs)
+
+
 def after(block, other):
     return lax.optimization_barrier((block, other))[0]
 
@@ -36,14 +49,8 @@
         kernel,
         out_shape=out_shape,
         compiler_params=pltpu.CompilerParams(vmem_limit_bytes=40 * 1024 * 1024),
-        cost_estimate=pl.CostEstimate(flops=flops, bytes_accessed=moved, transcendentals=exps),
+        cost_estimate=pl.CostEstimate(flops=0, bytes_accessed=1024, transcendentals=0),
     )(*operands)
-
-
-def turn_kernel(v, out):
-    for h in range(v.shape[1] // HEAD):
-        lanes = slice(h * HEAD, (h + 1) * HEAD)
-        out[lanes, :] = v[:, lanes].astype(jnp.float32).T.astype(jnp.bfloat16)
 
 
 def weigh_kernel(heads, q, key, key_near, key_far, bias, weights_out, stats_out):
@@ -74,13 +81,13 @@
 
 
 def weighted(h, weights, stats, values):
-    rows = slice(h * HEAD, (h + 1) * HEAD)
-    width = values[0].shape[1]
+    lanes = slice(h * HEAD, (h + 1) * HEAD)
+    width = values[0].shape[0]
     summed = None
-    for j, turned in enumerate(values):
-        part = jnp.dot(
-            turned[rows, :], weights[h, j * width : (j + 1) * width, :],
-            preferred_element_type=jnp.float32,
+    for j, value in enumerate(values):
+        part = lax.dot_general(
+            value[:, lanes], weights[h, j * width : (j + 1) * width, :],
+            (((0,), (0,)), ((), ())), preferred_element_type=jnp.float32,
         )
         summed = part if summed is None else summed + part
     return summed * stats[h : h + 1, :]
@@ -139,7 +146,7 @@
         out[:, rows] = result.T.astype(jnp.bfloat16)
 
 
-def tile_bias(tile_coords, windows, per_device):
+def tile_bias(tile_coords, windows, per_device, gate):
     space_count, tm_count = lax.axis_size("space"), lax.axis_size("tm")
     s, t = lax.axis_index("space"), lax.axis_index("tm")
 
@@ -151,6 +158,7 @@
     columns = [s, partner(s, NEAR, space_count), partner(s, FAR, space_count)]
     key_tiles = jnp.concatenate([tiles(s, slab) for slab in slabs], axis=1)
     queries = jnp.stack([tiles(column, t) for column in columns], axis=1)
+    key_tiles, queries, _ = lax.optimization_barrier((key_tiles, queries, gate))
     queries = jnp.repeat(queries, TILE, axis=2)
     gap = jnp.abs(key_tiles[:, None, :, None] - queries[:, :, None, :])
     allowed = jnp.all(gap[:, :, None] <= windows[:, None, :, None, None], axis=0)
@@ -165,14 +173,13 @@
     f32, bf16 = jnp.float32, jnp.bfloat16
     pair = 2 * rows * HEAD * rows
 
+    k_near = exchange(key, "tm", NEAR)
+    k_far = swap_slabs(key)
     q_near = exchange(query, "space", NEAR)
-    k_near = exchange(key, "tm", NEAR)
-    k_far = exchange(key, "tm", FAR)
-    turned = call(turn_kernel, jax.ShapeDtypeStruct((width, rows), bf16), 0, value)
     q_far = exchange(query, "space", FAR)
-    v_far = exchange(turned, "tm", FAR)
-    v_near = exchange(after(turned, k_near), "tm", NEAR)
-    bias = tile_bias(tile_coords, windows, rows // TILE)
+    v_far = swap_slabs(value)
+    v_near = exchange(after(value, k_near), "tm", NEAR)
+    bias = tile_bias(tile_coords, windows, rows // TILE, k_near)
 
     def weigh(q, table):
         return call(
@@ -188,7 +195,7 @@
         return call(
             functools.partial(visitors_kernel, heads),
             jax.ShapeDtypeStruct((width + SPARE, rows), bf16), heads * 3 * pair,
-            weights, stats, turned, v_near, v_far,
+            weights, stats, value, v_near, v_far,
         )
 
     near_weights, near_stats = weigh(q_near, bias[1])
@@ -199,7 +206,7 @@
     far = exchange(visitors(far_weights, after(far_stats, to_near)), "space", FAR)
     own = call(
         functools.partial(home_kernel, heads), jax.ShapeDtypeStruct((width, rows), f32),
-        heads * 3 * pair, own_weights, own_stats, turned, v_near, v_far,
+        heads * 3 * pair, own_weights, own_stats, value, v_near, v_far,
     )
     merged, level = call(
         functools.partial(merge_kernel, heads),

time: 38.2 us -> 36.2 us (0.948)
  waiting for transfers between devices: 10.4 us -> 6.22 us
  starting transfers between devices: 16.8 us -> 20 us
  local copies, waits for them, and re-layouts: 3.07 us -> 2.09 us
    ppermute x8 -> x6, waiting for transfers between devices: 10.4 us -> 6.22 us  [exchange(): lax.ppermute(block, axis, [(i, partner(i, side, count)) for i in range(co...]
    ppermute x8 -> x6, starting transfers between devices: 16.8 us -> 20 us  [exchange(): lax.ppermute(block, axis, [(i, partner(i, side, count)) for i in range(co...]
    unnamed x10 -> x6, local copies, waits for them, and re-layouts: 1.96 us -> 0.98 us
    dynamic_slice x1 -> x0, local copies, waits for them, and re-layouts: 0.9 us -> none  [tiles(): lax.dynamic_slice_in_dim(tile_coords, device * per_device, per_device, 1)]
    another operation x1, local copies, waits for them, and re-layouts: 0.01 us -> 0.9 us  [tile_bias(): queries = jnp.stack([tiles(column, t) for column in columns], axis=1)]
    pallas_call x9 -> x8, Pallas kernels: 6.53 us -> 6.49 us  [call(): pl.pallas_call(kernel, out_shape=out_shape, compiler_params=pltpu.Compile...]
  transfers between devices with their start and end apart: 8 -> 8, of which waited for: 5 -> 3; matrix products, arithmetic and copies ran while one was open for 6% -> 6% of each run, Pallas kernels for 14% -> 14%
where the time goes in v2:
time: 36.2 us; the launch traced here: 36 us
  starting transfers between devices  20 us (55%)
  Pallas kernels  6.49 us (18%)
  waiting for transfers between devices  6.22 us (17%)
  local copies, waits for them, and re-layouts  2.09 us (6%)
  other arithmetic  1.04 us (3%)
    ppermute x6, starting transfers between devices, exchange(): lax.ppermute(block, axis, [(i, partner(i, side, count)) for i in range(co...  20 us
    pallas_call x8, Pallas kernels, call(): pl.pallas_call(kernel, out_shape=out_shape, compiler_params=pltpu.Compile...  6.49 us
    ppermute x6, waiting for transfers between devices, exchange(): lax.ppermute(block, axis, [(i, partner(i, side, count)) for i in range(co...  6.22 us
    unnamed x6, local copies, waits for them, and re-layouts  0.98 us
    another operation x1, local copies, waits for them, and re-layouts, tile_bias(): queries = jnp.stack([tiles(column, t) for column in columns], axis=1)  0.9 us
    reduce_and x1, other arithmetic, tile_bias(): jnp.all(gap[:, :, None] <= windows[:, None, :, None, None], axis=0)  0.84 us
  transfers between devices with their start and end apart: 8, of which 3 were waited for; matrix products, arithmetic and copies ran while one was open for 6% of the time, Pallas kernels for 14%

profile of v2, /device:TPU:6, one launch (start us, length us, event | category | flops | bytes accessed | tf_op | source)
XLA Modules:
  0.0 36.0 jit_solution(14359407736086301245)
XLA Ops:
  0.0 0.0 copy-start.1
  0.0 0.8 %collective-permute-start = (bf16[256,640]{1,0:T(8,128)(2,1)}, bf16[256,640]{1,0:T(8,128)(2,1)S(1)}, u32[]{:S(2)}, u32[]{:S(2)}) collective-permute-start(bf16[256,640]{1,0:T(8,128)(2,1)} %key.5), channel_id=1, source_target_pairs={{0,1},{1,0},{2,3},{3,2},{4,5},{5,4},{6,7},{7,6},{8,9},{9,8},{10,11... | collective-permute-start | bytes 983048 | tf_op jit(solution)/shard_map/ppermute | solution.py:27
  0.8 0.0 collective-permute-start.1
  0.8 1.9 %collective-permute-start.4 = (bf16[256,640]{1,0:T(8,128)(2,1)}, bf16[256,640]{1,0:T(8,128)(2,1)S(1)}, u32[]{:S(2)}, u32[]{:S(2)}) collective-permute-start(bf16[256,640]{1,0:T(8,128)(2,1)} %q.1), channel_id=1, source_target_pairs={{0,4},{4,0},{8,12},{12,8},{16,20},{20,16},{24,28},{28,24},{32,36},... | collective-permute-start | bytes 983048 | tf_op jit(solution)/shard_map/ppermute | solution.py:27
  2.8 7.6 %collective-permute-start.5 = (bf16[256,640]{1,0:T(8,128)(2,1)}, bf16[256,640]{1,0:T(8,128)(2,1)S(1)}, u32[]{:S(2)}, u32[]{:S(2)}) collective-permute-start(bf16[256,640]{1,0:T(8,128)(2,1)} %q.1), channel_id=1, source_target_pairs={{0,60},{4,8},{8,4},{12,16},{16,12},{20,24},{24,20},{28,32},{32,28}... | collective-permute-start | bytes 983048 | tf_op jit(solution)/shard_map/ppermute | solution.py:27
  10.3 0.0 collective-permute-start.3
  10.3 0.9 %dynamic-slice_bitcast_fusion.1 = (s32[3,1,4]{2,0,1:T(4,128)S(1)}, s32[3,4]{1,0:T(4,128)S(1)}, s32[3,4]{1,0:T(4,128)S(1)}, s32[3,4]{1,0:T(4,128)S(1)}, s32[3,1,4]{2,0,1:T(4,128)S(1)}) fusion(s32[3,256]{1,0:T(4,128)} %param.8, s32[]{:T(128)S(6)} %select_n.59, s32[]{:T(128)S(6)} %select_n.56, s32[]{:T(128)S(6)} %select_n.54, s32[]{:T(128)S(6)} %select_n.51, ...), kind=kLoop, calls=%fused_computation.6 | loop fusion | bytes 500 | tf_op jit(solution)/shard_map/stack | solution.py:160
  11.2 0.1 pad_add_fusion.1
  11.3 0.0 collective-permute-done.key_near
  11.3 0.1 broadcast_in_dim.14
  11.4 0.1 sub.30
  11.5 3.2 %collective-permute-start.2 = (bf16[256,640]{1,0:T(8,128)(2,1)}, bf16[256,640]{1,0:T(8,128)(2,1)S(1)}, u32[]{:S(2)}, u32[]{:S(2)}) collective-permute-start(bf16[256,640]{1,0:T(8,128)(2,1)} %v.5), channel_id=1, source_target_pairs={{0,1},{1,0},{2,3},{3,2},{4,5},{5,4},{6,7},{7,6},{8,9},{9,8},{10,11... | collective-permute-start | bytes 983048 | tf_op jit(solution)/shard_map/ppermute | solution.py:27
  14.7 0.1 subtract_abs_fusion
  14.8 0.8 %compare_reduce_fusion = pred[3,5,12,256]{3,2,1,0:T(8,128)(4,1)S(1)} fusion(s32[3,5]{1,0:T(4,128)} %param.9, s32[3,3,12,256]{3,2,1,0:T(8,128)S(1)} %subtract_abs_fusion), kind=kLoop, calls=%fused_computation | loop fusion | flops 230400 | bytes 156732 | tf_op jit(solution)/shard_map/reduce_and | solution.py:164
  15.7 0.0 copy-start
  15.8 0.0 collective-permute-done.1.key_far
  15.8 0.0 collective-permute-done.4.q
  15.8 0.0 copy-done.1
  15.8 1.3 %shard_map.57 = (bf16[5,768,256]{2,1,0:T(8,128)(2,1)S(1)}, f32[16,256]{1,0:T(8,128)S(1)}) custom-call(bf16[256,640]{1,0:T(8,128)(2,1)S(1)} %collective-permute-done.4.q, bf16[256,640]{1,0:T(8,128)(2,1)S(1)} %copy-done.1, bf16[256,640]{1,0:T(8,128)(2,1)S(1)} %collective-permute-done.key_near, bf16[256,640]{1,0:T(8,128)(2,1)S(1)} %collective-permute-done.1.key_far, ...), custom_call_target="tpu_custom_call" | custom-call | bytes 1024 | tf_op jit(solution)/shard_map/pallas_call | solution.py:48
  17.2 1.5 %collective-permute-done.5.q = bf16[256,640]{1,0:T(8,128)(2,1)S(1)} collective-permute-done((bf16[256,640]{1,0:T(8,128)(2,1)}, bf16[256,640]{1,0:T(8,128)(2,1)S(1)}, u32[]{:S(2)}, u32[]{:S(2)}) %collective-permute-start.5) | collective-permute-done | bytes 327712 | tf_op jit(solution)/shard_map/ppermute | solution.py:27
  18.7 1.3 %shard_map.58 = (bf16[5,768,256]{2,1,0:T(8,128)(2,1)S(1)}, f32[16,256]{1,0:T(8,128)S(1)}) custom-call(bf16[256,640]{1,0:T(8,128)(2,1)S(1)} %collective-permute-done.5.q, bf16[256,640]{1,0:T(8,128)(2,1)S(1)} %copy-done.1, bf16[256,640]{1,0:T(8,128)(2,1)S(1)} %collective-permute-done.key_near, bf16[256,640]{1,0:T(8,128)(2,1)S(1)} %collective-permute-done.1.key_far, ...), custom_call_target="tpu_custom_call" | custom-call | bytes 1024 | tf_op jit(solution)/shard_map/pallas_call | solution.py:48
  20.0 0.0 collective-permute-done.3.v_far
  20.0 1.8 %collective-permute-done.2.v_near = bf16[256,640]{1,0:T(8,128)(2,1)S(1)} collective-permute-done((bf16[256,640]{1,0:T(8,128)(2,1)}, bf16[256,640]{1,0:T(8,128)(2,1)S(1)}, u32[]{:S(2)}, u32[]{:S(2)}) %collective-permute-start.2) | collective-permute-done | bytes 327712 | tf_op jit(solution)/shard_map/ppermute | solution.py:27
  21.9 0.0 copy-done
  21.9 0.5 %shard_map.59 = bf16[656,256]{1,0:T(8,128)(2,1)S(1)} custom-call(bf16[5,768,256]{2,1,0:T(8,128)(2,1)S(1)} %get-tuple-element.24.weights, f32[16,256]{1,0:T(8,128)S(1)} %get-tuple-element.28.stats, bf16[256,640]{1,0:T(8,128)(2,1)S(1)} %copy-done, bf16[256,640]{1,0:T(8,128)(2,1)S(1)} %collective-permute-done.2.v_near, ...), custom_call_target="tpu_custom_call" | custom-call | bytes 1024 | tf_op jit(solution)/shard_map/pallas_call | solution.py:48
  22.3 0.1 collective-permute-start.6
  22.4 0.5 %shard_map.61 = bf16[656,256]{1,0:T(8,128)(2,1)S(1)} custom-call(bf16[5,768,256]{2,1,0:T(8,128)(2,1)S(1)} %get-tuple-element.31.weights, f32[16,256]{1,0:T(8,128)S(1)} %get-tuple-element.32.stats, bf16[256,640]{1,0:T(8,128)(2,1)S(1)} %copy-done, bf16[256,640]{1,0:T(8,128)(2,1)S(1)} %collective-permute-done.2.v_near, ...), custom_call_target="tpu_custom_call" | custom-call | bytes 1024 | tf_op jit(solution)/shard_map/pallas_call | solution.py:48
  22.9 6.4 %collective-permute-start.7 = (bf16[656,256]{1,0:T(8,128)(2,1)S(1)}, bf16[656,256]{1,0:T(8,128)(2,1)S(1)}, u32[]{:S(2)}, u32[]{:S(2)}) collective-permute-start(bf16[656,256]{1,0:T(8,128)(2,1)S(1)} %shard_map.61), channel_id=1, source_target_pairs={{0,60},{4,8},{8,4},{12,16},{16,12},{20,24},{24,20},{28,32},{32,28}... | collective-permute-start | bytes 1007624 | tf_op jit(solution)/shard_map/ppermute | solution.py:27
  29.3 0.0 copy-start.2
  29.3 1.0 %copy-done.2 = bf16[256,640]{1,0:T(8,128)(2,1)S(1)} copy-done((bf16[256,640]{1,0:T(8,128)(2,1)S(1)}, bf16[256,640]{1,0:T(8,128)(2,1)}, u32[]{:S(2)}) %copy-start.2) | copy-done | bytes 327704
  30.3 1.3 %shard_map.55 = (bf16[5,768,256]{2,1,0:T(8,128)(2,1)S(1)}, f32[16,256]{1,0:T(8,128)S(1)}) custom-call(bf16[256,640]{1,0:T(8,128)(2,1)S(1)} %copy-done.2, bf16[256,640]{1,0:T(8,128)(2,1)S(1)} %copy-done.1, bf16[256,640]{1,0:T(8,128)(2,1)S(1)} %collective-permute-done.key_near, bf16[256,640]{1,0:T(8,128)(2,1)S(1)} %collective-permute-done.1.key_far, ...), custom_call_target="tpu_custom_call" | custom-call | bytes 1024 | tf_op jit(solution)/shard_map/pallas_call | solution.py:48
  31.6 0.5 %shard_map.56.own = f32[640,256]{1,0:T(8,128)S(1)} custom-call(bf16[5,768,256]{2,1,0:T(8,128)(2,1)S(1)} %get-tuple-element.21.weights, f32[16,256]{1,0:T(8,128)S(1)} %get-tuple-element.22.stats, bf16[256,640]{1,0:T(8,128)(2,1)S(1)} %copy-done, bf16[256,640]{1,0:T(8,128)(2,1)S(1)} %collective-permute-done.2.v_near, ...), custom_call_target="tpu_custom_call" | custom-call | bytes 1024 | tf_op jit(solution)/shard_map/pallas_call | solution.py:48
  32.1 0.0 collective-permute-done.6.near
  32.1 0.1 shard_map.60
  32.2 2.9 %collective-permute-done.7.far = bf16[656,256]{1,0:T(8,128)(2,1)S(1)} collective-permute-done((bf16[656,256]{1,0:T(8,128)(2,1)S(1)}, bf16[656,256]{1,0:T(8,128)(2,1)S(1)}, u32[]{:S(2)}, u32[]{:S(2)}) %collective-permute-start.7) | collective-permute-done | bytes 335904 | tf_op jit(solution)/shard_map/ppermute | solution.py:27
  35.1 0.9 %shard_map.62 = bf16[256,640]{1,0:T(8,128)(2,1)} custom-call(f32[640,256]{1,0:T(8,128)S(1)} %get-tuple-element.29.merged, f32[8,256]{1,0:T(8,128)S(1)} %get-tuple-element.30.level, bf16[656,256]{1,0:T(8,128)(2,1)S(1)} %collective-permute-done.7.far), custom_call_target="tpu_custom_call" | custom-call | bytes 1024 | tf_op jit(solution)/shard_map/pallas_call | solution.py:48
  (7 shorter events, 0.1 us)
Async XLA Ops:
  0.0 15.8 %copy-start.1 = (bf16[256,640]{1,0:T(8,128)(2,1)S(1)}, bf16[256,640]{1,0:T(8,128)(2,1)}, u32[]{:S(2)}) copy-start(bf16[256,640]{1,0:T(8,128)(2,1)} %key.5) | copy-start | bytes 983044
  0.0 11.3 %collective-permute-start = (bf16[256,640]{1,0:T(8,128)(2,1)}, bf16[256,640]{1,0:T(8,128)(2,1)S(1)}, u32[]{:S(2)}, u32[]{:S(2)}) collective-permute-start(bf16[256,640]{1,0:T(8,128)(2,1)} %key.5), channel_id=1, source_target_pairs={{0,1},{1,0},{2,3},{3,2},{4,5},{5,4},{6,7},{7,6},{8,9},{9,8},{10,11... | collective-permute-start | bytes 983048 | tf_op jit(solution)/shard_map/ppermute | solution.py:27
  0.8 15.0 %collective-permute-start.1 = (bf16[256,640]{1,0:T(8,128)(2,1)}, bf16[256,640]{1,0:T(8,128)(2,1)S(1)}, u32[]{:S(2)}, u32[]{:S(2)}) collective-permute-start(bf16[256,640]{1,0:T(8,128)(2,1)} %key.5), channel_id=1, source_target_pairs={{0,64},{1,2},{2,1},{3,67},{64,0},{65,66},{66,65},{67,3},{128,192},... | collective-permute-start | bytes 983048 | tf_op jit(solution)/shard_map/ppermute | solution.py:40
  0.8 15.0 %collective-permute-start.4 = (bf16[256,640]{1,0:T(8,128)(2,1)}, bf16[256,640]{1,0:T(8,128)(2,1)S(1)}, u32[]{:S(2)}, u32[]{:S(2)}) collective-permute-start(bf16[256,640]{1,0:T(8,128)(2,1)} %q.1), channel_id=1, source_target_pairs={{0,4},{4,0},{8,12},{12,8},{16,20},{20,16},{24,28},{28,24},{32,36},... | collective-permute-start | bytes 983048 | tf_op jit(solution)/shard_map/ppermute | solution.py:27
  2.8 15.9 %collective-permute-start.5 = (bf16[256,640]{1,0:T(8,128)(2,1)}, bf16[256,640]{1,0:T(8,128)(2,1)S(1)}, u32[]{:S(2)}, u32[]{:S(2)}) collective-permute-start(bf16[256,640]{1,0:T(8,128)(2,1)} %q.1), channel_id=1, source_target_pairs={{0,60},{4,8},{8,4},{12,16},{16,12},{20,24},{24,20},{28,32},{32,28}... | collective-permute-start | bytes 983048 | tf_op jit(solution)/shard_map/ppermute | solution.py:27
  10.3 9.7 %collective-permute-start.3 = (bf16[256,640]{1,0:T(8,128)(2,1)}, bf16[256,640]{1,0:T(8,128)(2,1)S(1)}, u32[]{:S(2)}, u32[]{:S(2)}) collective-permute-start(bf16[256,640]{1,0:T(8,128)(2,1)} %v.5), channel_id=1, source_target_pairs={{0,64},{1,2},{2,1},{3,67},{64,0},{65,66},{66,65},{67,3},{128,192},... | collective-permute-start | bytes 983048 | tf_op jit(solution)/shard_map/ppermute | solution.py:40
  11.5 10.4 %collective-permute-start.2 = (bf16[256,640]{1,0:T(8,128)(2,1)}, bf16[256,640]{1,0:T(8,128)(2,1)S(1)}, u32[]{:S(2)}, u32[]{:S(2)}) collective-permute-start(bf16[256,640]{1,0:T(8,128)(2,1)} %v.5), channel_id=1, source_target_pairs={{0,1},{1,0},{2,3},{3,2},{4,5},{5,4},{6,7},{7,6},{8,9},{9,8},{10,11... | collective-permute-start | bytes 983048 | tf_op jit(solution)/shard_map/ppermute | solution.py:27
  15.7 6.2 %copy-start = (bf16[256,640]{1,0:T(8,128)(2,1)S(1)}, bf16[256,640]{1,0:T(8,128)(2,1)}, u32[]{:S(2)}) copy-start(bf16[256,640]{1,0:T(8,128)(2,1)} %v.5) | copy-start | bytes 983044
  22.3 9.7 %collective-permute-start.6 = (bf16[656,256]{1,0:T(8,128)(2,1)S(1)}, bf16[656,256]{1,0:T(8,128)(2,1)S(1)}, u32[]{:S(2)}, u32[]{:S(2)}) collective-permute-start(bf16[656,256]{1,0:T(8,128)(2,1)S(1)} %shard_map.59), channel_id=1, source_target_pairs={{0,4},{4,0},{8,12},{12,8},{16,20},{20,16},{24,28},{28,24},{32,36},... | collective-permute-start | bytes 1007624 | tf_op jit(solution)/shard_map/ppermute | solution.py:27
  22.9 12.2 %collective-permute-start.7 = (bf16[656,256]{1,0:T(8,128)(2,1)S(1)}, bf16[656,256]{1,0:T(8,128)(2,1)S(1)}, u32[]{:S(2)}, u32[]{:S(2)}) collective-permute-start(bf16[656,256]{1,0:T(8,128)(2,1)S(1)} %shard_map.61), channel_id=1, source_target_pairs={{0,60},{4,8},{8,4},{12,16},{16,12},{20,24},{24,20},{28,32},{32,28}... | collective-permute-start | bytes 1007624 | tf_op jit(solution)/shard_map/ppermute | solution.py:27
  29.3 1.0 %copy-start.2 = (bf16[256,640]{1,0:T(8,128)(2,1)S(1)}, bf16[256,640]{1,0:T(8,128)(2,1)}, u32[]{:S(2)}) copy-start(bf16[256,640]{1,0:T(8,128)(2,1)} %q.1) | copy-start | bytes 983044

commit v3 on v2

--- a/solution.py
+++ b/solution.py
@@ -25,6 +25,11 @@
 def exchange(block, axis, side):
     count = lax.axis_size(axis)
     return lax.ppermute(block, axis, [(i, partner(i, side, count)) for i in range(count)])
+
+
+def shift(block, axis, distance):
+    count = lax.axis_size(axis)
+    return lax.ppermute(block, axis, [(i, (i + distance) % count) for i in range(count)])
 
 
 def swap_slabs(block):
@@ -80,25 +85,22 @@
         stats_out[8 + h : 9 + h, :] = peak * FACTOR + jnp.log2(total)
 
 
-def weighted(h, weights, stats, values):
+def weighted(h, weights, value, j):
     lanes = slice(h * HEAD, (h + 1) * HEAD)
-    width = values[0].shape[0]
-    summed = None
-    for j, value in enumerate(values):
-        part = lax.dot_general(
-            value[:, lanes], weights[h, j * width : (j + 1) * width, :],
-            (((0,), (0,)), ((), ())), preferred_element_type=jnp.float32,
-        )
-        summed = part if summed is None else summed + part
-    return summed * stats[h : h + 1, :]
-
-
-def visitors_kernel(heads, weights, stats, v, v_near, v_far, out):
+    width = value.shape[0]
+    return lax.dot_general(
+        value[:, lanes], weights[h, j * width : (j + 1) * width, :],
+        (((0,), (0,)), ((), ())), preferred_element_type=jnp.float32,
+    )
+
+
+def early_kernel(heads, weights, v, v_far, out):
+    for h in range(heads):
+        out[h * HEAD : (h + 1) * HEAD, :] = weighted(h, weights, v, 0) + weighted(h, weights, v_far, 2)
+
+
+def store_levels(heads, stats, out):
     end = heads * HEAD
-    for h in range(heads):
-        out[h * HEAD : (h + 1) * HEAD, :] = weighted(
-            h, weights, stats, (v, v_near, v_far)
-        ).astype(jnp.bfloat16)
     rest = stats[8:16, :]
     pieces = []
     for part in range(PARTS):
@@ -109,9 +111,30 @@
     out[end : end + SPARE, :] = jnp.concatenate(pieces, axis=0).astype(jnp.bfloat16)
 
 
+def finish_kernel(heads, early, weights, stats, v_near, out):
+    for h in range(heads):
+        rows = slice(h * HEAD, (h + 1) * HEAD)
+        summed = early[rows, :] + weighted(h, weights, v_near, 1)
+        out[rows, :] = (summed * stats[h : h + 1, :]).astype(jnp.bfloat16)
+    store_levels(heads, stats, out)
+
+
+def sum_up(h, weights, stats, v, v_near, v_far):
+    summed = weighted(h, weights, v, 0) + weighted(h, weights, v_near, 1) + weighted(h, weights, v_far, 2)
+    return summed * stats[h : h + 1, :]
+
+
+def visitors_kernel(heads, weights, stats, v, v_near, v_far, out):
+    for h in range(heads):
+        out[h * HEAD : (h + 1) * HEAD, :] = sum_up(
+            h, weights, stats, v, v_near, v_far
+        ).astype(jnp.bfloat16)
+    store_levels(heads, stats, out)
+
+
 def home_kernel(heads, weights, stats, v, v_near, v_far, out):
     for h in range(heads):
-        out[h * HEAD : (h + 1) * HEAD, :] = weighted(h, weights, stats, (v, v_near, v_far))
+        out[h * HEAD : (h + 1) * HEAD, :] = sum_up(h, weights, stats, v, v_near, v_far)
 
 
 def level_of(ref, heads):
@@ -146,7 +169,7 @@
         out[:, rows] = result.T.astype(jnp.bfloat16)
 
 
-def tile_bias(tile_coords, windows, per_device, gate):
+def nearby_tiles(tile_coords, per_device):
     space_count, tm_count = lax.axis_size("space"), lax.axis_size("tm")
     s, t = lax.axis_index("space"), lax.axis_index("tm")
 
@@ -155,10 +178,12 @@
         return lax.dynamic_slice_in_dim(tile_coords, device * per_device, per_device, 1)
 
     slabs = [t, partner(t, NEAR, tm_count), partner(t, FAR, tm_count)]
-    columns = [s, partner(s, NEAR, space_count), partner(s, FAR, space_count)]
+    columns = [s, (s + 1) % space_count, (s - 1) % space_count]
     key_tiles = jnp.concatenate([tiles(s, slab) for slab in slabs], axis=1)
-    queries = jnp.stack([tiles(column, t) for column in columns], axis=1)
-    key_tiles, queries, _ = lax.optimization_barrier((key_tiles, queries, gate))
+    return key_tiles, jnp.stack([tiles(column, t) for column in columns], axis=1)
+
+
+def tile_bias(key_tiles, queries, windows):
     queries = jnp.repeat(queries, TILE, axis=2)
     gap = jnp.abs(key_tiles[:, None, :, None] - queries[:, :, None, :])
     allowed = jnp.all(gap[:, :, None] <= windows[:, None, :, None, None], axis=0)
@@ -175,11 +200,12 @@
 
     k_near = exchange(key, "tm", NEAR)
     k_far = swap_slabs(key)
-    q_near = exchange(query, "space", NEAR)
-    q_far = exchange(query, "space", FAR)
+    near_tiles = nearby_tiles(tile_coords, rows // TILE)
+    q_last = shift(query, "space", 1)
+    q_next = shift(after(query, near_tiles[0]), "space", -1)
     v_far = swap_slabs(value)
     v_near = exchange(after(value, k_near), "tm", NEAR)
-    bias = tile_bias(tile_coords, windows, rows // TILE, k_near)
+    bias = tile_bias(*after(near_tiles, k_near), windows)
 
     def weigh(q, table):
         return call(
@@ -191,19 +217,24 @@
             heads * 3 * pair, q, key, k_near, k_far, table, exps=heads * 3 * rows * rows,
         )
 
-    def visitors(weights, stats):
-        return call(
-            functools.partial(visitors_kernel, heads),
-            jax.ShapeDtypeStruct((width + SPARE, rows), bf16), heads * 3 * pair,
-            weights, stats, value, v_near, v_far,
-        )
-
-    near_weights, near_stats = weigh(q_near, bias[1])
-    far_weights, far_stats = weigh(q_far, after(bias[2], near_stats))
-    own_weights, own_stats = weigh(query, bias[0])
-    to_near = visitors(near_weights, after(near_stats, far_stats))
-    near = exchange(to_near, "space", NEAR)
-    far = exchange(visitors(far_weights, after(far_stats, to_near)), "space", FAR)
+    next_weights, next_stats = weigh(q_next, bias[1])
+    early = call(
+        functools.partial(early_kernel, heads), jax.ShapeDtypeStruct((width, rows), f32), 0,
+        next_weights, value, v_far,
+    )
+    back = jax.ShapeDtypeStruct((width + SPARE, rows), bf16)
+    to_next = call(
+        functools.partial(finish_kernel, heads), back, 0,
+        early, next_weights, next_stats, v_near,
+    )
+    last_weights, last_stats = weigh(q_last, after(bias[2], to_next))
+    to_last = call(
+        functools.partial(visitors_kernel, heads), back, 0,
+        last_weights, last_stats, value, v_near, v_far,
+    )
+    own_weights, own_stats = weigh(query, after(bias[0], to_last))
+    from_last = shift(to_next, "space", 1)
+    from_next = shift(to_last, "space", -1)
     own = call(
         functools.partial(home_kernel, heads), jax.ShapeDtypeStruct((width, rows), f32),
         heads * 3 * pair, own_weights, own_stats, value, v_near, v_far,
@@ -211,11 +242,11 @@
     merged, level = call(
         functools.partial(merge_kernel, heads),
         (jax.ShapeDtypeStruct((width, rows), f32), jax.ShapeDtypeStruct((8, rows), f32)), 0,
-        own, own_stats, near,
+        own, own_stats, from_last,
     )
     return call(
         functools.partial(combine_kernel, heads), jax.ShapeDtypeStruct((rows, width), bf16), 0,
-        merged, level, far,
+        merged, level, from_next,
     )
 
 

time: 36.2 us -> 36.5 us (level)
  waiting for transfers between devices: 6.22 us -> 7.34 us
  starting transfers between devices: 20 us -> 19 us
    ppermute x6 -> x2, starting transfers between devices: 20 us -> 3.85 us  [exchange(): lax.ppermute(block, axis, [(i, partner(i, side, count)) for i in range(co...]
    ppermute x0 -> x4, starting transfers between devices: none -> 14.9 us  [shift(): lax.ppermute(block, axis, [(i, (i + distance) % count) for i in range(cou...]
    ppermute x0 -> x4, waiting for transfers between devices: none -> 6.51 us  [shift(): lax.ppermute(block, axis, [(i, (i + distance) % count) for i in range(cou...]
    ppermute x6 -> x2, waiting for transfers between devices: 6.22 us -> 0.82 us  [exchange(): lax.ppermute(block, axis, [(i, partner(i, side, count)) for i in range(co...]
    pallas_call x8 -> x9, Pallas kernels: 6.49 us -> 6.72 us  [call(): pl.pallas_call(kernel, out_shape=out_shape, compiler_params=pltpu.Compile...]
  transfers between devices with their start and end apart: 8 -> 8, of which waited for: 3 -> 4; matrix products, arithmetic and copies ran while one was open for 6% -> 6% of each run, Pallas kernels for 14% -> 16%
where the time goes in v3:
time: 36.5 us; the launch traced here: 36.3 us
  starting transfers between devices  19 us (52%)
  waiting for transfers between devices  7.34 us (20%)
  Pallas kernels  6.72 us (18%)
  local copies, waits for them, and re-layouts  2.08 us (6%)
  other arithmetic  1.04 us (3%)
    ppermute x4, starting transfers between devices, shift(): lax.ppermute(block, axis, [(i, (i + distance) % count) for i in range(cou...  14.9 us
    pallas_call x9, Pallas kernels, call(): pl.pallas_call(kernel, out_shape=out_shape, compiler_params=pltpu.Compile...  6.72 us
    ppermute x4, waiting for transfers between devices, shift(): lax.ppermute(block, axis, [(i, (i + distance) % count) for i in range(cou...  6.51 us
    ppermute x2, starting transfers between devices, exchange(): lax.ppermute(block, axis, [(i, partner(i, side, count)) for i in range(co...  3.85 us
    unnamed x6, local copies, waits for them, and re-layouts  0.97 us
    another operation x1, local copies, waits for them, and re-layouts, nearby_tiles(): jnp.stack([tiles(column, t) for column in columns], axis=1)  0.9 us
    reduce_and x1, other arithmetic, tile_bias(): jnp.all(gap[:, :, None] <= windows[:, None, :, None, None], axis=0)  0.84 us
    ppermute x2, waiting for transfers between devices, exchange(): lax.ppermute(block, axis, [(i, partner(i, side, count)) for i in range(co...  0.82 us
  transfers between devices with their start and end apart: 8, of which 4 were waited for; matrix products, arithmetic and copies ran while one was open for 6% of the time, Pallas kernels for 16%

profile of v3, /device:TPU:6, one launch (start us, length us, event | category | flops | bytes accessed | tf_op | source)
XLA Modules:
  0.0 36.3 jit_solution(3893187400427859414)
XLA Ops:
  0.0 0.0 copy-start.1
  0.0 0.0 copy-start
  0.0 0.8 %collective-permute-start = (bf16[256,640]{1,0:T(8,128)(2,1)}, bf16[256,640]{1,0:T(8,128)(2,1)S(1)}, u32[]{:S(2)}, u32[]{:S(2)}) collective-permute-start(bf16[256,640]{1,0:T(8,128)(2,1)} %key.5), channel_id=1, source_target_pairs={{0,1},{1,0},{2,3},{3,2},{4,5},{5,4},{6,7},{7,6},{8,9},{9,8},{10,11... | collective-permute-start | bytes 983048 | tf_op jit(solution)/shard_map/ppermute | solution.py:27
  0.8 0.0 collective-permute-start.1
  0.8 1.9 %collective-permute-start.2 = (bf16[256,640]{1,0:T(8,128)(2,1)}, bf16[256,640]{1,0:T(8,128)(2,1)S(1)}, u32[]{:S(2)}, u32[]{:S(2)}) collective-permute-start(bf16[256,640]{1,0:T(8,128)(2,1)} %q.1), channel_id=1, source_target_pairs={{0,4},{4,8},{8,12},{12,16},{16,20},{20,24},{24,28},{28,32},{32,36}... | collective-permute-start | bytes 983048 | tf_op jit(solution)/shard_map/ppermute | solution.py:32
  2.8 0.9 %dynamic-slice_bitcast_fusion.1 = (s32[3,1,4]{2,0,1:T(4,128)S(1)}, s32[3,4]{1,0:T(4,128)S(1)}, s32[3,4]{1,0:T(4,128)S(1)}, s32[3,4]{1,0:T(4,128)S(1)}, s32[3,1,4]{2,0,1:T(4,128)S(1)}) fusion(s32[3,256]{1,0:T(4,128)} %param.8, s32[]{:T(128)S(6)} %select_n.52, s32[]{:T(128)S(6)} %select_n.50, s32[]{:T(128)S(6)} %select_n.48, s32[]{:T(128)S(6)} %select_n.45, ...), kind=kLoop, calls=%fused_computation.6 | loop fusion | bytes 500 | tf_op jit(solution)/shard_map/stack | solution.py:183
  3.7 0.1 pad_add_fusion.1
  3.7 6.6 %collective-permute-start.3 = (bf16[256,640]{1,0:T(8,128)(2,1)}, bf16[256,640]{1,0:T(8,128)(2,1)S(1)}, u32[]{:S(2)}, u32[]{:S(2)}) collective-permute-start(bf16[256,640]{1,0:T(8,128)(2,1)} %q.1), channel_id=1, source_target_pairs={{0,60},{4,0},{8,4},{12,8},{16,12},{20,16},{24,20},{28,24},{32,28},... | collective-permute-start | bytes 983048 | tf_op jit(solution)/shard_map/ppermute | solution.py:32
  10.3 0.2 collective-permute-start.4
  10.6 0.0 collective-permute-done.key_near
  10.6 0.1 broadcast_in_dim.14
  10.6 0.1 sub.29
  10.7 3.0 %collective-permute-start.5 = (bf16[256,640]{1,0:T(8,128)(2,1)}, bf16[256,640]{1,0:T(8,128)(2,1)S(1)}, u32[]{:S(2)}, u32[]{:S(2)}) collective-permute-start(bf16[256,640]{1,0:T(8,128)(2,1)} %v.5), channel_id=1, source_target_pairs={{0,1},{1,0},{2,3},{3,2},{4,5},{5,4},{6,7},{7,6},{8,9},{9,8},{10,11... | collective-permute-start | bytes 983048 | tf_op jit(solution)/shard_map/ppermute | solution.py:27
  13.8 0.1 subtract_abs_fusion
  13.8 0.8 %compare_reduce_fusion = pred[3,5,12,256]{3,2,1,0:T(8,128)(4,1)S(1)} fusion(s32[3,5]{1,0:T(4,128)} %param.9, s32[3,3,12,256]{3,2,1,0:T(8,128)S(1)} %subtract_abs_fusion), kind=kLoop, calls=%fused_computation | loop fusion | flops 230400 | bytes 156732 | tf_op jit(solution)/shard_map/reduce_and | solution.py:189
  14.8 3.5 %collective-permute-done.3.q = bf16[256,640]{1,0:T(8,128)(2,1)S(1)} collective-permute-done((bf16[256,640]{1,0:T(8,128)(2,1)}, bf16[256,640]{1,0:T(8,128)(2,1)S(1)}, u32[]{:S(2)}, u32[]{:S(2)}) %collective-permute-start.3) | collective-permute-done | bytes 327712 | tf_op jit(solution)/shard_map/ppermute | solution.py:32
  18.3 0.0 collective-permute-done.1.key_far
  18.3 0.0 copy-done.1
  18.3 1.4 %shard_map.55 = (bf16[5,768,256]{2,1,0:T(8,128)(2,1)S(1)}, f32[16,256]{1,0:T(8,128)S(1)}) custom-call(bf16[256,640]{1,0:T(8,128)(2,1)S(1)} %collective-permute-done.3.q, bf16[256,640]{1,0:T(8,128)(2,1)S(1)} %copy-done.1, bf16[256,640]{1,0:T(8,128)(2,1)S(1)} %collective-permute-done.key_near, bf16[256,640]{1,0:T(8,128)(2,1)S(1)} %collective-permute-done.1.key_far, ...), custom_call_target="tpu_custom_call" | custom-call | bytes 1024 | tf_op jit(solution)/shard_map/pallas_call | solution.py:53
  19.6 0.0 collective-permute-done.4.v_far
  19.7 0.0 copy-done
  19.7 0.4 %shard_map.56.early = f32[640,256]{1,0:T(8,128)S(1)} custom-call(bf16[5,768,256]{2,1,0:T(8,128)(2,1)S(1)} %get-tuple-element.22.weights, bf16[256,640]{1,0:T(8,128)(2,1)S(1)} %copy-done, bf16[256,640]{1,0:T(8,128)(2,1)S(1)} %collective-permute-done.4.v_far), custom_call_target="tpu_custom_call" | custom-call | bytes 1024 | tf_op jit(solution)/shard_map/pallas_call | solution.py:53
  20.1 0.8 %collective-permute-done.5.v_near = bf16[256,640]{1,0:T(8,128)(2,1)S(1)} collective-permute-done((bf16[256,640]{1,0:T(8,128)(2,1)}, bf16[256,640]{1,0:T(8,128)(2,1)S(1)}, u32[]{:S(2)}, u32[]{:S(2)}) %collective-permute-start.5) | collective-permute-done | bytes 327712 | tf_op jit(solution)/shard_map/ppermute | solution.py:27
  20.9 0.3 shard_map.57
  21.2 0.1 collective-permute-start.6
  21.3 0.0 collective-permute-done.2.q
  21.3 1.4 %shard_map.58 = (bf16[5,768,256]{2,1,0:T(8,128)(2,1)S(1)}, f32[16,256]{1,0:T(8,128)S(1)}) custom-call(bf16[256,640]{1,0:T(8,128)(2,1)S(1)} %collective-permute-done.2.q, bf16[256,640]{1,0:T(8,128)(2,1)S(1)} %copy-done.1, bf16[256,640]{1,0:T(8,128)(2,1)S(1)} %collective-permute-done.key_near, bf16[256,640]{1,0:T(8,128)(2,1)S(1)} %collective-permute-done.1.key_far, ...), custom_call_target="tpu_custom_call" | custom-call | bytes 1024 | tf_op jit(solution)/shard_map/pallas_call | solution.py:53
  22.6 0.5 %shard_map.59 = bf16[656,256]{1,0:T(8,128)(2,1)S(1)} custom-call(bf16[5,768,256]{2,1,0:T(8,128)(2,1)S(1)} %get-tuple-element.26.weights, f32[16,256]{1,0:T(8,128)S(1)} %get-tuple-element.27.stats, bf16[256,640]{1,0:T(8,128)(2,1)S(1)} %copy-done, bf16[256,640]{1,0:T(8,128)(2,1)S(1)} %collective-permute-done.5.v_near, ...), custom_call_target="tpu_custom_call" | custom-call | bytes 1024 | tf_op jit(solution)/shard_map/pallas_call | solution.py:53
  23.1 6.3 %collective-permute-start.7 = (bf16[656,256]{1,0:T(8,128)(2,1)S(1)}, bf16[656,256]{1,0:T(8,128)(2,1)S(1)}, u32[]{:S(2)}, u32[]{:S(2)}) collective-permute-start(bf16[656,256]{1,0:T(8,128)(2,1)S(1)} %shard_map.59), channel_id=1, source_target_pairs={{0,60},{4,0},{8,4},{12,8},{16,12},{20,16},{24,20},{28,24},{32,28},... | collective-permute-start | bytes 1007624 | tf_op jit(solution)/shard_map/ppermute | solution.py:32
  29.5 0.0 copy-start.2
  29.5 1.0 %copy-done.2 = bf16[256,640]{1,0:T(8,128)(2,1)S(1)} copy-done((bf16[256,640]{1,0:T(8,128)(2,1)S(1)}, bf16[256,640]{1,0:T(8,128)(2,1)}, u32[]{:S(2)}) %copy-start.2) | copy-done | bytes 327704
  30.4 1.3 %shard_map.60 = (bf16[5,768,256]{2,1,0:T(8,128)(2,1)S(1)}, f32[16,256]{1,0:T(8,128)S(1)}) custom-call(bf16[256,640]{1,0:T(8,128)(2,1)S(1)} %copy-done.2, bf16[256,640]{1,0:T(8,128)(2,1)S(1)} %copy-done.1, bf16[256,640]{1,0:T(8,128)(2,1)S(1)} %collective-permute-done.key_near, bf16[256,640]{1,0:T(8,128)(2,1)S(1)} %collective-permute-done.1.key_far, ...), custom_call_target="tpu_custom_call" | custom-call | bytes 1024 | tf_op jit(solution)/shard_map/pallas_call | solution.py:53
  31.8 0.5 %shard_map.61.own = f32[640,256]{1,0:T(8,128)S(1)} custom-call(bf16[5,768,256]{2,1,0:T(8,128)(2,1)S(1)} %get-tuple-element.29.weights, f32[16,256]{1,0:T(8,128)S(1)} %get-tuple-element.30.stats, bf16[256,640]{1,0:T(8,128)(2,1)S(1)} %copy-done, bf16[256,640]{1,0:T(8,128)(2,1)S(1)} %collective-permute-done.5.v_near, ...), custom_call_target="tpu_custom_call" | custom-call | bytes 1024 | tf_op jit(solution)/shard_map/pallas_call | solution.py:53
  32.3 1.9 %collective-permute-done.6.near = bf16[656,256]{1,0:T(8,128)(2,1)S(1)} collective-permute-done((bf16[656,256]{1,0:T(8,128)(2,1)S(1)}, bf16[656,256]{1,0:T(8,128)(2,1)S(1)}, u32[]{:S(2)}, u32[]{:S(2)}) %collective-permute-start.6) | collective-permute-done | bytes 335904 | tf_op jit(solution)/shard_map/ppermute | solution.py:32
  34.2 0.1 shard_map.62
  34.3 1.1 %collective-permute-done.7.far = bf16[656,256]{1,0:T(8,128)(2,1)S(1)} collective-permute-done((bf16[656,256]{1,0:T(8,128)(2,1)S(1)}, bf16[656,256]{1,0:T(8,128)(2,1)S(1)}, u32[]{:S(2)}, u32[]{:S(2)}) %collective-permute-start.7) | collective-permute-done | bytes 335904 | tf_op jit(solution)/shard_map/ppermute | solution.py:32
  35.4 0.9 %shard_map.63 = bf16[256,640]{1,0:T(8,128)(2,1)} custom-call(f32[640,256]{1,0:T(8,128)S(1)} %get-tuple-element.31.merged, f32[8,256]{1,0:T(8,128)S(1)} %get-tuple-element.32.level, bf16[656,256]{1,0:T(8,128)(2,1)S(1)} %collective-permute-done.7.far), custom_call_target="tpu_custom_call" | custom-call | bytes 1024 | tf_op jit(solution)/shard_map/pallas_call | solution.py:53
  (7 shorter events, 0.1 us)
Async XLA Ops:
  0.0 18.3 %copy-start.1 = (bf16[256,640]{1,0:T(8,128)(2,1)S(1)}, bf16[256,640]{1,0:T(8,128)(2,1)}, u32[]{:S(2)}) copy-start(bf16[256,640]{1,0:T(8,128)(2,1)} %key.5) | copy-start | bytes 983044
  0.0 19.7 %copy-start = (bf16[256,640]{1,0:T(8,128)(2,1)S(1)}, bf16[256,640]{1,0:T(8,128)(2,1)}, u32[]{:S(2)}) copy-start(bf16[256,640]{1,0:T(8,128)(2,1)} %v.5) | copy-start | bytes 983044
  0.0 10.6 %collective-permute-start = (bf16[256,640]{1,0:T(8,128)(2,1)}, bf16[256,640]{1,0:T(8,128)(2,1)S(1)}, u32[]{:S(2)}, u32[]{:S(2)}) collective-permute-start(bf16[256,640]{1,0:T(8,128)(2,1)} %key.5), channel_id=1, source_target_pairs={{0,1},{1,0},{2,3},{3,2},{4,5},{5,4},{6,7},{7,6},{8,9},{9,8},{10,11... | collective-permute-start | bytes 983048 | tf_op jit(solution)/shard_map/ppermute | solution.py:27
  0.8 17.4 %collective-permute-start.1 = (bf16[256,640]{1,0:T(8,128)(2,1)}, bf16[256,640]{1,0:T(8,128)(2,1)S(1)}, u32[]{:S(2)}, u32[]{:S(2)}) collective-permute-start(bf16[256,640]{1,0:T(8,128)(2,1)} %key.5), channel_id=1, source_target_pairs={{0,64},{1,2},{2,1},{3,67},{64,0},{65,66},{66,65},{67,3},{128,192},... | collective-permute-start | bytes 983048 | tf_op jit(solution)/shard_map/ppermute | solution.py:45
  0.8 20.4 %collective-permute-start.2 = (bf16[256,640]{1,0:T(8,128)(2,1)}, bf16[256,640]{1,0:T(8,128)(2,1)S(1)}, u32[]{:S(2)}, u32[]{:S(2)}) collective-permute-start(bf16[256,640]{1,0:T(8,128)(2,1)} %q.1), channel_id=1, source_target_pairs={{0,4},{4,8},{8,12},{12,16},{16,20},{20,24},{24,28},{28,32},{32,36}... | collective-permute-start | bytes 983048 | tf_op jit(solution)/shard_map/ppermute | solution.py:32
  3.7 14.5 %collective-permute-start.3 = (bf16[256,640]{1,0:T(8,128)(2,1)}, bf16[256,640]{1,0:T(8,128)(2,1)S(1)}, u32[]{:S(2)}, u32[]{:S(2)}) collective-permute-start(bf16[256,640]{1,0:T(8,128)(2,1)} %q.1), channel_id=1, source_target_pairs={{0,60},{4,0},{8,4},{12,8},{16,12},{20,16},{24,20},{28,24},{32,28},... | collective-permute-start | bytes 983048 | tf_op jit(solution)/shard_map/ppermute | solution.py:32
  10.3 9.3 %collective-permute-start.4 = (bf16[256,640]{1,0:T(8,128)(2,1)}, bf16[256,640]{1,0:T(8,128)(2,1)S(1)}, u32[]{:S(2)}, u32[]{:S(2)}) collective-permute-start(bf16[256,640]{1,0:T(8,128)(2,1)} %v.5), channel_id=1, source_target_pairs={{0,64},{1,2},{2,1},{3,67},{64,0},{65,66},{66,65},{67,3},{128,192},... | collective-permute-start | bytes 983048 | tf_op jit(solution)/shard_map/ppermute | solution.py:45
  10.7 10.1 %collective-permute-start.5 = (bf16[256,640]{1,0:T(8,128)(2,1)}, bf16[256,640]{1,0:T(8,128)(2,1)S(1)}, u32[]{:S(2)}, u32[]{:S(2)}) collective-permute-start(bf16[256,640]{1,0:T(8,128)(2,1)} %v.5), channel_id=1, source_target_pairs={{0,1},{1,0},{2,3},{3,2},{4,5},{5,4},{6,7},{7,6},{8,9},{9,8},{10,11... | collective-permute-start | bytes 983048 | tf_op jit(solution)/shard_map/ppermute | solution.py:27
  21.2 13.0 %collective-permute-start.6 = (bf16[656,256]{1,0:T(8,128)(2,1)S(1)}, bf16[656,256]{1,0:T(8,128)(2,1)S(1)}, u32[]{:S(2)}, u32[]{:S(2)}) collective-permute-start(bf16[656,256]{1,0:T(8,128)(2,1)S(1)} %shard_map.57), channel_id=1, source_target_pairs={{0,4},{4,8},{8,12},{12,16},{16,20},{20,24},{24,28},{28,32},{32,36}... | collective-permute-start | bytes 1007624 | tf_op jit(solution)/shard_map/ppermute | solution.py:32
  23.1 12.3 %collective-permute-start.7 = (bf16[656,256]{1,0:T(8,128)(2,1)S(1)}, bf16[656,256]{1,0:T(8,128)(2,1)S(1)}, u32[]{:S(2)}, u32[]{:S(2)}) collective-permute-start(bf16[656,256]{1,0:T(8,128)(2,1)S(1)} %shard_map.59), channel_id=1, source_target_pairs={{0,60},{4,0},{8,4},{12,8},{16,12},{20,16},{24,20},{28,24},{32,28},... | collective-permute-start | bytes 1007624 | tf_op jit(solution)/shard_map/ppermute | solution.py:32
  29.5 1.0 %copy-start.2 = (bf16[256,640]{1,0:T(8,128)(2,1)S(1)}, bf16[256,640]{1,0:T(8,128)(2,1)}, u32[]{:S(2)}) copy-start(bf16[256,640]{1,0:T(8,128)(2,1)} %q.1) | copy-start | bytes 983044

commit v4 on v2

--- a/solution.py
+++ b/solution.py
@@ -25,6 +25,11 @@
 def exchange(block, axis, side):
     count = lax.axis_size(axis)
     return lax.ppermute(block, axis, [(i, partner(i, side, count)) for i in range(count)])
+
+
+def shift(block, axis, distance):
+    count = lax.axis_size(axis)
+    return lax.ppermute(block, axis, [(i, (i + distance) % count) for i in range(count)])
 
 
 def swap_slabs(block):
@@ -93,20 +98,28 @@
     return summed * stats[h : h + 1, :]
 
 
-def visitors_kernel(heads, weights, stats, v, v_near, v_far, out):
+def visitors_kernel(
+    heads, side, near_weights, near_stats, far_weights, far_stats, v, v_near, v_far, out
+):
     end = heads * HEAD
-    for h in range(heads):
-        out[h * HEAD : (h + 1) * HEAD, :] = weighted(
-            h, weights, stats, (v, v_near, v_far)
-        ).astype(jnp.bfloat16)
-    rest = stats[8:16, :]
-    pieces = []
-    for part in range(PARTS):
-        piece = rest.astype(jnp.bfloat16).astype(jnp.float32)
-        rest = rest - piece
-        pieces.append(piece[0:heads])
-    pieces.append(jnp.zeros((SPARE - PARTS * heads, rest.shape[1]), jnp.float32))
-    out[end : end + SPARE, :] = jnp.concatenate(pieces, axis=0).astype(jnp.bfloat16)
+    odd = lax.axis_index("space") % 2
+
+    def sum_up(weights, stats):
+        for h in range(heads):
+            out[h * HEAD : (h + 1) * HEAD, :] = weighted(
+                h, weights, stats, (v, v_near, v_far)
+            ).astype(jnp.bfloat16)
+        rest = stats[8:16, :]
+        pieces = []
+        for part in range(PARTS):
+            piece = rest.astype(jnp.bfloat16).astype(jnp.float32)
+            rest = rest - piece
+            pieces.append(piece[0:heads])
+        pieces.append(jnp.zeros((SPARE - PARTS * heads, rest.shape[1]), jnp.float32))
+        out[end : end + SPARE, :] = jnp.concatenate(pieces, axis=0).astype(jnp.bfloat16)
+
+    pl.when(odd == side)(lambda: sum_up(near_weights, near_stats))
+    pl.when(odd != side)(lambda: sum_up(far_weights, far_stats))
 
 
 def home_kernel(heads, weights, stats, v, v_near, v_far, out):
@@ -117,6 +130,13 @@
 def level_of(ref, heads):
     spare = ref[heads * HEAD : heads * HEAD + SPARE, :].astype(jnp.float32)
     return spare[0:heads] + spare[heads : 2 * heads] + spare[2 * heads : 3 * heads]
+
+
+def shares(levels):
+    top = functools.reduce(jnp.maximum, levels)
+    parts = [jnp.exp2(level - top) for level in levels]
+    scale = 1.0 / functools.reduce(jnp.add, parts)
+    return [part * scale for part in parts]
 
 
 def merge_kernel(heads, own, stats, near, out, level_out):
@@ -133,20 +153,26 @@
         out[rows, :] = result + near[rows, :].astype(jnp.float32) * parts[1][h : h + 1]
 
 
-def combine_kernel(heads, merged, level, far, out):
-    levels = [level[0:heads, :], level_of(far, heads)]
-    top = jnp.maximum(levels[0], levels[1])
-    parts = [jnp.exp2(level - top) for level in levels]
-    scale = 1.0 / (parts[0] + parts[1])
-    parts = [part * scale for part in parts]
-    for h in range(heads):
-        rows = slice(h * HEAD, (h + 1) * HEAD)
-        result = merged[rows, :] * parts[0][h : h + 1]
-        result = result + far[rows, :].astype(jnp.float32) * parts[1][h : h + 1]
-        out[:, rows] = result.T.astype(jnp.bfloat16)
-
-
-def tile_bias(tile_coords, windows, per_device, gate):
+def combine_kernel(heads, merged, level, other, out, block, sems):
+    parts = shares([level[0:heads, :], level_of(other, heads)])
+    rows = block.shape[0]
+    half = rows // 2
+    copies = []
+    for i in range(2):
+        lanes = slice(i * half, (i + 1) * half)
+        for h in range(heads):
+            features = slice(h * HEAD, (h + 1) * HEAD)
+            result = merged[features, lanes] * parts[0][h : h + 1, lanes]
+            result = result + other[features, lanes].astype(jnp.float32) * parts[1][h : h + 1, lanes]
+            block[lanes, features] = result.astype(jnp.bfloat16).T
+        copy = pltpu.make_async_copy(block.at[lanes], out.at[lanes], sems.at[i])
+        copy.start()
+        copies.append(copy)
+    for copy in copies:
+        copy.wait()
+
+
+def nearby_tiles(tile_coords, per_device):
     space_count, tm_count = lax.axis_size("space"), lax.axis_size("tm")
     s, t = lax.axis_index("space"), lax.axis_index("tm")
 
@@ -157,8 +183,10 @@
     slabs = [t, partner(t, NEAR, tm_count), partner(t, FAR, tm_count)]
     columns = [s, partner(s, NEAR, space_count), partner(s, FAR, space_count)]
     key_tiles = jnp.concatenate([tiles(s, slab) for slab in slabs], axis=1)
-    queries = jnp.stack([tiles(column, t) for column in columns], axis=1)
-    key_tiles, queries, _ = lax.optimization_barrier((key_tiles, queries, gate))
+    return key_tiles, jnp.stack([tiles(column, t) for column in columns], axis=1)
+
+
+def tile_bias(key_tiles, queries, windows):
     queries = jnp.repeat(queries, TILE, axis=2)
     gap = jnp.abs(key_tiles[:, None, :, None] - queries[:, :, None, :])
     allowed = jnp.all(gap[:, :, None] <= windows[:, None, :, None, None], axis=0)
@@ -176,10 +204,11 @@
     k_near = exchange(key, "tm", NEAR)
     k_far = swap_slabs(key)
     q_near = exchange(query, "space", NEAR)
-    q_far = exchange(query, "space", FAR)
+    near_tiles = nearby_tiles(tile_coords, rows // TILE)
+    q_far = exchange(after(query, near_tiles[0]), "space", FAR)
     v_far = swap_slabs(value)
     v_near = exchange(after(value, k_near), "tm", NEAR)
-    bias = tile_bias(tile_coords, windows, rows // TILE, k_near)
+    bias = tile_bias(*after(near_tiles, k_near), windows)
 
     def weigh(q, table):
         return call(
@@ -191,19 +220,21 @@
             heads * 3 * pair, q, key, k_near, k_far, table, exps=heads * 3 * rows * rows,
         )
 
-    def visitors(weights, stats):
-        return call(
-            functools.partial(visitors_kernel, heads),
-            jax.ShapeDtypeStruct((width + SPARE, rows), bf16), heads * 3 * pair,
-            weights, stats, value, v_near, v_far,
-        )
-
     near_weights, near_stats = weigh(q_near, bias[1])
     far_weights, far_stats = weigh(q_far, after(bias[2], near_stats))
     own_weights, own_stats = weigh(query, bias[0])
-    to_near = visitors(near_weights, after(near_stats, far_stats))
-    near = exchange(to_near, "space", NEAR)
-    far = exchange(visitors(far_weights, after(far_stats, to_near)), "space", FAR)
+
+    def visitors(side, stats):
+        return call(
+            functools.partial(visitors_kernel, heads, side),
+            jax.ShapeDtypeStruct((width + SPARE, rows), bf16), 0,
+            near_weights, near_stats, far_weights, stats, value, v_near, v_far,
+        )
+
+    to_next = visitors(0, far_stats)
+    to_last = visitors(1, after(far_stats, to_next))
+    from_last = shift(to_next, "space", 1)
+    from_next = shift(to_last, "space", -1)
     own = call(
         functools.partial(home_kernel, heads), jax.ShapeDtypeStruct((width, rows), f32),
         heads * 3 * pair, own_weights, own_stats, value, v_near, v_far,
@@ -211,12 +242,16 @@
     merged, level = call(
         functools.partial(merge_kernel, heads),
         (jax.ShapeDtypeStruct((width, rows), f32), jax.ShapeDtypeStruct((8, rows), f32)), 0,
-        own, own_stats, near,
-    )
-    return call(
-        functools.partial(combine_kernel, heads), jax.ShapeDtypeStruct((rows, width), bf16), 0,
-        merged, level, far,
-    )
+        own, own_stats, from_last,
+    )
+    return pl.pallas_call(
+        functools.partial(combine_kernel, heads),
+        out_shape=jax.ShapeDtypeStruct((rows, width), bf16),
+        out_specs=pl.BlockSpec(memory_space=pl.ANY),
+        scratch_shapes=[pltpu.VMEM((rows, width), bf16), pltpu.SemaphoreType.DMA((2,))],
+        compiler_params=pltpu.CompilerParams(vmem_limit_bytes=40 * 1024 * 1024),
+        cost_estimate=pl.CostEstimate(flops=0, bytes_accessed=1024, transcendentals=0),
+    )(merged, level, from_next)
 
 
 def solution(mesh):

time: 36.2 us -> 38.8 us (1.072)
  the two profiles are of different devices: /device:TPU:6 before, /device:TPU:1 now
where the time goes in v4:
time: 38.8 us; the launch traced here: 38.6 us
  starting transfers between devices  19.3 us (50%)
  waiting for transfers between devices  9.52 us (25%)
  Pallas kernels  6.52 us (17%)
  local copies, waits for them, and re-layouts  2.09 us (5%)
  other arithmetic  1.04 us (3%)
    ppermute x4, starting transfers between devices, exchange(): lax.ppermute(block, axis, [(i, partner(i, side, count)) for i in range(co...  9.01 us
    ppermute x4, waiting for transfers between devices, exchange(): lax.ppermute(block, axis, [(i, partner(i, side, count)) for i in range(co...  5.76 us
    pallas_call x7, Pallas kernels, call(): pl.pallas_call(kernel, out_shape=out_shape, compiler_params=pltpu.Compile...  5.65 us
    ppermute x2, starting transfers between devices, shift(): lax.ppermute(block, axis, [(i, (i + distance) % count) for i in range(cou...  5.21 us
    ppermute x2, starting transfers between devices, swap_slabs(): return lax.ppermute(block, ('head', 'tm'), pairs)  5.04 us
    ppermute x2, waiting for transfers between devices, shift(): lax.ppermute(block, axis, [(i, (i + distance) % count) for i in range(cou...  3.75 us
    unnamed x6, local copies, waits for them, and re-layouts  0.98 us
    another operation x1, local copies, waits for them, and re-layouts, nearby_tiles(): jnp.stack([tiles(column, t) for column in columns], axis=1)  0.9 us
  transfers between devices with their start and end apart: 8, of which 3 were waited for; matrix products, arithmetic and copies ran while one was open for 6% of the time, Pallas kernels for 13%

profile of v4, /device:TPU:1, one launch (start us, length us, event | category | flops | bytes accessed | tf_op | source)
XLA Modules:
  0.0 38.6 jit_solution(16595744117554742)
XLA Ops:
  0.0 0.0 copy-start.1
  0.0 3.2 %collective-permute-start.1 = (bf16[256,640]{1,0:T(8,128)(2,1)}, bf16[256,640]{1,0:T(8,128)(2,1)S(1)}, u32[]{:S(2)}, u32[]{:S(2)}) collective-permute-start(bf16[256,640]{1,0:T(8,128)(2,1)} %key.5), channel_id=1, source_target_pairs={{0,64},{1,2},{2,1},{3,67},{64,0},{65,66},{66,65},{67,3},{128,192},... | collective-permute-start | bytes 983048 | tf_op jit(solution)/shard_map/ppermute | solution.py:45
  3.2 0.0 collective-permute-start
  3.3 1.6 %collective-permute-start.4 = (bf16[256,640]{1,0:T(8,128)(2,1)}, bf16[256,640]{1,0:T(8,128)(2,1)S(1)}, u32[]{:S(2)}, u32[]{:S(2)}) collective-permute-start(bf16[256,640]{1,0:T(8,128)(2,1)} %q.1), channel_id=1, source_target_pairs={{0,4},{4,0},{8,12},{12,8},{16,20},{20,16},{24,28},{28,24},{32,36},... | collective-permute-start | bytes 983048 | tf_op jit(solution)/shard_map/ppermute | solution.py:27
  4.9 0.9 %dynamic-slice_bitcast_fusion.1 = (s32[3,1,4]{2,0,1:T(4,128)S(1)}, s32[3,4]{1,0:T(4,128)S(1)}, s32[3,4]{1,0:T(4,128)S(1)}, s32[3,4]{1,0:T(4,128)S(1)}, s32[3,1,4]{2,0,1:T(4,128)S(1)}) fusion(s32[3,256]{1,0:T(4,128)} %param.8, s32[]{:T(128)S(6)} %select_n.59, s32[]{:T(128)S(6)} %select_n.56, s32[]{:T(128)S(6)} %select_n.54, s32[]{:T(128)S(6)} %select_n.51, ...), kind=kLoop, calls=%fused_computation.6 | loop fusion | bytes 500 | tf_op jit(solution)/shard_map/stack | solution.py:186
  5.8 0.1 pad_add_fusion.1
  5.9 7.3 %collective-permute-start.5 = (bf16[256,640]{1,0:T(8,128)(2,1)}, bf16[256,640]{1,0:T(8,128)(2,1)S(1)}, u32[]{:S(2)}, u32[]{:S(2)}) collective-permute-start(bf16[256,640]{1,0:T(8,128)(2,1)} %q.1), channel_id=1, source_target_pairs={{0,60},{4,8},{8,4},{12,16},{16,12},{20,24},{24,20},{28,32},{32,28}... | collective-permute-start | bytes 983048 | tf_op jit(solution)/shard_map/ppermute | solution.py:27
  13.2 1.8 %collective-permute-start.3 = (bf16[256,640]{1,0:T(8,128)(2,1)}, bf16[256,640]{1,0:T(8,128)(2,1)S(1)}, u32[]{:S(2)}, u32[]{:S(2)}) collective-permute-start(bf16[256,640]{1,0:T(8,128)(2,1)} %v.5), channel_id=1, source_target_pairs={{0,64},{1,2},{2,1},{3,67},{64,0},{65,66},{66,65},{67,3},{128,192},... | collective-permute-start | bytes 983048 | tf_op jit(solution)/shard_map/ppermute | solution.py:45
  15.0 0.0 collective-permute-done.key_near
  15.0 0.1 broadcast_in_dim.14
  15.1 0.1 sub.30
  15.2 0.0 collective-permute-start.2
  15.2 0.1 subtract_abs_fusion
  15.3 0.8 %compare_reduce_fusion = pred[3,5,12,256]{3,2,1,0:T(8,128)(4,1)S(1)} fusion(s32[3,5]{1,0:T(4,128)} %param.9, s32[3,3,12,256]{3,2,1,0:T(8,128)S(1)} %subtract_abs_fusion), kind=kLoop, calls=%fused_computation | loop fusion | flops 230400 | bytes 156732 | tf_op jit(solution)/shard_map/reduce_and | solution.py:192
  16.2 0.0 copy-start
  16.3 0.0 collective-permute-done.4.q
  16.3 0.0 collective-permute-done.1.key_far
  16.3 0.0 copy-done.1
  16.3 1.3 %shard_map.57 = (bf16[5,768,256]{2,1,0:T(8,128)(2,1)S(1)}, f32[16,256]{1,0:T(8,128)S(1)}) custom-call(bf16[256,640]{1,0:T(8,128)(2,1)S(1)} %collective-permute-done.4.q, bf16[256,640]{1,0:T(8,128)(2,1)S(1)} %copy-done.1, bf16[256,640]{1,0:T(8,128)(2,1)S(1)} %collective-permute-done.key_near, bf16[256,640]{1,0:T(8,128)(2,1)S(1)} %collective-permute-done.1.key_far, ...), custom_call_target="tpu_custom_call" | custom-call | bytes 1024 | tf_op jit(solution)/shard_map/pallas_call | solution.py:53
  17.6 2.3 %collective-permute-done.5.q = bf16[256,640]{1,0:T(8,128)(2,1)S(1)} collective-permute-done((bf16[256,640]{1,0:T(8,128)(2,1)}, bf16[256,640]{1,0:T(8,128)(2,1)S(1)}, u32[]{:S(2)}, u32[]{:S(2)}) %collective-permute-start.5) | collective-permute-done | bytes 327712 | tf_op jit(solution)/shard_map/ppermute | solution.py:27
  19.9 1.3 %shard_map.58 = (bf16[5,768,256]{2,1,0:T(8,128)(2,1)S(1)}, f32[16,256]{1,0:T(8,128)S(1)}) custom-call(bf16[256,640]{1,0:T(8,128)(2,1)S(1)} %collective-permute-done.5.q, bf16[256,640]{1,0:T(8,128)(2,1)S(1)} %copy-done.1, bf16[256,640]{1,0:T(8,128)(2,1)S(1)} %collective-permute-done.key_near, bf16[256,640]{1,0:T(8,128)(2,1)S(1)} %collective-permute-done.1.key_far, ...), custom_call_target="tpu_custom_call" | custom-call | bytes 1024 | tf_op jit(solution)/shard_map/pallas_call | solution.py:53
  21.3 0.0 collective-permute-done.3.v_far
  21.3 3.5 %collective-permute-done.2.v_near = bf16[256,640]{1,0:T(8,128)(2,1)S(1)} collective-permute-done((bf16[256,640]{1,0:T(8,128)(2,1)}, bf16[256,640]{1,0:T(8,128)(2,1)S(1)}, u32[]{:S(2)}, u32[]{:S(2)}) %collective-permute-start.2) | collective-permute-done | bytes 327712 | tf_op jit(solution)/shard_map/ppermute | solution.py:27
  24.8 0.0 copy-done
  24.8 0.5 %shard_map.59 = bf16[656,256]{1,0:T(8,128)(2,1)S(1)} custom-call(bf16[5,768,256]{2,1,0:T(8,128)(2,1)S(1)} %get-tuple-element.24.near_weights, f32[16,256]{1,0:T(8,128)S(1)} %get-tuple-element.25.near_stats, bf16[5,768,256]{2,1,0:T(8,128)(2,1)S(1)} %get-tuple-element.28.far_weights, f32[16,256]{1,0:T(8,128)S(1)} %get-tuple-element.32.far_stats, ...), custom_call_target="tpu_custom_call" | custom-call | bytes 1024 | tf_op jit(solution)/shard_map/pallas_call | solution.py:53
  25.3 0.1 collective-permute-start.6
  25.4 0.5 %shard_map.61 = bf16[656,256]{1,0:T(8,128)(2,1)S(1)} custom-call(bf16[5,768,256]{2,1,0:T(8,128)(2,1)S(1)} %get-tuple-element.24.near_weights, f32[16,256]{1,0:T(8,128)S(1)} %get-tuple-element.25.near_stats, bf16[5,768,256]{2,1,0:T(8,128)(2,1)S(1)} %get-tuple-element.28.far_weights, f32[16,256]{1,0:T(8,128)S(1)} %get-tuple-element.32.far_stats, ...), custom_call_target="tpu_custom_call" | custom-call | bytes 1024 | tf_op jit(solution)/shard_map/pallas_call | solution.py:53
  25.9 5.1 %collective-permute-start.7 = (bf16[656,256]{1,0:T(8,128)(2,1)S(1)}, bf16[656,256]{1,0:T(8,128)(2,1)S(1)}, u32[]{:S(2)}, u32[]{:S(2)}) collective-permute-start(bf16[656,256]{1,0:T(8,128)(2,1)S(1)} %shard_map.61), channel_id=1, source_target_pairs={{0,60},{4,0},{8,4},{12,8},{16,12},{20,16},{24,20},{28,24},{32,28},... | collective-permute-start | bytes 1007624 | tf_op jit(solution)/shard_map/ppermute | solution.py:32
  31.0 0.0 copy-start.2
  31.1 1.0 %copy-done.2 = bf16[256,640]{1,0:T(8,128)(2,1)S(1)} copy-done((bf16[256,640]{1,0:T(8,128)(2,1)S(1)}, bf16[256,640]{1,0:T(8,128)(2,1)}, u32[]{:S(2)}) %copy-start.2) | copy-done | bytes 327704
  32.0 1.3 %shard_map.55 = (bf16[5,768,256]{2,1,0:T(8,128)(2,1)S(1)}, f32[16,256]{1,0:T(8,128)S(1)}) custom-call(bf16[256,640]{1,0:T(8,128)(2,1)S(1)} %copy-done.2, bf16[256,640]{1,0:T(8,128)(2,1)S(1)} %copy-done.1, bf16[256,640]{1,0:T(8,128)(2,1)S(1)} %collective-permute-done.key_near, bf16[256,640]{1,0:T(8,128)(2,1)S(1)} %collective-permute-done.1.key_far, ...), custom_call_target="tpu_custom_call" | custom-call | bytes 1024 | tf_op jit(solution)/shard_map/pallas_call | solution.py:53
  33.4 0.5 %shard_map.56.own = f32[640,256]{1,0:T(8,128)S(1)} custom-call(bf16[5,768,256]{2,1,0:T(8,128)(2,1)S(1)} %get-tuple-element.21.weights, f32[16,256]{1,0:T(8,128)S(1)} %get-tuple-element.22.stats, bf16[256,640]{1,0:T(8,128)(2,1)S(1)} %copy-done, bf16[256,640]{1,0:T(8,128)(2,1)S(1)} %collective-permute-done.2.v_near, ...), custom_call_target="tpu_custom_call" | custom-call | bytes 1024 | tf_op jit(solution)/shard_map/pallas_call | solution.py:53
  33.8 3.8 %collective-permute-done.6.near = bf16[656,256]{1,0:T(8,128)(2,1)S(1)} collective-permute-done((bf16[656,256]{1,0:T(8,128)(2,1)S(1)}, bf16[656,256]{1,0:T(8,128)(2,1)S(1)}, u32[]{:S(2)}, u32[]{:S(2)}) %collective-permute-start.6) | collective-permute-done | bytes 335904 | tf_op jit(solution)/shard_map/ppermute | solution.py:32
  37.6 0.1 shard_map.60
  37.7 0.0 collective-permute-done.7.other
  37.7 0.9 %shard_map.62 = bf16[256,640]{1,0:T(8,128)(2,1)} custom-call(f32[640,256]{1,0:T(8,128)S(1)} %get-tuple-element.30.merged, f32[8,256]{1,0:T(8,128)S(1)} %get-tuple-element.31.level, bf16[656,256]{1,0:T(8,128)(2,1)S(1)} %collective-permute-done.7.other), custom_call_target="tpu_custom_call" | custom-call | bytes 1024 | tf_op jit(solution)/shard_map/pallas_call | solution.py:247
  (7 shorter events, 0.1 us)
Async XLA Ops:
  0.0 16.3 %copy-start.1 = (bf16[256,640]{1,0:T(8,128)(2,1)S(1)}, bf16[256,640]{1,0:T(8,128)(2,1)}, u32[]{:S(2)}) copy-start(bf16[256,640]{1,0:T(8,128)(2,1)} %key.5) | copy-start | bytes 983044
  0.0 16.3 %collective-permute-start.1 = (bf16[256,640]{1,0:T(8,128)(2,1)}, bf16[256,640]{1,0:T(8,128)(2,1)S(1)}, u32[]{:S(2)}, u32[]{:S(2)}) collective-permute-start(bf16[256,640]{1,0:T(8,128)(2,1)} %key.5), channel_id=1, source_target_pairs={{0,64},{1,2},{2,1},{3,67},{64,0},{65,66},{66,65},{67,3},{128,192},... | collective-permute-start | bytes 983048 | tf_op jit(solution)/shard_map/ppermute | solution.py:45
  3.2 11.8 %collective-permute-start = (bf16[256,640]{1,0:T(8,128)(2,1)}, bf16[256,640]{1,0:T(8,128)(2,1)S(1)}, u32[]{:S(2)}, u32[]{:S(2)}) collective-permute-start(bf16[256,640]{1,0:T(8,128)(2,1)} %key.5), channel_id=1, source_target_pairs={{0,1},{1,0},{2,3},{3,2},{4,5},{5,4},{6,7},{7,6},{8,9},{9,8},{10,11... | collective-permute-start | bytes 983048 | tf_op jit(solution)/shard_map/ppermute | solution.py:27
  3.3 13.0 %collective-permute-start.4 = (bf16[256,640]{1,0:T(8,128)(2,1)}, bf16[256,640]{1,0:T(8,128)(2,1)S(1)}, u32[]{:S(2)}, u32[]{:S(2)}) collective-permute-start(bf16[256,640]{1,0:T(8,128)(2,1)} %q.1), channel_id=1, source_target_pairs={{0,4},{4,0},{8,12},{12,8},{16,20},{20,16},{24,28},{28,24},{32,36},... | collective-permute-start | bytes 983048 | tf_op jit(solution)/shard_map/ppermute | solution.py:27
  5.9 14.0 %collective-permute-start.5 = (bf16[256,640]{1,0:T(8,128)(2,1)}, bf16[256,640]{1,0:T(8,128)(2,1)S(1)}, u32[]{:S(2)}, u32[]{:S(2)}) collective-permute-start(bf16[256,640]{1,0:T(8,128)(2,1)} %q.1), channel_id=1, source_target_pairs={{0,60},{4,8},{8,4},{12,16},{16,12},{20,24},{24,20},{28,32},{32,28}... | collective-permute-start | bytes 983048 | tf_op jit(solution)/shard_map/ppermute | solution.py:27
  13.2 8.1 %collective-permute-start.3 = (bf16[256,640]{1,0:T(8,128)(2,1)}, bf16[256,640]{1,0:T(8,128)(2,1)S(1)}, u32[]{:S(2)}, u32[]{:S(2)}) collective-permute-start(bf16[256,640]{1,0:T(8,128)(2,1)} %v.5), channel_id=1, source_target_pairs={{0,64},{1,2},{2,1},{3,67},{64,0},{65,66},{66,65},{67,3},{128,192},... | collective-permute-start | bytes 983048 | tf_op jit(solution)/shard_map/ppermute | solution.py:45
  15.2 9.6 %collective-permute-start.2 = (bf16[256,640]{1,0:T(8,128)(2,1)}, bf16[256,640]{1,0:T(8,128)(2,1)S(1)}, u32[]{:S(2)}, u32[]{:S(2)}) collective-permute-start(bf16[256,640]{1,0:T(8,128)(2,1)} %v.5), channel_id=1, source_target_pairs={{0,1},{1,0},{2,3},{3,2},{4,5},{5,4},{6,7},{7,6},{8,9},{9,8},{10,11... | collective-permute-start | bytes 983048 | tf_op jit(solution)/shard_map/ppermute | solution.py:27
  16.2 8.6 %copy-start = (bf16[256,640]{1,0:T(8,128)(2,1)S(1)}, bf16[256,640]{1,0:T(8,128)(2,1)}, u32[]{:S(2)}) copy-start(bf16[256,640]{1,0:T(8,128)(2,1)} %v.5) | copy-start | bytes 983044
  25.3 12.3 %collective-permute-start.6 = (bf16[656,256]{1,0:T(8,128)(2,1)S(1)}, bf16[656,256]{1,0:T(8,128)(2,1)S(1)}, u32[]{:S(2)}, u32[]{:S(2)}) collective-permute-start(bf16[656,256]{1,0:T(8,128)(2,1)S(1)} %shard_map.59), channel_id=1, source_target_pairs={{0,4},{4,8},{8,12},{12,16},{16,20},{20,24},{24,28},{28,32},{32,36}... | collective-permute-start | bytes 1007624 | tf_op jit(solution)/shard_map/ppermute | solution.py:32
  25.9 11.8 %collective-permute-start.7 = (bf16[656,256]{1,0:T(8,128)(2,1)S(1)}, bf16[656,256]{1,0:T(8,128)(2,1)S(1)}, u32[]{:S(2)}, u32[]{:S(2)}) collective-permute-start(bf16[656,256]{1,0:T(8,128)(2,1)S(1)} %shard_map.61), channel_id=1, source_target_pairs={{0,60},{4,0},{8,4},{12,8},{16,12},{20,16},{24,20},{28,24},{32,28},... | collective-permute-start | bytes 1007624 | tf_op jit(solution)/shard_map/ppermute | solution.py:32
  31.0 1.0 %copy-start.2 = (bf16[256,640]{1,0:T(8,128)(2,1)S(1)}, bf16[256,640]{1,0:T(8,128)(2,1)}, u32[]{:S(2)}) copy-start(bf16[256,640]{1,0:T(8,128)(2,1)} %q.1) | copy-start | bytes 983044

commit v5 on v4

--- a/solution.py
+++ b/solution.py
@@ -58,7 +58,11 @@
     )(*operands)
 
 
-def weigh_kernel(heads, q, key, key_near, key_far, bias, weights_out, stats_out):
+def mark_kernel(out):
+    out[...] = jnp.zeros(out.shape, out.dtype)
+
+
+def weigh_kernel(heads, key_far, key_near, q, key, bias, weights_out, stats_out):
     stats_out[...] = jnp.zeros(stats_out.shape, jnp.float32)
     tiles = key.shape[0] // TILE
     for h in range(heads):
@@ -172,7 +176,7 @@
         copy.wait()
 
 
-def nearby_tiles(tile_coords, per_device):
+def tile_bias(tile_coords, windows, per_device, gate):
     space_count, tm_count = lax.axis_size("space"), lax.axis_size("tm")
     s, t = lax.axis_index("space"), lax.axis_index("tm")
 
@@ -183,10 +187,8 @@
     slabs = [t, partner(t, NEAR, tm_count), partner(t, FAR, tm_count)]
     columns = [s, partner(s, NEAR, space_count), partner(s, FAR, space_count)]
     key_tiles = jnp.concatenate([tiles(s, slab) for slab in slabs], axis=1)
-    return key_tiles, jnp.stack([tiles(column, t) for column in columns], axis=1)
-
-
-def tile_bias(key_tiles, queries, windows):
+    queries = jnp.stack([tiles(column, t) for column in columns], axis=1)
+    key_tiles, queries, _ = lax.optimization_barrier((key_tiles, queries, gate))
     queries = jnp.repeat(queries, TILE, axis=2)
     gap = jnp.abs(key_tiles[:, None, :, None] - queries[:, :, None, :])
     allowed = jnp.all(gap[:, :, None] <= windows[:, None, :, None, None], axis=0)
@@ -203,12 +205,13 @@
 
     k_near = exchange(key, "tm", NEAR)
     k_far = swap_slabs(key)
+    mark = call(mark_kernel, jax.ShapeDtypeStruct((8, HEAD), f32), 0)
+    sent = after(query, mark)
     q_near = exchange(query, "space", NEAR)
-    near_tiles = nearby_tiles(tile_coords, rows // TILE)
-    q_far = exchange(after(query, near_tiles[0]), "space", FAR)
+    q_far = exchange(sent, "space", FAR)
     v_far = swap_slabs(value)
     v_near = exchange(after(value, k_near), "tm", NEAR)
-    bias = tile_bias(*after(near_tiles, k_near), windows)
+    bias = tile_bias(tile_coords, windows, rows // TILE, k_near)
 
     def weigh(q, table):
         return call(
@@ -217,7 +220,7 @@
                 jax.ShapeDtypeStruct((heads, 3 * rows, rows), bf16),
                 jax.ShapeDtypeStruct((16, rows), f32),
             ),
-            heads * 3 * pair, q, key, k_near, k_far, table, exps=heads * 3 * rows * rows,
+            heads * 3 * pair, k_far, k_near, q, key, table, exps=heads * 3 * rows * rows,
         )
 
     near_weights, near_stats = weigh(q_near, bias[1])

time: 38.8 us -> 35.8 us (0.923)
  the two profiles are of different devices: /device:TPU:1 before, /device:TPU:6 now
where the time goes in v5:
time: 35.8 us; the launch traced here: 35.3 us
  starting transfers between devices  19.3 us (54%)
  Pallas kernels  6.52 us (18%)
  waiting for transfers between devices  6.09 us (17%)
  local copies, waits for them, and re-layouts  2.09 us (6%)
  other arithmetic  1.04 us (3%)
    ppermute x4, starting transfers between devices, exchange(): lax.ppermute(block, axis, [(i, partner(i, side, count)) for i in range(co...  13.6 us
    ppermute x2, starting transfers between devices, shift(): lax.ppermute(block, axis, [(i, (i + distance) % count) for i in range(cou...  5.77 us
    pallas_call x7, Pallas kernels, call(): pl.pallas_call(kernel, out_shape=out_shape, compiler_params=pltpu.Compile...  5.65 us
    ppermute x4, waiting for transfers between devices, exchange(): lax.ppermute(block, axis, [(i, partner(i, side, count)) for i in range(co...  3.34 us
    ppermute x2, waiting for transfers between devices, shift(): lax.ppermute(block, axis, [(i, (i + distance) % count) for i in range(cou...  2.75 us
    unnamed x6, local copies, waits for them, and re-layouts  0.98 us
    another operation x1, local copies, waits for them, and re-layouts, tile_bias(): queries = jnp.stack([tiles(column, t) for column in columns], axis=1)  0.9 us
    pallas_call x1, Pallas kernels, shards(): pl.pallas_call(functools.partial(combine_kernel, heads), out_shape=jax.Sh...  0.88 us
  transfers between devices with their start and end apart: 8, of which 3 were waited for; matrix products, arithmetic and copies ran while one was open for 6% of the time, Pallas kernels for 15%

profile of v5, /device:TPU:6, one launch (start us, length us, event | category | flops | bytes accessed | tf_op | source)
XLA Modules:
  0.0 35.3 jit_solution(9968030616748699155)
XLA Ops:
  0.0 0.0 copy-start.1
  0.0 0.8 %collective-permute-start.1 = (bf16[256,640]{1,0:T(8,128)(2,1)}, bf16[256,640]{1,0:T(8,128)(2,1)S(1)}, u32[]{:S(2)}, u32[]{:S(2)}) collective-permute-start(bf16[256,640]{1,0:T(8,128)(2,1)} %key.5), channel_id=1, source_target_pairs={{0,1},{1,0},{2,3},{3,2},{4,5},{5,4},{6,7},{7,6},{8,9},{9,8},{10,11... | collective-permute-start | bytes 983048 | tf_op jit(solution)/shard_map/ppermute | solution.py:27
  0.8 0.0 collective-permute-start
  0.8 1.9 %collective-permute-start.4 = (bf16[256,640]{1,0:T(8,128)(2,1)}, bf16[256,640]{1,0:T(8,128)(2,1)S(1)}, u32[]{:S(2)}, u32[]{:S(2)}) collective-permute-start(bf16[256,640]{1,0:T(8,128)(2,1)} %q.1), channel_id=1, source_target_pairs={{0,4},{4,0},{8,12},{12,8},{16,20},{20,16},{24,28},{28,24},{32,36},... | collective-permute-start | bytes 983048 | tf_op jit(solution)/shard_map/ppermute | solution.py:27
  2.8 7.6 %collective-permute-start.5 = (bf16[256,640]{1,0:T(8,128)(2,1)}, bf16[256,640]{1,0:T(8,128)(2,1)S(1)}, u32[]{:S(2)}, u32[]{:S(2)}) collective-permute-start(bf16[256,640]{1,0:T(8,128)(2,1)} %q.1), channel_id=1, source_target_pairs={{0,60},{4,8},{8,4},{12,16},{16,12},{20,24},{24,20},{28,32},{32,28}... | collective-permute-start | bytes 983048 | tf_op jit(solution)/shard_map/ppermute | solution.py:27
  10.3 0.0 collective-permute-start.3
  10.3 0.9 %dynamic-slice_bitcast_fusion.1 = (s32[3,1,4]{2,0,1:T(4,128)S(1)}, s32[3,4]{1,0:T(4,128)S(1)}, s32[3,4]{1,0:T(4,128)S(1)}, s32[3,4]{1,0:T(4,128)S(1)}, s32[3,1,4]{2,0,1:T(4,128)S(1)}) fusion(s32[3,256]{1,0:T(4,128)} %param.8, s32[]{:T(128)S(6)} %select_n.59, s32[]{:T(128)S(6)} %select_n.56, s32[]{:T(128)S(6)} %select_n.54, s32[]{:T(128)S(6)} %select_n.51, ...), kind=kLoop, calls=%fused_computation.6 | loop fusion | bytes 500 | tf_op jit(solution)/shard_map/stack | solution.py:190
  11.2 0.1 pad_add_fusion.1
  11.3 0.0 collective-permute-done.1.key_near
  11.3 0.1 broadcast_in_dim.14
  11.4 0.1 sub.30
  11.5 3.2 %collective-permute-start.2 = (bf16[256,640]{1,0:T(8,128)(2,1)}, bf16[256,640]{1,0:T(8,128)(2,1)S(1)}, u32[]{:S(2)}, u32[]{:S(2)}) collective-permute-start(bf16[256,640]{1,0:T(8,128)(2,1)} %v.5), channel_id=1, source_target_pairs={{0,1},{1,0},{2,3},{3,2},{4,5},{5,4},{6,7},{7,6},{8,9},{9,8},{10,11... | collective-permute-start | bytes 983048 | tf_op jit(solution)/shard_map/ppermute | solution.py:27
  14.7 0.1 subtract_abs_fusion
  14.8 0.8 %compare_reduce_fusion = pred[3,5,12,256]{3,2,1,0:T(8,128)(4,1)S(1)} fusion(s32[3,5]{1,0:T(4,128)} %param.9, s32[3,3,12,256]{3,2,1,0:T(8,128)S(1)} %subtract_abs_fusion), kind=kLoop, calls=%fused_computation | loop fusion | flops 230400 | bytes 156732 | tf_op jit(solution)/shard_map/reduce_and | solution.py:194
  15.7 0.0 copy-start
  15.8 0.0 collective-permute-done.4.q
  15.8 0.0 collective-permute-done.key_far
  15.8 0.0 copy-done.1
  15.8 1.3 %shard_map.57 = (bf16[5,768,256]{2,1,0:T(8,128)(2,1)S(1)}, f32[16,256]{1,0:T(8,128)S(1)}) custom-call(bf16[256,640]{1,0:T(8,128)(2,1)S(1)} %collective-permute-done.key_far, bf16[256,640]{1,0:T(8,128)(2,1)S(1)} %collective-permute-done.1.key_near, bf16[256,640]{1,0:T(8,128)(2,1)S(1)} %collective-permute-done.4.q, bf16[256,640]{1,0:T(8,128)(2,1)S(1)} %copy-done.1, ...), custom_call_target="tpu_custom_call" | custom-call | bytes 1024 | tf_op jit(solution)/shard_map/pallas_call | solution.py:53
  17.2 1.5 %collective-permute-done.5.q = bf16[256,640]{1,0:T(8,128)(2,1)S(1)} collective-permute-done((bf16[256,640]{1,0:T(8,128)(2,1)}, bf16[256,640]{1,0:T(8,128)(2,1)S(1)}, u32[]{:S(2)}, u32[]{:S(2)}) %collective-permute-start.5) | collective-permute-done | bytes 327712 | tf_op jit(solution)/shard_map/ppermute | solution.py:27
  18.7 1.3 %shard_map.58 = (bf16[5,768,256]{2,1,0:T(8,128)(2,1)S(1)}, f32[16,256]{1,0:T(8,128)S(1)}) custom-call(bf16[256,640]{1,0:T(8,128)(2,1)S(1)} %collective-permute-done.key_far, bf16[256,640]{1,0:T(8,128)(2,1)S(1)} %collective-permute-done.1.key_near, bf16[256,640]{1,0:T(8,128)(2,1)S(1)} %collective-permute-done.5.q, bf16[256,640]{1,0:T(8,128)(2,1)S(1)} %copy-done.1, ...), custom_call_target="tpu_custom_call" | custom-call | bytes 1024 | tf_op jit(solution)/shard_map/pallas_call | solution.py:53
  20.0 0.0 collective-permute-done.3.v_far
  20.0 1.8 %collective-permute-done.2.v_near = bf16[256,640]{1,0:T(8,128)(2,1)S(1)} collective-permute-done((bf16[256,640]{1,0:T(8,128)(2,1)}, bf16[256,640]{1,0:T(8,128)(2,1)S(1)}, u32[]{:S(2)}, u32[]{:S(2)}) %collective-permute-start.2) | collective-permute-done | bytes 327712 | tf_op jit(solution)/shard_map/ppermute | solution.py:27
  21.9 0.0 copy-done
  21.9 0.5 %shard_map.59 = bf16[656,256]{1,0:T(8,128)(2,1)S(1)} custom-call(bf16[5,768,256]{2,1,0:T(8,128)(2,1)S(1)} %get-tuple-element.23.near_weights, f32[16,256]{1,0:T(8,128)S(1)} %get-tuple-element.24.near_stats, bf16[5,768,256]{2,1,0:T(8,128)(2,1)S(1)} %get-tuple-element.26.far_weights, f32[16,256]{1,0:T(8,128)S(1)} %get-tuple-element.30.far_stats, ...), custom_call_target="tpu_custom_call" | custom-call | bytes 1024 | tf_op jit(solution)/shard_map/pallas_call | solution.py:53
  22.4 0.1 collective-permute-start.6
  22.5 0.5 %shard_map.61 = bf16[656,256]{1,0:T(8,128)(2,1)S(1)} custom-call(bf16[5,768,256]{2,1,0:T(8,128)(2,1)S(1)} %get-tuple-element.23.near_weights, f32[16,256]{1,0:T(8,128)S(1)} %get-tuple-element.24.near_stats, bf16[5,768,256]{2,1,0:T(8,128)(2,1)S(1)} %get-tuple-element.26.far_weights, f32[16,256]{1,0:T(8,128)S(1)} %get-tuple-element.30.far_stats, ...), custom_call_target="tpu_custom_call" | custom-call | bytes 1024 | tf_op jit(solution)/shard_map/pallas_call | solution.py:53
  23.0 5.7 %collective-permute-start.7 = (bf16[656,256]{1,0:T(8,128)(2,1)S(1)}, bf16[656,256]{1,0:T(8,128)(2,1)S(1)}, u32[]{:S(2)}, u32[]{:S(2)}) collective-permute-start(bf16[656,256]{1,0:T(8,128)(2,1)S(1)} %shard_map.61), channel_id=1, source_target_pairs={{0,60},{4,0},{8,4},{12,8},{16,12},{20,16},{24,20},{28,24},{32,28},... | collective-permute-start | bytes 1007624 | tf_op jit(solution)/shard_map/ppermute | solution.py:32
  28.7 0.0 copy-start.2
  28.7 1.0 %copy-done.2 = bf16[256,640]{1,0:T(8,128)(2,1)S(1)} copy-done((bf16[256,640]{1,0:T(8,128)(2,1)S(1)}, bf16[256,640]{1,0:T(8,128)(2,1)}, u32[]{:S(2)}) %copy-start.2) | copy-done | bytes 327704
  29.7 1.3 %shard_map.55 = (bf16[5,768,256]{2,1,0:T(8,128)(2,1)S(1)}, f32[16,256]{1,0:T(8,128)S(1)}) custom-call(bf16[256,640]{1,0:T(8,128)(2,1)S(1)} %collective-permute-done.key_far, bf16[256,640]{1,0:T(8,128)(2,1)S(1)} %collective-permute-done.1.key_near, bf16[256,640]{1,0:T(8,128)(2,1)S(1)} %copy-done.2, bf16[256,640]{1,0:T(8,128)(2,1)S(1)} %copy-done.1, ...), custom_call_target="tpu_custom_call" | custom-call | bytes 1024 | tf_op jit(solution)/shard_map/pallas_call | solution.py:53
  31.0 0.5 %shard_map.56.own = f32[640,256]{1,0:T(8,128)S(1)} custom-call(bf16[5,768,256]{2,1,0:T(8,128)(2,1)S(1)} %get-tuple-element.20.weights, f32[16,256]{1,0:T(8,128)S(1)} %get-tuple-element.21.stats, bf16[256,640]{1,0:T(8,128)(2,1)S(1)} %copy-done, bf16[256,640]{1,0:T(8,128)(2,1)S(1)} %collective-permute-done.2.v_near, ...), custom_call_target="tpu_custom_call" | custom-call | bytes 1024 | tf_op jit(solution)/shard_map/pallas_call | solution.py:53
  31.5 2.7 %collective-permute-done.6.near = bf16[656,256]{1,0:T(8,128)(2,1)S(1)} collective-permute-done((bf16[656,256]{1,0:T(8,128)(2,1)S(1)}, bf16[656,256]{1,0:T(8,128)(2,1)S(1)}, u32[]{:S(2)}, u32[]{:S(2)}) %collective-permute-start.6) | collective-permute-done | bytes 335904 | tf_op jit(solution)/shard_map/ppermute | solution.py:32
  34.3 0.1 shard_map.60
  34.4 0.0 collective-permute-done.7.other
  34.4 0.9 %shard_map.62 = bf16[256,640]{1,0:T(8,128)(2,1)} custom-call(f32[640,256]{1,0:T(8,128)S(1)} %get-tuple-element.28.merged, f32[8,256]{1,0:T(8,128)S(1)} %get-tuple-element.29.level, bf16[656,256]{1,0:T(8,128)(2,1)S(1)} %collective-permute-done.7.other), custom_call_target="tpu_custom_call" | custom-call | bytes 1024 | tf_op jit(solution)/shard_map/pallas_call | solution.py:250
  (7 shorter events, 0.1 us)
Async XLA Ops:
  0.0 15.8 %copy-start.1 = (bf16[256,640]{1,0:T(8,128)(2,1)S(1)}, bf16[256,640]{1,0:T(8,128)(2,1)}, u32[]{:S(2)}) copy-start(bf16[256,640]{1,0:T(8,128)(2,1)} %key.5) | copy-start | bytes 983044
  0.0 11.3 %collective-permute-start.1 = (bf16[256,640]{1,0:T(8,128)(2,1)}, bf16[256,640]{1,0:T(8,128)(2,1)S(1)}, u32[]{:S(2)}, u32[]{:S(2)}) collective-permute-start(bf16[256,640]{1,0:T(8,128)(2,1)} %key.5), channel_id=1, source_target_pairs={{0,1},{1,0},{2,3},{3,2},{4,5},{5,4},{6,7},{7,6},{8,9},{9,8},{10,11... | collective-permute-start | bytes 983048 | tf_op jit(solution)/shard_map/ppermute | solution.py:27
  0.8 15.0 %collective-permute-start = (bf16[256,640]{1,0:T(8,128)(2,1)}, bf16[256,640]{1,0:T(8,128)(2,1)S(1)}, u32[]{:S(2)}, u32[]{:S(2)}) collective-permute-start(bf16[256,640]{1,0:T(8,128)(2,1)} %key.5), channel_id=1, source_target_pairs={{0,64},{1,2},{2,1},{3,67},{64,0},{65,66},{66,65},{67,3},{128,192},... | collective-permute-start | bytes 983048 | tf_op jit(solution)/shard_map/ppermute | solution.py:45
  0.8 15.0 %collective-permute-start.4 = (bf16[256,640]{1,0:T(8,128)(2,1)}, bf16[256,640]{1,0:T(8,128)(2,1)S(1)}, u32[]{:S(2)}, u32[]{:S(2)}) collective-permute-start(bf16[256,640]{1,0:T(8,128)(2,1)} %q.1), channel_id=1, source_target_pairs={{0,4},{4,0},{8,12},{12,8},{16,20},{20,16},{24,28},{28,24},{32,36},... | collective-permute-start | bytes 983048 | tf_op jit(solution)/shard_map/ppermute | solution.py:27
  2.8 15.9 %collective-permute-start.5 = (bf16[256,640]{1,0:T(8,128)(2,1)}, bf16[256,640]{1,0:T(8,128)(2,1)S(1)}, u32[]{:S(2)}, u32[]{:S(2)}) collective-permute-start(bf16[256,640]{1,0:T(8,128)(2,1)} %q.1), channel_id=1, source_target_pairs={{0,60},{4,8},{8,4},{12,16},{16,12},{20,24},{24,20},{28,32},{32,28}... | collective-permute-start | bytes 983048 | tf_op jit(solution)/shard_map/ppermute | solution.py:27
  10.3 9.7 %collective-permute-start.3 = (bf16[256,640]{1,0:T(8,128)(2,1)}, bf16[256,640]{1,0:T(8,128)(2,1)S(1)}, u32[]{:S(2)}, u32[]{:S(2)}) collective-permute-start(bf16[256,640]{1,0:T(8,128)(2,1)} %v.5), channel_id=1, source_target_pairs={{0,64},{1,2},{2,1},{3,67},{64,0},{65,66},{66,65},{67,3},{128,192},... | collective-permute-start | bytes 983048 | tf_op jit(solution)/shard_map/ppermute | solution.py:45
  11.5 10.4 %collective-permute-start.2 = (bf16[256,640]{1,0:T(8,128)(2,1)}, bf16[256,640]{1,0:T(8,128)(2,1)S(1)}, u32[]{:S(2)}, u32[]{:S(2)}) collective-permute-start(bf16[256,640]{1,0:T(8,128)(2,1)} %v.5), channel_id=1, source_target_pairs={{0,1},{1,0},{2,3},{3,2},{4,5},{5,4},{6,7},{7,6},{8,9},{9,8},{10,11... | collective-permute-start | bytes 983048 | tf_op jit(solution)/shard_map/ppermute | solution.py:27
  15.7 6.2 %copy-start = (bf16[256,640]{1,0:T(8,128)(2,1)S(1)}, bf16[256,640]{1,0:T(8,128)(2,1)}, u32[]{:S(2)}) copy-start(bf16[256,640]{1,0:T(8,128)(2,1)} %v.5) | copy-start | bytes 983044
  22.4 11.9 %collective-permute-start.6 = (bf16[656,256]{1,0:T(8,128)(2,1)S(1)}, bf16[656,256]{1,0:T(8,128)(2,1)S(1)}, u32[]{:S(2)}, u32[]{:S(2)}) collective-permute-start(bf16[656,256]{1,0:T(8,128)(2,1)S(1)} %shard_map.59), channel_id=1, source_target_pairs={{0,4},{4,8},{8,12},{12,16},{16,20},{20,24},{24,28},{28,32},{32,36}... | collective-permute-start | bytes 1007624 | tf_op jit(solution)/shard_map/ppermute | solution.py:32
  23.0 11.4 %collective-permute-start.7 = (bf16[656,256]{1,0:T(8,128)(2,1)S(1)}, bf16[656,256]{1,0:T(8,128)(2,1)S(1)}, u32[]{:S(2)}, u32[]{:S(2)}) collective-permute-start(bf16[656,256]{1,0:T(8,128)(2,1)S(1)} %shard_map.61), channel_id=1, source_target_pairs={{0,60},{4,0},{8,4},{12,8},{16,12},{20,16},{24,20},{28,24},{32,28},... | collective-permute-start | bytes 1007624 | tf_op jit(solution)/shard_map/ppermute | solution.py:32
  28.7 1.0 %copy-start.2 = (bf16[256,640]{1,0:T(8,128)(2,1)S(1)}, bf16[256,640]{1,0:T(8,128)(2,1)}, u32[]{:S(2)}) copy-start(bf16[256,640]{1,0:T(8,128)(2,1)} %q.1) | copy-start | bytes 983044

commit v6 on v5

--- a/solution.py
+++ b/solution.py
@@ -89,46 +89,67 @@
         stats_out[8 + h : 9 + h, :] = peak * FACTOR + jnp.log2(total)
 
 
-def weighted(h, weights, stats, values):
+def weighted(h, weights, value, j):
     lanes = slice(h * HEAD, (h + 1) * HEAD)
-    width = values[0].shape[0]
-    summed = None
-    for j, value in enumerate(values):
-        part = lax.dot_general(
-            value[:, lanes], weights[h, j * width : (j + 1) * width, :],
-            (((0,), (0,)), ((), ())), preferred_element_type=jnp.float32,
-        )
-        summed = part if summed is None else summed + part
-    return summed * stats[h : h + 1, :]
+    width = value.shape[0]
+    return lax.dot_general(
+        value[:, lanes], weights[h, j * width : (j + 1) * width, :],
+        (((0,), (0,)), ((), ())), preferred_element_type=jnp.float32,
+    )
+
+
+def by_side(side, body, near, far):
+    odd = lax.axis_index("space") % 2
+    pl.when(odd == side)(lambda: body(*near))
+    pl.when(odd != side)(lambda: body(*far))
+
+
+def store(heads, out, stats, summed):
+    for h in range(heads):
+        rows = slice(h * HEAD, (h + 1) * HEAD)
+        out[rows, :] = (summed(h, rows) * stats[h : h + 1, :]).astype(jnp.bfloat16)
+    end = heads * HEAD
+    rest = stats[8:16, :]
+    pieces = []
+    for part in range(PARTS):
+        piece = rest.astype(jnp.bfloat16).astype(jnp.float32)
+        rest = rest - piece
+        pieces.append(piece[0:heads])
+    pieces.append(jnp.zeros((SPARE - PARTS * heads, rest.shape[1]), jnp.float32))
+    out[end : end + SPARE, :] = jnp.concatenate(pieces, axis=0).astype(jnp.bfloat16)
+
+
+def early_kernel(heads, side, near_weights, far_weights, v, v_far, out):
+    def body(weights):
+        for h in range(heads):
+            out[h * HEAD : (h + 1) * HEAD, :] = weighted(h, weights, v, 0) + weighted(h, weights, v_far, 2)
+
+    by_side(side, body, (near_weights,), (far_weights,))
+
+
+def finish_kernel(heads, side, near_weights, near_stats, far_weights, far_stats, early, v_near, out):
+    def body(weights, stats):
+        store(heads, out, stats, lambda h, rows: early[rows, :] + weighted(h, weights, v_near, 1))
+
+    by_side(side, body, (near_weights, near_stats), (far_weights, far_stats))
 
 
 def visitors_kernel(
     heads, side, near_weights, near_stats, far_weights, far_stats, v, v_near, v_far, out
 ):
-    end = heads * HEAD
-    odd = lax.axis_index("space") % 2
-
-    def sum_up(weights, stats):
-        for h in range(heads):
-            out[h * HEAD : (h + 1) * HEAD, :] = weighted(
-                h, weights, stats, (v, v_near, v_far)
-            ).astype(jnp.bfloat16)
-        rest = stats[8:16, :]
-        pieces = []
-        for part in range(PARTS):
-            piece = rest.astype(jnp.bfloat16).astype(jnp.float32)
-            rest = rest - piece
-            pieces.append(piece[0:heads])
-        pieces.append(jnp.zeros((SPARE - PARTS * heads, rest.shape[1]), jnp.float32))
-        out[end : end + SPARE, :] = jnp.concatenate(pieces, axis=0).astype(jnp.bfloat16)
-
-    pl.when(odd == side)(lambda: sum_up(near_weights, near_stats))
-    pl.when(odd != side)(lambda: sum_up(far_weights, far_stats))
+    def body(weights, stats):
+        store(
+            heads, out, stats,
+            lambda h, rows: sum(weighted(h, weights, x, j) for j, x in enumerate((v, v_near, v_far))),
+        )
+
+    by_side(side, body, (near_weights, near_stats), (far_weights, far_stats))
 
 
 def home_kernel(heads, weights, stats, v, v_near, v_far, out):
     for h in range(heads):
-        out[h * HEAD : (h + 1) * HEAD, :] = weighted(h, weights, stats, (v, v_near, v_far))
+        summed = sum(weighted(h, weights, x, j) for j, x in enumerate((v, v_near, v_far)))
+        out[h * HEAD : (h + 1) * HEAD, :] = summed * stats[h : h + 1, :]
 
 
 def level_of(ref, heads):
@@ -211,7 +232,7 @@
     q_far = exchange(sent, "space", FAR)
     v_far = swap_slabs(value)
     v_near = exchange(after(value, k_near), "tm", NEAR)
-    bias = tile_bias(tile_coords, windows, rows // TILE, k_near)
+    bias = tile_bias(after(tile_coords, k_far), windows, rows // TILE, k_near)
 
     def weigh(q, table):
         return call(
@@ -227,15 +248,19 @@
     far_weights, far_stats = weigh(q_far, after(bias[2], near_stats))
     own_weights, own_stats = weigh(query, bias[0])
 
-    def visitors(side, stats):
-        return call(
-            functools.partial(visitors_kernel, heads, side),
-            jax.ShapeDtypeStruct((width + SPARE, rows), bf16), 0,
-            near_weights, near_stats, far_weights, stats, value, v_near, v_far,
-        )
-
-    to_next = visitors(0, far_stats)
-    to_last = visitors(1, after(far_stats, to_next))
+    back = jax.ShapeDtypeStruct((width + SPARE, rows), bf16)
+    early = call(
+        functools.partial(early_kernel, heads, 0), jax.ShapeDtypeStruct((width, rows), f32), 0,
+        near_weights, far_weights, value, v_far,
+    )
+    to_next = call(
+        functools.partial(finish_kernel, heads, 0), back, 0,
+        near_weights, near_stats, far_weights, far_stats, early, v_near,
+    )
+    to_last = call(
+        functools.partial(visitors_kernel, heads, 1), back, 0,
+        near_weights, near_stats, far_weights, after(far_stats, to_next), value, v_near, v_far,
+    )
     from_last = shift(to_next, "space", 1)
     from_next = shift(to_last, "space", -1)
     own = call(

time: 35.8 us -> 35.4 us (0.989)
  waiting for transfers between devices: 6.09 us -> 5.01 us
  starting transfers between devices: 19.3 us -> 20 us
    ppermute x4, waiting for transfers between devices: 3.34 us -> 1.75 us  [exchange(): lax.ppermute(block, axis, [(i, partner(i, side, count)) for i in range(co...]
    ppermute x2, starting transfers between devices: 5.77 us -> 6.42 us  [shift(): lax.ppermute(block, axis, [(i, (i + distance) % count) for i in range(cou...]
    ppermute x2, waiting for transfers between devices: 2.75 us -> 3.25 us  [shift(): lax.ppermute(block, axis, [(i, (i + distance) % count) for i in range(cou...]
    pallas_call x7 -> x8, Pallas kernels: 5.65 us -> 5.86 us  [call(): pl.pallas_call(kernel, out_shape=out_shape, compiler_params=pltpu.Compile...]
  transfers between devices with their start and end apart: 8 -> 8, of which waited for: 3 -> 3; matrix products, arithmetic and copies ran while one was open for 6% -> 6% of each run, Pallas kernels for 15% -> 16%
where the time goes in v6:
time: 35.4 us; the launch traced here: 35 us
  starting transfers between devices  20 us (56%)
  Pallas kernels  6.74 us (19%)
  waiting for transfers between devices  5.01 us (14%)
  local copies, waits for them, and re-layouts  2.09 us (6%)
  other arithmetic  1.04 us (3%)
    ppermute x4, starting transfers between devices, exchange(): lax.ppermute(block, axis, [(i, partner(i, side, count)) for i in range(co...  13.5 us
    ppermute x2, starting transfers between devices, shift(): lax.ppermute(block, axis, [(i, (i + distance) % count) for i in range(cou...  6.42 us
    pallas_call x8, Pallas kernels, call(): pl.pallas_call(kernel, out_shape=out_shape, compiler_params=pltpu.Compile...  5.86 us
    ppermute x2, waiting for transfers between devices, shift(): lax.ppermute(block, axis, [(i, (i + distance) % count) for i in range(cou...  3.25 us
    ppermute x4, waiting for transfers between devices, exchange(): lax.ppermute(block, axis, [(i, partner(i, side, count)) for i in range(co...  1.75 us
    unnamed x6, local copies, waits for them, and re-layouts  0.98 us
    another operation x1, local copies, waits for them, and re-layouts, tile_bias(): queries = jnp.stack([tiles(column, t) for column in columns], axis=1)  0.9 us
    pallas_call x1, Pallas kernels, shards(): pl.pallas_call(functools.partial(combine_kernel, heads), out_shape=jax.Sh...  0.88 us
  transfers between devices with their start and end apart: 8, of which 3 were waited for; matrix products, arithmetic and copies ran while one was open for 6% of the time, Pallas kernels for 16%

profile of v6, /device:TPU:6, one launch (start us, length us, event | category | flops | bytes accessed | tf_op | source)
XLA Modules:
  0.0 35.0 jit_solution(16555106412956511871)
XLA Ops:
  0.0 0.0 copy-start.1
  0.0 0.8 %collective-permute-start.1 = (bf16[256,640]{1,0:T(8,128)(2,1)}, bf16[256,640]{1,0:T(8,128)(2,1)S(1)}, u32[]{:S(2)}, u32[]{:S(2)}) collective-permute-start(bf16[256,640]{1,0:T(8,128)(2,1)} %key.5), channel_id=1, source_target_pairs={{0,1},{1,0},{2,3},{3,2},{4,5},{5,4},{6,7},{7,6},{8,9},{9,8},{10,11... | collective-permute-start | bytes 983048 | tf_op jit(solution)/shard_map/ppermute | solution.py:27
  0.8 0.0 collective-permute-start
  0.8 1.9 %collective-permute-start.4 = (bf16[256,640]{1,0:T(8,128)(2,1)}, bf16[256,640]{1,0:T(8,128)(2,1)S(1)}, u32[]{:S(2)}, u32[]{:S(2)}) collective-permute-start(bf16[256,640]{1,0:T(8,128)(2,1)} %q.1), channel_id=1, source_target_pairs={{0,4},{4,0},{8,12},{12,8},{16,20},{20,16},{24,28},{28,24},{32,36},... | collective-permute-start | bytes 983048 | tf_op jit(solution)/shard_map/ppermute | solution.py:27
  2.8 7.6 %collective-permute-start.5 = (bf16[256,640]{1,0:T(8,128)(2,1)}, bf16[256,640]{1,0:T(8,128)(2,1)S(1)}, u32[]{:S(2)}, u32[]{:S(2)}) collective-permute-start(bf16[256,640]{1,0:T(8,128)(2,1)} %q.1), channel_id=1, source_target_pairs={{0,60},{4,8},{8,4},{12,16},{16,12},{20,24},{24,20},{28,32},{32,28}... | collective-permute-start | bytes 983048 | tf_op jit(solution)/shard_map/ppermute | solution.py:27
  10.3 0.0 collective-permute-start.3
  10.3 0.0 collective-permute-done.1.key_near
  10.3 3.2 %collective-permute-start.2 = (bf16[256,640]{1,0:T(8,128)(2,1)}, bf16[256,640]{1,0:T(8,128)(2,1)S(1)}, u32[]{:S(2)}, u32[]{:S(2)}) collective-permute-start(bf16[256,640]{1,0:T(8,128)(2,1)} %v.5), channel_id=1, source_target_pairs={{0,1},{1,0},{2,3},{3,2},{4,5},{5,4},{6,7},{7,6},{8,9},{9,8},{10,11... | collective-permute-start | bytes 983048 | tf_op jit(solution)/shard_map/ppermute | solution.py:27
  13.6 0.0 collective-permute-done.key_far
  13.6 0.9 %dynamic-slice_bitcast_fusion.1 = (s32[3,1,4]{2,0,1:T(4,128)S(1)}, s32[3,1,4]{2,0,1:T(4,128)S(1)}, s32[3,4]{1,0:T(4,128)S(1)}, s32[3,4]{1,0:T(4,128)S(1)}, s32[3,4]{1,0:T(4,128)S(1)}) fusion(s32[3,256]{1,0:T(4,128)} %param.8, s32[]{:T(128)S(6)} %select_n.59, s32[]{:T(128)S(6)} %select_n.61, s32[]{:T(128)S(6)} %select_n.56, s32[]{:T(128)S(6)} %select_n.54, ...), kind=kLoop, calls=%fused_computation.6 | loop fusion | bytes 500 | tf_op jit(solution)/shard_map/stack | solution.py:211
  14.5 0.1 pad_add_fusion.1
  14.6 0.1 broadcast_in_dim.14
  14.6 0.1 sub.30
  14.7 0.1 subtract_abs_fusion
  14.8 0.8 %compare_reduce_fusion = pred[3,5,12,256]{3,2,1,0:T(8,128)(4,1)S(1)} fusion(s32[3,5]{1,0:T(4,128)} %param.9, s32[3,3,12,256]{3,2,1,0:T(8,128)S(1)} %subtract_abs_fusion), kind=kLoop, calls=%fused_computation | loop fusion | flops 230400 | bytes 156732 | tf_op jit(solution)/shard_map/reduce_and | solution.py:215
  15.7 0.0 copy-start
  15.8 0.0 collective-permute-done.4.q
  15.8 0.0 copy-done.1
  15.8 1.3 %shard_map.57 = (bf16[5,768,256]{2,1,0:T(8,128)(2,1)S(1)}, f32[16,256]{1,0:T(8,128)S(1)}) custom-call(bf16[256,640]{1,0:T(8,128)(2,1)S(1)} %collective-permute-done.key_far, bf16[256,640]{1,0:T(8,128)(2,1)S(1)} %collective-permute-done.1.key_near, bf16[256,640]{1,0:T(8,128)(2,1)S(1)} %collective-permute-done.4.q, bf16[256,640]{1,0:T(8,128)(2,1)S(1)} %copy-done.1, ...), custom_call_target="tpu_custom_call" | custom-call | bytes 1024 | tf_op jit(solution)/shard_map/pallas_call | solution.py:53
  17.1 1.5 %collective-permute-done.5.q = bf16[256,640]{1,0:T(8,128)(2,1)S(1)} collective-permute-done((bf16[256,640]{1,0:T(8,128)(2,1)}, bf16[256,640]{1,0:T(8,128)(2,1)S(1)}, u32[]{:S(2)}, u32[]{:S(2)}) %collective-permute-start.5) | collective-permute-done | bytes 327712 | tf_op jit(solution)/shard_map/ppermute | solution.py:27
  18.7 1.3 %shard_map.58 = (bf16[5,768,256]{2,1,0:T(8,128)(2,1)S(1)}, f32[16,256]{1,0:T(8,128)S(1)}) custom-call(bf16[256,640]{1,0:T(8,128)(2,1)S(1)} %collective-permute-done.key_far, bf16[256,640]{1,0:T(8,128)(2,1)S(1)} %collective-permute-done.1.key_near, bf16[256,640]{1,0:T(8,128)(2,1)S(1)} %collective-permute-done.5.q, bf16[256,640]{1,0:T(8,128)(2,1)S(1)} %copy-done.1, ...), custom_call_target="tpu_custom_call" | custom-call | bytes 1024 | tf_op jit(solution)/shard_map/pallas_call | solution.py:53
  20.0 0.0 collective-permute-done.3.v_far
  20.0 0.0 copy-done
  20.0 0.4 %shard_map.59.early = f32[640,256]{1,0:T(8,128)S(1)} custom-call(bf16[5,768,256]{2,1,0:T(8,128)(2,1)S(1)} %get-tuple-element.25.near_weights, bf16[5,768,256]{2,1,0:T(8,128)(2,1)S(1)} %get-tuple-element.28.far_weights, bf16[256,640]{1,0:T(8,128)(2,1)S(1)} %copy-done, bf16[256,640]{1,0:T(8,128)(2,1)S(1)} %collective-permute-done.3.v_far), custom_call_target="tpu_custom_call" | custom-call | bytes 1024 | tf_op jit(solution)/shard_map/pallas_call | solution.py:53
  20.5 0.2 collective-permute-done.2.v_near
  20.7 0.3 shard_map.60
  21.0 0.1 collective-permute-start.6
  21.1 0.5 %shard_map.62 = bf16[656,256]{1,0:T(8,128)(2,1)S(1)} custom-call(bf16[5,768,256]{2,1,0:T(8,128)(2,1)S(1)} %get-tuple-element.25.near_weights, f32[16,256]{1,0:T(8,128)S(1)} %get-tuple-element.26.near_stats, bf16[5,768,256]{2,1,0:T(8,128)(2,1)S(1)} %get-tuple-element.28.far_weights, f32[16,256]{1,0:T(8,128)S(1)} %get-tuple-element.32.far_stats, ...), custom_call_target="tpu_custom_call" | custom-call | bytes 1024 | tf_op jit(solution)/shard_map/pallas_call | solution.py:53
  21.6 6.3 %collective-permute-start.7 = (bf16[656,256]{1,0:T(8,128)(2,1)S(1)}, bf16[656,256]{1,0:T(8,128)(2,1)S(1)}, u32[]{:S(2)}, u32[]{:S(2)}) collective-permute-start(bf16[656,256]{1,0:T(8,128)(2,1)S(1)} %shard_map.62), channel_id=1, source_target_pairs={{0,60},{4,0},{8,4},{12,8},{16,12},{20,16},{24,20},{28,24},{32,28},... | collective-permute-start | bytes 1007624 | tf_op jit(solution)/shard_map/ppermute | solution.py:32
  28.0 0.0 copy-start.2
  28.0 1.0 %copy-done.2 = bf16[256,640]{1,0:T(8,128)(2,1)S(1)} copy-done((bf16[256,640]{1,0:T(8,128)(2,1)S(1)}, bf16[256,640]{1,0:T(8,128)(2,1)}, u32[]{:S(2)}) %copy-start.2) | copy-done | bytes 327704
  28.9 1.3 %shard_map.55 = (bf16[5,768,256]{2,1,0:T(8,128)(2,1)S(1)}, f32[16,256]{1,0:T(8,128)S(1)}) custom-call(bf16[256,640]{1,0:T(8,128)(2,1)S(1)} %collective-permute-done.key_far, bf16[256,640]{1,0:T(8,128)(2,1)S(1)} %collective-permute-done.1.key_near, bf16[256,640]{1,0:T(8,128)(2,1)S(1)} %copy-done.2, bf16[256,640]{1,0:T(8,128)(2,1)S(1)} %copy-done.1, ...), custom_call_target="tpu_custom_call" | custom-call | bytes 1024 | tf_op jit(solution)/shard_map/pallas_call | solution.py:53
  30.3 0.5 %shard_map.56.own = f32[640,256]{1,0:T(8,128)S(1)} custom-call(bf16[5,768,256]{2,1,0:T(8,128)(2,1)S(1)} %get-tuple-element.22.weights, f32[16,256]{1,0:T(8,128)S(1)} %get-tuple-element.23.stats, bf16[256,640]{1,0:T(8,128)(2,1)S(1)} %copy-done, bf16[256,640]{1,0:T(8,128)(2,1)S(1)} %collective-permute-done.2.v_near, ...), custom_call_target="tpu_custom_call" | custom-call | bytes 1024 | tf_op jit(solution)/shard_map/pallas_call | solution.py:53
  30.8 3.3 %collective-permute-done.6.near = bf16[656,256]{1,0:T(8,128)(2,1)S(1)} collective-permute-done((bf16[656,256]{1,0:T(8,128)(2,1)S(1)}, bf16[656,256]{1,0:T(8,128)(2,1)S(1)}, u32[]{:S(2)}, u32[]{:S(2)}) %collective-permute-start.6) | collective-permute-done | bytes 335904 | tf_op jit(solution)/shard_map/ppermute | solution.py:32
  34.0 0.1 shard_map.61
  34.1 0.0 collective-permute-done.7.other
  34.1 0.9 %shard_map.63 = bf16[256,640]{1,0:T(8,128)(2,1)} custom-call(f32[640,256]{1,0:T(8,128)S(1)} %get-tuple-element.30.merged, f32[8,256]{1,0:T(8,128)S(1)} %get-tuple-element.31.level, bf16[656,256]{1,0:T(8,128)(2,1)S(1)} %collective-permute-done.7.other), custom_call_target="tpu_custom_call" | custom-call | bytes 1024 | tf_op jit(solution)/shard_map/pallas_call | solution.py:275
  (7 shorter events, 0.1 us)
Async XLA Ops:
  0.0 15.8 %copy-start.1 = (bf16[256,640]{1,0:T(8,128)(2,1)S(1)}, bf16[256,640]{1,0:T(8,128)(2,1)}, u32[]{:S(2)}) copy-start(bf16[256,640]{1,0:T(8,128)(2,1)} %key.5) | copy-start | bytes 983044
  0.0 10.3 %collective-permute-start.1 = (bf16[256,640]{1,0:T(8,128)(2,1)}, bf16[256,640]{1,0:T(8,128)(2,1)S(1)}, u32[]{:S(2)}, u32[]{:S(2)}) collective-permute-start(bf16[256,640]{1,0:T(8,128)(2,1)} %key.5), channel_id=1, source_target_pairs={{0,1},{1,0},{2,3},{3,2},{4,5},{5,4},{6,7},{7,6},{8,9},{9,8},{10,11... | collective-permute-start | bytes 983048 | tf_op jit(solution)/shard_map/ppermute | solution.py:27
  0.8 12.7 %collective-permute-start = (bf16[256,640]{1,0:T(8,128)(2,1)}, bf16[256,640]{1,0:T(8,128)(2,1)S(1)}, u32[]{:S(2)}, u32[]{:S(2)}) collective-permute-start(bf16[256,640]{1,0:T(8,128)(2,1)} %key.5), channel_id=1, source_target_pairs={{0,64},{1,2},{2,1},{3,67},{64,0},{65,66},{66,65},{67,3},{128,192},... | collective-permute-start | bytes 983048 | tf_op jit(solution)/shard_map/ppermute | solution.py:45
  0.8 14.9 %collective-permute-start.4 = (bf16[256,640]{1,0:T(8,128)(2,1)}, bf16[256,640]{1,0:T(8,128)(2,1)S(1)}, u32[]{:S(2)}, u32[]{:S(2)}) collective-permute-start(bf16[256,640]{1,0:T(8,128)(2,1)} %q.1), channel_id=1, source_target_pairs={{0,4},{4,0},{8,12},{12,8},{16,20},{20,16},{24,28},{28,24},{32,36},... | collective-permute-start | bytes 983048 | tf_op jit(solution)/shard_map/ppermute | solution.py:27
  2.8 15.9 %collective-permute-start.5 = (bf16[256,640]{1,0:T(8,128)(2,1)}, bf16[256,640]{1,0:T(8,128)(2,1)S(1)}, u32[]{:S(2)}, u32[]{:S(2)}) collective-permute-start(bf16[256,640]{1,0:T(8,128)(2,1)} %q.1), channel_id=1, source_target_pairs={{0,60},{4,8},{8,4},{12,16},{16,12},{20,24},{24,20},{28,32},{32,28}... | collective-permute-start | bytes 983048 | tf_op jit(solution)/shard_map/ppermute | solution.py:27
  10.3 9.7 %collective-permute-start.3 = (bf16[256,640]{1,0:T(8,128)(2,1)}, bf16[256,640]{1,0:T(8,128)(2,1)S(1)}, u32[]{:S(2)}, u32[]{:S(2)}) collective-permute-start(bf16[256,640]{1,0:T(8,128)(2,1)} %v.5), channel_id=1, source_target_pairs={{0,64},{1,2},{2,1},{3,67},{64,0},{65,66},{66,65},{67,3},{128,192},... | collective-permute-start | bytes 983048 | tf_op jit(solution)/shard_map/ppermute | solution.py:45
  10.3 10.3 %collective-permute-start.2 = (bf16[256,640]{1,0:T(8,128)(2,1)}, bf16[256,640]{1,0:T(8,128)(2,1)S(1)}, u32[]{:S(2)}, u32[]{:S(2)}) collective-permute-start(bf16[256,640]{1,0:T(8,128)(2,1)} %v.5), channel_id=1, source_target_pairs={{0,1},{1,0},{2,3},{3,2},{4,5},{5,4},{6,7},{7,6},{8,9},{9,8},{10,11... | collective-permute-start | bytes 983048 | tf_op jit(solution)/shard_map/ppermute | solution.py:27
  15.7 4.4 %copy-start = (bf16[256,640]{1,0:T(8,128)(2,1)S(1)}, bf16[256,640]{1,0:T(8,128)(2,1)}, u32[]{:S(2)}) copy-start(bf16[256,640]{1,0:T(8,128)(2,1)} %v.5) | copy-start | bytes 983044
  21.0 13.0 %collective-permute-start.6 = (bf16[656,256]{1,0:T(8,128)(2,1)S(1)}, bf16[656,256]{1,0:T(8,128)(2,1)S(1)}, u32[]{:S(2)}, u32[]{:S(2)}) collective-permute-start(bf16[656,256]{1,0:T(8,128)(2,1)S(1)} %shard_map.60), channel_id=1, source_target_pairs={{0,4},{4,8},{8,12},{12,16},{16,20},{20,24},{24,28},{28,32},{32,36}... | collective-permute-start | bytes 1007624 | tf_op jit(solution)/shard_map/ppermute | solution.py:32
  21.6 12.5 %collective-permute-start.7 = (bf16[656,256]{1,0:T(8,128)(2,1)S(1)}, bf16[656,256]{1,0:T(8,128)(2,1)S(1)}, u32[]{:S(2)}, u32[]{:S(2)}) collective-permute-start(bf16[656,256]{1,0:T(8,128)(2,1)S(1)} %shard_map.62), channel_id=1, source_target_pairs={{0,60},{4,0},{8,4},{12,8},{16,12},{20,16},{24,20},{28,24},{32,28},... | collective-permute-start | bytes 1007624 | tf_op jit(solution)/shard_map/ppermute | solution.py:32
  28.0 1.0 %copy-start.2 = (bf16[256,640]{1,0:T(8,128)(2,1)S(1)}, bf16[256,640]{1,0:T(8,128)(2,1)}, u32[]{:S(2)}) copy-start(bf16[256,640]{1,0:T(8,128)(2,1)} %q.1) | copy-start | bytes 983044

commit v7 on v6

--- a/solution.py
+++ b/solution.py
@@ -60,6 +60,10 @@
 
 def mark_kernel(out):
     out[...] = jnp.zeros(out.shape, out.dtype)
+
+
+def weigh_if_kernel(heads, parity, *refs):
+    pl.when(lax.axis_index("space") % 2 == parity)(lambda: weigh_kernel(heads, *refs))
 
 
 def weigh_kernel(heads, key_far, key_near, q, key, bias, weights_out, stats_out):
@@ -234,33 +238,39 @@
     v_near = exchange(after(value, k_near), "tm", NEAR)
     bias = tile_bias(after(tile_coords, k_far), windows, rows // TILE, k_near)
 
-    def weigh(q, table):
+    def weigh(kernel, q, table):
         return call(
-            functools.partial(weigh_kernel, heads),
+            kernel,
             (
                 jax.ShapeDtypeStruct((heads, 3 * rows, rows), bf16),
                 jax.ShapeDtypeStruct((16, rows), f32),
             ),
-            heads * 3 * pair, k_far, k_near, q, key, table, exps=heads * 3 * rows * rows,
+            heads * 3 * pair, k_far, k_near, q, key, table,
+            exps=heads * 3 * rows * rows,
         )
 
-    near_weights, near_stats = weigh(q_near, bias[1])
-    far_weights, far_stats = weigh(q_far, after(bias[2], near_stats))
-    own_weights, own_stats = weigh(query, bias[0])
-
+    always = functools.partial(weigh_kernel, heads)
+    near_weights, near_stats = weigh(always, q_near, bias[1])
+    odd_weights, odd_stats = weigh(
+        functools.partial(weigh_if_kernel, heads, 1), q_far, after(bias[2], near_stats)
+    )
     back = jax.ShapeDtypeStruct((width + SPARE, rows), bf16)
     early = call(
         functools.partial(early_kernel, heads, 0), jax.ShapeDtypeStruct((width, rows), f32), 0,
-        near_weights, far_weights, value, v_far,
+        near_weights, odd_weights, value, v_far,
     )
     to_next = call(
         functools.partial(finish_kernel, heads, 0), back, 0,
-        near_weights, near_stats, far_weights, far_stats, early, v_near,
+        near_weights, near_stats, odd_weights, odd_stats, early, v_near,
+    )
+    even_weights, even_stats = weigh(
+        functools.partial(weigh_if_kernel, heads, 0), q_far, after(bias[2], to_next)
     )
     to_last = call(
         functools.partial(visitors_kernel, heads, 1), back, 0,
-        near_weights, near_stats, far_weights, after(far_stats, to_next), value, v_near, v_far,
-    )
+        near_weights, near_stats, even_weights, even_stats, value, v_near, v_far,
+    )
+    own_weights, own_stats = weigh(always, query, after(bias[0], to_last))
     from_last = shift(to_next, "space", 1)
     from_next = shift(to_last, "space", -1)
     own = call(

time: 35.4 us -> 34.9 us (0.986)
  starting transfers between devices: 20 us -> 18.6 us
  waiting for transfers between devices: 5.01 us -> 5.99 us
    ppermute x4, waiting for transfers between devices: 1.75 us -> 3.12 us  [exchange(): lax.ppermute(block, axis, [(i, partner(i, side, count)) for i in range(co...]
    ppermute x2, starting transfers between devices: 6.42 us -> 5.09 us  [shift(): lax.ppermute(block, axis, [(i, (i + distance) % count) for i in range(cou...]
    ppermute x2, waiting for transfers between devices: 3.25 us -> 2.87 us  [shift(): lax.ppermute(block, axis, [(i, (i + distance) % count) for i in range(cou...]
    pallas_call x8 -> x9, Pallas kernels: 5.86 us -> 5.86 us  [call(): pl.pallas_call(kernel, out_shape=out_shape, compiler_params=pltpu.Compile...]
where the time goes in v7:
time: 34.9 us; the launch traced here: 34.7 us
  starting transfers between devices  18.6 us (53%)
  Pallas kernels  6.75 us (19%)
  waiting for transfers between devices  5.99 us (17%)
  local copies, waits for them, and re-layouts  2.09 us (6%)
  other arithmetic  1.04 us (3%)
    ppermute x4, starting transfers between devices, exchange(): lax.ppermute(block, axis, [(i, partner(i, side, count)) for i in range(co...  13.5 us
    pallas_call x9, Pallas kernels, call(): pl.pallas_call(kernel, out_shape=out_shape, compiler_params=pltpu.Compile...  5.86 us
    ppermute x2, starting transfers between devices, shift(): lax.ppermute(block, axis, [(i, (i + distance) % count) for i in range(cou...  5.09 us
    ppermute x4, waiting for transfers between devices, exchange(): lax.ppermute(block, axis, [(i, partner(i, side, count)) for i in range(co...  3.12 us
    ppermute x2, waiting for transfers between devices, shift(): lax.ppermute(block, axis, [(i, (i + distance) % count) for i in range(cou...  2.87 us
    unnamed x6, local copies, waits for them, and re-layouts  0.98 us
    another operation x1, local copies, waits for them, and re-layouts, tile_bias(): queries = jnp.stack([tiles(column, t) for column in columns], axis=1)  0.9 us
    pallas_call x1, Pallas kernels, shards(): pl.pallas_call(functools.partial(combine_kernel, heads), out_shape=jax.Sh...  0.88 us
  transfers between devices with their start and end apart: 8, of which 3 were waited for; matrix products, arithmetic and copies ran while one was open for 6% of the time, Pallas kernels for 16%

profile of v7, /device:TPU:6, one launch (start us, length us, event | category | flops | bytes accessed | tf_op | source)
XLA Modules:
  0.0 34.7 jit_solution(18157946339089909812)
XLA Ops:
  0.0 0.0 copy-start
  0.0 0.8 %collective-permute-start.1 = (bf16[256,640]{1,0:T(8,128)(2,1)}, bf16[256,640]{1,0:T(8,128)(2,1)S(1)}, u32[]{:S(2)}, u32[]{:S(2)}) collective-permute-start(bf16[256,640]{1,0:T(8,128)(2,1)} %key.3), channel_id=1, source_target_pairs={{0,1},{1,0},{2,3},{3,2},{4,5},{5,4},{6,7},{7,6},{8,9},{9,8},{10,11... | collective-permute-start | bytes 983048 | tf_op jit(solution)/shard_map/ppermute | solution.py:27
  0.8 0.0 collective-permute-start
  0.8 1.9 %collective-permute-start.2 = (bf16[256,640]{1,0:T(8,128)(2,1)}, bf16[256,640]{1,0:T(8,128)(2,1)S(1)}, u32[]{:S(2)}, u32[]{:S(2)}) collective-permute-start(bf16[256,640]{1,0:T(8,128)(2,1)} %q.1), channel_id=1, source_target_pairs={{0,4},{4,0},{8,12},{12,8},{16,20},{20,16},{24,28},{28,24},{32,36},... | collective-permute-start | bytes 983048 | tf_op jit(solution)/shard_map/ppermute | solution.py:27
  2.8 7.6 %collective-permute-start.3 = (bf16[256,640]{1,0:T(8,128)(2,1)}, bf16[256,640]{1,0:T(8,128)(2,1)S(1)}, u32[]{:S(2)}, u32[]{:S(2)}) collective-permute-start(bf16[256,640]{1,0:T(8,128)(2,1)} %q.1), channel_id=1, source_target_pairs={{0,60},{4,8},{8,4},{12,16},{16,12},{20,24},{24,20},{28,32},{32,28}... | collective-permute-start | bytes 983048 | tf_op jit(solution)/shard_map/ppermute | solution.py:27
  10.3 0.0 collective-permute-start.4
  10.3 0.0 collective-permute-done.1.key_near.refs_1_
  10.3 3.2 %collective-permute-start.5 = (bf16[256,640]{1,0:T(8,128)(2,1)}, bf16[256,640]{1,0:T(8,128)(2,1)S(1)}, u32[]{:S(2)}, u32[]{:S(2)}) collective-permute-start(bf16[256,640]{1,0:T(8,128)(2,1)} %v.5), channel_id=1, source_target_pairs={{0,1},{1,0},{2,3},{3,2},{4,5},{5,4},{6,7},{7,6},{8,9},{9,8},{10,11... | collective-permute-start | bytes 983048 | tf_op jit(solution)/shard_map/ppermute | solution.py:27
  13.6 0.0 collective-permute-done.key_far.refs_0_
  13.6 0.9 %dynamic-slice_bitcast_fusion.1 = (s32[3,1,4]{2,0,1:T(4,128)S(1)}, s32[3,1,4]{2,0,1:T(4,128)S(1)}, s32[3,4]{1,0:T(4,128)S(1)}, s32[3,4]{1,0:T(4,128)S(1)}, s32[3,4]{1,0:T(4,128)S(1)}) fusion(s32[3,256]{1,0:T(4,128)} %param.8, s32[]{:T(128)S(6)} %select_n.59, s32[]{:T(128)S(6)} %select_n.61, s32[]{:T(128)S(6)} %select_n.56, s32[]{:T(128)S(6)} %select_n.54, ...), kind=kLoop, calls=%fused_computation.6 | loop fusion | bytes 500 | tf_op jit(solution)/shard_map/stack | solution.py:215
  14.5 0.1 pad_add_fusion.1
  14.6 0.1 broadcast_in_dim.14
  14.6 0.1 sub.30
  14.7 0.1 subtract_abs_fusion
  14.8 0.8 %compare_reduce_fusion = pred[3,5,12,256]{3,2,1,0:T(8,128)(4,1)S(1)} fusion(s32[3,5]{1,0:T(4,128)} %param.9, s32[3,3,12,256]{3,2,1,0:T(8,128)S(1)} %subtract_abs_fusion), kind=kLoop, calls=%fused_computation | loop fusion | flops 230400 | bytes 156732 | tf_op jit(solution)/shard_map/reduce_and | solution.py:219
  15.7 0.0 copy-start.1
  15.8 0.0 collective-permute-done.2.q
  15.8 0.0 copy-done
  15.8 1.3 %shard_map.55 = (bf16[5,768,256]{2,1,0:T(8,128)(2,1)S(1)}, f32[16,256]{1,0:T(8,128)S(1)}) custom-call(bf16[256,640]{1,0:T(8,128)(2,1)S(1)} %collective-permute-done.key_far.refs_0_, bf16[256,640]{1,0:T(8,128)(2,1)S(1)} %collective-permute-done.1.key_near.refs_1_, bf16[256,640]{1,0:T(8,128)(2,1)S(1)} %collective-permute-done.2.q, ...), custom_call_target="tpu_custom_call" | custom-call | bytes 1024 | tf_op jit(solution)/shard_map/pallas_call | solution.py:53
  17.1 1.5 %collective-permute-done.3.refs_2_ = bf16[256,640]{1,0:T(8,128)(2,1)S(1)} collective-permute-done((bf16[256,640]{1,0:T(8,128)(2,1)}, bf16[256,640]{1,0:T(8,128)(2,1)S(1)}, u32[]{:S(2)}, u32[]{:S(2)}) %collective-permute-start.3) | collective-permute-done | bytes 327712 | tf_op jit(solution)/shard_map/ppermute | solution.py:27
  18.7 0.0 collective-permute-done.4.v_far
  18.7 0.0 copy-done.1
  18.7 0.4 %shard_map.57.early = f32[640,256]{1,0:T(8,128)S(1)} custom-call(bf16[5,768,256]{2,1,0:T(8,128)(2,1)S(1)} %get-tuple-element.25.near_weights, bf16[5,768,256]{2,1,0:T(8,128)(2,1)S(1)} %get-tuple-element.28.far_weights, bf16[256,640]{1,0:T(8,128)(2,1)S(1)} %copy-done.1, bf16[256,640]{1,0:T(8,128)(2,1)S(1)} %collective-permute-done.4.v_far), custom_call_target="tpu_custom_call" | custom-call | bytes 1024 | tf_op jit(solution)/shard_map/pallas_call | solution.py:53
  19.1 1.6 %collective-permute-done.5.v_near = bf16[256,640]{1,0:T(8,128)(2,1)S(1)} collective-permute-done((bf16[256,640]{1,0:T(8,128)(2,1)}, bf16[256,640]{1,0:T(8,128)(2,1)S(1)}, u32[]{:S(2)}, u32[]{:S(2)}) %collective-permute-start.5) | collective-permute-done | bytes 327712 | tf_op jit(solution)/shard_map/ppermute | solution.py:27
  20.7 0.3 shard_map.58
  21.0 0.1 collective-permute-start.6
  21.1 1.3 %shard_map.59 = (bf16[5,768,256]{2,1,0:T(8,128)(2,1)S(1)}, f32[16,256]{1,0:T(8,128)S(1)}) custom-call(bf16[256,640]{1,0:T(8,128)(2,1)S(1)} %collective-permute-done.key_far.refs_0_, bf16[256,640]{1,0:T(8,128)(2,1)S(1)} %collective-permute-done.1.key_near.refs_1_, bf16[256,640]{1,0:T(8,128)(2,1)S(1)} %collective-permute-done.3.refs_2_, ...), custom_call_target="tpu_custom_call" | custom-call | bytes 1024 | tf_op jit(solution)/shard_map/pallas_call | solution.py:53
  22.4 0.5 %shard_map.60 = bf16[656,256]{1,0:T(8,128)(2,1)S(1)} custom-call(bf16[5,768,256]{2,1,0:T(8,128)(2,1)S(1)} %get-tuple-element.25.near_weights, f32[16,256]{1,0:T(8,128)S(1)} %get-tuple-element.26.near_stats, bf16[5,768,256]{2,1,0:T(8,128)(2,1)S(1)} %get-tuple-element.32.far_weights, f32[16,256]{1,0:T(8,128)S(1)} %get-tuple-element.33.far_stats, ...), custom_call_target="tpu_custom_call" | custom-call | bytes 1024 | tf_op jit(solution)/shard_map/pallas_call | solution.py:53
  23.0 5.0 %collective-permute-start.7 = (bf16[656,256]{1,0:T(8,128)(2,1)S(1)}, bf16[656,256]{1,0:T(8,128)(2,1)S(1)}, u32[]{:S(2)}, u32[]{:S(2)}) collective-permute-start(bf16[656,256]{1,0:T(8,128)(2,1)S(1)} %shard_map.60), channel_id=1, source_target_pairs={{0,60},{4,0},{8,4},{12,8},{16,12},{20,16},{24,20},{28,24},{32,28},... | collective-permute-start | bytes 1007624 | tf_op jit(solution)/shard_map/ppermute | solution.py:32
  28.0 0.0 copy-start.2
  28.0 1.0 %copy-done.2 = bf16[256,640]{1,0:T(8,128)(2,1)S(1)} copy-done((bf16[256,640]{1,0:T(8,128)(2,1)S(1)}, bf16[256,640]{1,0:T(8,128)(2,1)}, u32[]{:S(2)}) %copy-start.2) | copy-done | bytes 327704
  29.0 1.3 %shard_map.61 = (bf16[5,768,256]{2,1,0:T(8,128)(2,1)S(1)}, f32[16,256]{1,0:T(8,128)S(1)}) custom-call(bf16[256,640]{1,0:T(8,128)(2,1)S(1)} %collective-permute-done.key_far.refs_0_, bf16[256,640]{1,0:T(8,128)(2,1)S(1)} %collective-permute-done.1.key_near.refs_1_, bf16[256,640]{1,0:T(8,128)(2,1)S(1)} %copy-done.2, bf16[256,640]{1,0:T(8,128)(2,1)S(1)} %copy-done, ...), custom_call_target="tpu_custom_call" | custom-call | bytes 1024 | tf_op jit(solution)/shard_map/pallas_call | solution.py:53
  30.3 0.5 %shard_map.62.own = f32[640,256]{1,0:T(8,128)S(1)} custom-call(bf16[5,768,256]{2,1,0:T(8,128)(2,1)S(1)} %get-tuple-element.35.weights, f32[16,256]{1,0:T(8,128)S(1)} %get-tuple-element.36.stats, bf16[256,640]{1,0:T(8,128)(2,1)S(1)} %copy-done.1, bf16[256,640]{1,0:T(8,128)(2,1)S(1)} %collective-permute-done.5.v_near, ...), custom_call_target="tpu_custom_call" | custom-call | bytes 1024 | tf_op jit(solution)/shard_map/pallas_call | solution.py:53
  30.8 2.9 %collective-permute-done.6.near = bf16[656,256]{1,0:T(8,128)(2,1)S(1)} collective-permute-done((bf16[656,256]{1,0:T(8,128)(2,1)S(1)}, bf16[656,256]{1,0:T(8,128)(2,1)S(1)}, u32[]{:S(2)}, u32[]{:S(2)}) %collective-permute-start.6) | collective-permute-done | bytes 335904 | tf_op jit(solution)/shard_map/ppermute | solution.py:32
  33.7 0.1 shard_map.63
  33.8 0.0 collective-permute-done.7.other
  33.8 0.9 %shard_map.64 = bf16[256,640]{1,0:T(8,128)(2,1)} custom-call(f32[640,256]{1,0:T(8,128)S(1)} %get-tuple-element.37.merged, f32[8,256]{1,0:T(8,128)S(1)} %get-tuple-element.38.level, bf16[656,256]{1,0:T(8,128)(2,1)S(1)} %collective-permute-done.7.other), custom_call_target="tpu_custom_call" | custom-call | bytes 1024 | tf_op jit(solution)/shard_map/pallas_call | solution.py:285
  (8 shorter events, 0.1 us)
Async XLA Ops:
  0.0 15.8 %copy-start = (bf16[256,640]{1,0:T(8,128)(2,1)S(1)}, bf16[256,640]{1,0:T(8,128)(2,1)}, u32[]{:S(2)}) copy-start(bf16[256,640]{1,0:T(8,128)(2,1)} %key.3) | copy-start | bytes 983044
  0.0 10.3 %collective-permute-start.1 = (bf16[256,640]{1,0:T(8,128)(2,1)}, bf16[256,640]{1,0:T(8,128)(2,1)S(1)}, u32[]{:S(2)}, u32[]{:S(2)}) collective-permute-start(bf16[256,640]{1,0:T(8,128)(2,1)} %key.3), channel_id=1, source_target_pairs={{0,1},{1,0},{2,3},{3,2},{4,5},{5,4},{6,7},{7,6},{8,9},{9,8},{10,11... | collective-permute-start | bytes 983048 | tf_op jit(solution)/shard_map/ppermute | solution.py:27
  0.8 12.7 %collective-permute-start = (bf16[256,640]{1,0:T(8,128)(2,1)}, bf16[256,640]{1,0:T(8,128)(2,1)S(1)}, u32[]{:S(2)}, u32[]{:S(2)}) collective-permute-start(bf16[256,640]{1,0:T(8,128)(2,1)} %key.3), channel_id=1, source_target_pairs={{0,64},{1,2},{2,1},{3,67},{64,0},{65,66},{66,65},{67,3},{128,192},... | collective-permute-start | bytes 983048 | tf_op jit(solution)/shard_map/ppermute | solution.py:45
  0.8 14.9 %collective-permute-start.2 = (bf16[256,640]{1,0:T(8,128)(2,1)}, bf16[256,640]{1,0:T(8,128)(2,1)S(1)}, u32[]{:S(2)}, u32[]{:S(2)}) collective-permute-start(bf16[256,640]{1,0:T(8,128)(2,1)} %q.1), channel_id=1, source_target_pairs={{0,4},{4,0},{8,12},{12,8},{16,20},{20,16},{24,28},{28,24},{32,36},... | collective-permute-start | bytes 983048 | tf_op jit(solution)/shard_map/ppermute | solution.py:27
  2.8 15.9 %collective-permute-start.3 = (bf16[256,640]{1,0:T(8,128)(2,1)}, bf16[256,640]{1,0:T(8,128)(2,1)S(1)}, u32[]{:S(2)}, u32[]{:S(2)}) collective-permute-start(bf16[256,640]{1,0:T(8,128)(2,1)} %q.1), channel_id=1, source_target_pairs={{0,60},{4,8},{8,4},{12,16},{16,12},{20,24},{24,20},{28,32},{32,28}... | collective-permute-start | bytes 983048 | tf_op jit(solution)/shard_map/ppermute | solution.py:27
  10.3 8.3 %collective-permute-start.4 = (bf16[256,640]{1,0:T(8,128)(2,1)}, bf16[256,640]{1,0:T(8,128)(2,1)S(1)}, u32[]{:S(2)}, u32[]{:S(2)}) collective-permute-start(bf16[256,640]{1,0:T(8,128)(2,1)} %v.5), channel_id=1, source_target_pairs={{0,64},{1,2},{2,1},{3,67},{64,0},{65,66},{66,65},{67,3},{128,192},... | collective-permute-start | bytes 983048 | tf_op jit(solution)/shard_map/ppermute | solution.py:45
  10.3 10.3 %collective-permute-start.5 = (bf16[256,640]{1,0:T(8,128)(2,1)}, bf16[256,640]{1,0:T(8,128)(2,1)S(1)}, u32[]{:S(2)}, u32[]{:S(2)}) collective-permute-start(bf16[256,640]{1,0:T(8,128)(2,1)} %v.5), channel_id=1, source_target_pairs={{0,1},{1,0},{2,3},{3,2},{4,5},{5,4},{6,7},{7,6},{8,9},{9,8},{10,11... | collective-permute-start | bytes 983048 | tf_op jit(solution)/shard_map/ppermute | solution.py:27
  15.7 3.0 %copy-start.1 = (bf16[256,640]{1,0:T(8,128)(2,1)S(1)}, bf16[256,640]{1,0:T(8,128)(2,1)}, u32[]{:S(2)}) copy-start(bf16[256,640]{1,0:T(8,128)(2,1)} %v.5) | copy-start | bytes 983044
  21.0 12.7 %collective-permute-start.6 = (bf16[656,256]{1,0:T(8,128)(2,1)S(1)}, bf16[656,256]{1,0:T(8,128)(2,1)S(1)}, u32[]{:S(2)}, u32[]{:S(2)}) collective-permute-start(bf16[656,256]{1,0:T(8,128)(2,1)S(1)} %shard_map.58), channel_id=1, source_target_pairs={{0,4},{4,8},{8,12},{12,16},{16,20},{20,24},{24,28},{28,32},{32,36}... | collective-permute-start | bytes 1007624 | tf_op jit(solution)/shard_map/ppermute | solution.py:32
  23.0 10.8 %collective-permute-start.7 = (bf16[656,256]{1,0:T(8,128)(2,1)S(1)}, bf16[656,256]{1,0:T(8,128)(2,1)S(1)}, u32[]{:S(2)}, u32[]{:S(2)}) collective-permute-start(bf16[656,256]{1,0:T(8,128)(2,1)S(1)} %shard_map.60), channel_id=1, source_target_pairs={{0,60},{4,0},{8,4},{12,8},{16,12},{20,16},{24,20},{28,24},{32,28},... | collective-permute-start | bytes 1007624 | tf_op jit(solution)/shard_map/ppermute | solution.py:32
  28.0 1.0 %copy-start.2 = (bf16[256,640]{1,0:T(8,128)(2,1)S(1)}, bf16[256,640]{1,0:T(8,128)(2,1)}, u32[]{:S(2)}) copy-start(bf16[256,640]{1,0:T(8,128)(2,1)} %q.1) | copy-start | bytes 983044

commit v8 on v7

--- a/solution.py
+++ b/solution.py
@@ -123,17 +123,17 @@
     out[end : end + SPARE, :] = jnp.concatenate(pieces, axis=0).astype(jnp.bfloat16)
 
 
-def early_kernel(heads, side, near_weights, far_weights, v, v_far, out):
+def early_kernel(heads, side, near_weights, far_weights, v, v_near, out):
     def body(weights):
         for h in range(heads):
-            out[h * HEAD : (h + 1) * HEAD, :] = weighted(h, weights, v, 0) + weighted(h, weights, v_far, 2)
+            out[h * HEAD : (h + 1) * HEAD, :] = weighted(h, weights, v, 0) + weighted(h, weights, v_near, 1)
 
     by_side(side, body, (near_weights,), (far_weights,))
 
 
-def finish_kernel(heads, side, near_weights, near_stats, far_weights, far_stats, early, v_near, out):
+def finish_kernel(heads, side, near_weights, near_stats, far_weights, far_stats, early, v_far, out):
     def body(weights, stats):
-        store(heads, out, stats, lambda h, rows: early[rows, :] + weighted(h, weights, v_near, 1))
+        store(heads, out, stats, lambda h, rows: early[rows, :] + weighted(h, weights, v_far, 2))
 
     by_side(side, body, (near_weights, near_stats), (far_weights, far_stats))
 
@@ -234,8 +234,8 @@
     sent = after(query, mark)
     q_near = exchange(query, "space", NEAR)
     q_far = exchange(sent, "space", FAR)
-    v_far = swap_slabs(value)
-    v_near = exchange(after(value, k_near), "tm", NEAR)
+    v_near = exchange(value, "tm", NEAR)
+    v_far = swap_slabs(after(value, k_near))
     bias = tile_bias(after(tile_coords, k_far), windows, rows // TILE, k_near)
 
     def weigh(kernel, q, table):
@@ -257,11 +257,11 @@
     back = jax.ShapeDtypeStruct((width + SPARE, rows), bf16)
     early = call(
         functools.partial(early_kernel, heads, 0), jax.ShapeDtypeStruct((width, rows), f32), 0,
-        near_weights, odd_weights, value, v_far,
+        near_weights, odd_weights, value, v_near,
     )
     to_next = call(
         functools.partial(finish_kernel, heads, 0), back, 0,
-        near_weights, near_stats, odd_weights, odd_stats, early, v_near,
+        near_weights, near_stats, odd_weights, odd_stats, early, v_far,
     )
     even_weights, even_stats = weigh(
         functools.partial(weigh_if_kernel, heads, 0), q_far, after(bias[2], to_next)

time: 34.9 us -> 34.9 us (level)
  starting transfers between devices: 18.6 us -> 15.9 us
  waiting for transfers between devices: 5.99 us -> 8.67 us
    ppermute x4, starting transfers between devices: 13.5 us -> 11.5 us  [exchange(): lax.ppermute(block, axis, [(i, partner(i, side, count)) for i in range(co...]
    ppermute x4, waiting for transfers between devices: 3.12 us -> 4.98 us  [exchange(): lax.ppermute(block, axis, [(i, partner(i, side, count)) for i in range(co...]
    ppermute x2, waiting for transfers between devices: 2.87 us -> 3.69 us  [shift(): lax.ppermute(block, axis, [(i, (i + distance) % count) for i in range(cou...]
    ppermute x2, starting transfers between devices: 5.09 us -> 4.41 us  [shift(): lax.ppermute(block, axis, [(i, (i + distance) % count) for i in range(cou...]
where the time goes in v8:
time: 34.9 us; the launch traced here: 34.7 us
  starting transfers between devices  15.9 us (46%)
  waiting for transfers between devices  8.67 us (25%)
  Pallas kernels  6.77 us (19%)
  local copies, waits for them, and re-layouts  2.11 us (6%)
  other arithmetic  1.04 us (3%)
    ppermute x4, starting transfers between devices, exchange(): lax.ppermute(block, axis, [(i, partner(i, side, count)) for i in range(co...  11.5 us
    pallas_call x9, Pallas kernels, call(): pl.pallas_call(kernel, out_shape=out_shape, compiler_params=pltpu.Compile...  5.88 us
    ppermute x4, waiting for transfers between devices, exchange(): lax.ppermute(block, axis, [(i, partner(i, side, count)) for i in range(co...  4.98 us
    ppermute x2, starting transfers between devices, shift(): lax.ppermute(block, axis, [(i, (i + distance) % count) for i in range(cou...  4.41 us
    ppermute x2, waiting for transfers between devices, shift(): lax.ppermute(block, axis, [(i, (i + distance) % count) for i in range(cou...  3.69 us
    unnamed x6, local copies, waits for them, and re-layouts  0.98 us
    another operation x1, local copies, waits for them, and re-layouts, tile_bias(): queries = jnp.stack([tiles(column, t) for column in columns], axis=1)  0.92 us
    pallas_call x1, Pallas kernels, shards(): pl.pallas_call(functools.partial(combine_kernel, heads), out_shape=jax.Sh...  0.88 us
  transfers between devices with their start and end apart: 8, of which 3 were waited for; matrix products, arithmetic and copies ran while one was open for 6% of the time, Pallas kernels for 16%

profile of v8, /device:TPU:6, one launch (start us, length us, event | category | flops | bytes accessed | tf_op | source)
XLA Modules:
  0.0 34.7 jit_solution(17579962514677569845)
XLA Ops:
  0.0 0.0 copy-start
  0.0 0.8 %collective-permute-start.1 = (bf16[256,640]{1,0:T(8,128)(2,1)}, bf16[256,640]{1,0:T(8,128)(2,1)S(1)}, u32[]{:S(2)}, u32[]{:S(2)}) collective-permute-start(bf16[256,640]{1,0:T(8,128)(2,1)} %key.3), channel_id=1, source_target_pairs={{0,1},{1,0},{2,3},{3,2},{4,5},{5,4},{6,7},{7,6},{8,9},{9,8},{10,11... | collective-permute-start | bytes 983048 | tf_op jit(solution)/shard_map/ppermute | solution.py:27
  0.8 0.0 collective-permute-start
  0.8 1.9 %collective-permute-start.2 = (bf16[256,640]{1,0:T(8,128)(2,1)}, bf16[256,640]{1,0:T(8,128)(2,1)S(1)}, u32[]{:S(2)}, u32[]{:S(2)}) collective-permute-start(bf16[256,640]{1,0:T(8,128)(2,1)} %q.1), channel_id=1, source_target_pairs={{0,4},{4,0},{8,12},{12,8},{16,20},{20,16},{24,28},{28,24},{32,36},... | collective-permute-start | bytes 983048 | tf_op jit(solution)/shard_map/ppermute | solution.py:27
  2.8 7.6 %collective-permute-start.3 = (bf16[256,640]{1,0:T(8,128)(2,1)}, bf16[256,640]{1,0:T(8,128)(2,1)S(1)}, u32[]{:S(2)}, u32[]{:S(2)}) collective-permute-start(bf16[256,640]{1,0:T(8,128)(2,1)} %q.1), channel_id=1, source_target_pairs={{0,60},{4,8},{8,4},{12,16},{16,12},{20,24},{24,20},{28,32},{32,28}... | collective-permute-start | bytes 983048 | tf_op jit(solution)/shard_map/ppermute | solution.py:27
  10.3 1.2 %collective-permute-start.4 = (bf16[256,640]{1,0:T(8,128)(2,1)}, bf16[256,640]{1,0:T(8,128)(2,1)S(1)}, u32[]{:S(2)}, u32[]{:S(2)}) collective-permute-start(bf16[256,640]{1,0:T(8,128)(2,1)} %v.5), channel_id=1, source_target_pairs={{0,1},{1,0},{2,3},{3,2},{4,5},{5,4},{6,7},{7,6},{8,9},{9,8},{10,11... | collective-permute-start | bytes 983048 | tf_op jit(solution)/shard_map/ppermute | solution.py:27
  11.5 0.0 collective-permute-done.1.key_near.refs_1_
  11.5 0.0 collective-permute-start.5
  11.5 0.0 collective-permute-done.key_far.refs_0_
  11.5 0.9 %dynamic-slice_bitcast_fusion.1 = (s32[3,1,4]{2,0,1:T(4,128)S(1)}, s32[3,1,4]{2,0,1:T(4,128)S(1)}, s32[3,4]{1,0:T(4,128)S(1)}, s32[3,4]{1,0:T(4,128)S(1)}, s32[3,4]{1,0:T(4,128)S(1)}) fusion(s32[3,256]{1,0:T(4,128)} %param.8, s32[]{:T(128)S(6)} %select_n.59, s32[]{:T(128)S(6)} %select_n.61, s32[]{:T(128)S(6)} %select_n.56, s32[]{:T(128)S(6)} %select_n.54, ...), kind=kLoop, calls=%fused_computation.6 | loop fusion | bytes 500 | tf_op jit(solution)/shard_map/stack | solution.py:215
  12.5 0.1 pad_add_fusion.1
  12.5 0.1 broadcast_in_dim.14
  12.6 0.1 sub.30
  12.7 0.1 subtract_abs_fusion
  12.8 0.8 %compare_reduce_fusion = pred[3,5,12,256]{3,2,1,0:T(8,128)(4,1)S(1)} fusion(s32[3,5]{1,0:T(4,128)} %param.9, s32[3,3,12,256]{3,2,1,0:T(8,128)S(1)} %subtract_abs_fusion), kind=kLoop, calls=%fused_computation | loop fusion | flops 230400 | bytes 156732 | tf_op jit(solution)/shard_map/reduce_and | solution.py:219
  13.7 0.0 copy-start.1
  13.8 0.0 collective-permute-done.2.q
  13.8 0.0 copy-done
  13.8 1.3 %shard_map.55 = (bf16[5,768,256]{2,1,0:T(8,128)(2,1)S(1)}, f32[16,256]{1,0:T(8,128)S(1)}) custom-call(bf16[256,640]{1,0:T(8,128)(2,1)S(1)} %collective-permute-done.key_far.refs_0_, bf16[256,640]{1,0:T(8,128)(2,1)S(1)} %collective-permute-done.1.key_near.refs_1_, bf16[256,640]{1,0:T(8,128)(2,1)S(1)} %collective-permute-done.2.q, ...), custom_call_target="tpu_custom_call" | custom-call | bytes 1024 | tf_op jit(solution)/shard_map/pallas_call | solution.py:53
  15.1 3.5 %collective-permute-done.3.refs_2_ = bf16[256,640]{1,0:T(8,128)(2,1)S(1)} collective-permute-done((bf16[256,640]{1,0:T(8,128)(2,1)}, bf16[256,640]{1,0:T(8,128)(2,1)S(1)}, u32[]{:S(2)}, u32[]{:S(2)}) %collective-permute-start.3) | collective-permute-done | bytes 327712 | tf_op jit(solution)/shard_map/ppermute | solution.py:27
  18.7 1.4 %collective-permute-done.4.v_near = bf16[256,640]{1,0:T(8,128)(2,1)S(1)} collective-permute-done((bf16[256,640]{1,0:T(8,128)(2,1)}, bf16[256,640]{1,0:T(8,128)(2,1)S(1)}, u32[]{:S(2)}, u32[]{:S(2)}) %collective-permute-start.4) | collective-permute-done | bytes 327712 | tf_op jit(solution)/shard_map/ppermute | solution.py:27
  20.1 0.0 copy-done.1
  20.1 0.4 %shard_map.57.early = f32[640,256]{1,0:T(8,128)S(1)} custom-call(bf16[5,768,256]{2,1,0:T(8,128)(2,1)S(1)} %get-tuple-element.25.near_weights, bf16[5,768,256]{2,1,0:T(8,128)(2,1)S(1)} %get-tuple-element.28.far_weights, bf16[256,640]{1,0:T(8,128)(2,1)S(1)} %copy-done.1, bf16[256,640]{1,0:T(8,128)(2,1)S(1)} %collective-permute-done.4.v_near), custom_call_target="tpu_custom_call" | custom-call | bytes 1024 | tf_op jit(solution)/shard_map/pallas_call | solution.py:53
  20.5 0.0 collective-permute-done.5.v_far
  20.5 0.3 shard_map.58
  20.9 0.1 collective-permute-start.6
  20.9 1.4 %shard_map.59 = (bf16[5,768,256]{2,1,0:T(8,128)(2,1)S(1)}, f32[16,256]{1,0:T(8,128)S(1)}) custom-call(bf16[256,640]{1,0:T(8,128)(2,1)S(1)} %collective-permute-done.key_far.refs_0_, bf16[256,640]{1,0:T(8,128)(2,1)S(1)} %collective-permute-done.1.key_near.refs_1_, bf16[256,640]{1,0:T(8,128)(2,1)S(1)} %collective-permute-done.3.refs_2_, ...), custom_call_target="tpu_custom_call" | custom-call | bytes 1024 | tf_op jit(solution)/shard_map/pallas_call | solution.py:53
  22.3 0.5 %shard_map.60 = bf16[656,256]{1,0:T(8,128)(2,1)S(1)} custom-call(bf16[5,768,256]{2,1,0:T(8,128)(2,1)S(1)} %get-tuple-element.25.near_weights, f32[16,256]{1,0:T(8,128)S(1)} %get-tuple-element.26.near_stats, bf16[5,768,256]{2,1,0:T(8,128)(2,1)S(1)} %get-tuple-element.32.far_weights, f32[16,256]{1,0:T(8,128)S(1)} %get-tuple-element.33.far_stats, ...), custom_call_target="tpu_custom_call" | custom-call | bytes 1024 | tf_op jit(solution)/shard_map/pallas_call | solution.py:53
  22.8 4.3 %collective-permute-start.7 = (bf16[656,256]{1,0:T(8,128)(2,1)S(1)}, bf16[656,256]{1,0:T(8,128)(2,1)S(1)}, u32[]{:S(2)}, u32[]{:S(2)}) collective-permute-start(bf16[656,256]{1,0:T(8,128)(2,1)S(1)} %shard_map.60), channel_id=1, source_target_pairs={{0,60},{4,0},{8,4},{12,8},{16,12},{20,16},{24,20},{28,24},{32,28},... | collective-permute-start | bytes 1007624 | tf_op jit(solution)/shard_map/ppermute | solution.py:32
  27.2 0.0 copy-start.2
  27.2 1.0 %copy-done.2 = bf16[256,640]{1,0:T(8,128)(2,1)S(1)} copy-done((bf16[256,640]{1,0:T(8,128)(2,1)S(1)}, bf16[256,640]{1,0:T(8,128)(2,1)}, u32[]{:S(2)}) %copy-start.2) | copy-done | bytes 327704
  28.2 1.3 %shard_map.61 = (bf16[5,768,256]{2,1,0:T(8,128)(2,1)S(1)}, f32[16,256]{1,0:T(8,128)S(1)}) custom-call(bf16[256,640]{1,0:T(8,128)(2,1)S(1)} %collective-permute-done.key_far.refs_0_, bf16[256,640]{1,0:T(8,128)(2,1)S(1)} %collective-permute-done.1.key_near.refs_1_, bf16[256,640]{1,0:T(8,128)(2,1)S(1)} %copy-done.2, bf16[256,640]{1,0:T(8,128)(2,1)S(1)} %copy-done, ...), custom_call_target="tpu_custom_call" | custom-call | bytes 1024 | tf_op jit(solution)/shard_map/pallas_call | solution.py:53
  29.5 0.5 %shard_map.62.own = f32[640,256]{1,0:T(8,128)S(1)} custom-call(bf16[5,768,256]{2,1,0:T(8,128)(2,1)S(1)} %get-tuple-element.35.weights, f32[16,256]{1,0:T(8,128)S(1)} %get-tuple-element.36.stats, bf16[256,640]{1,0:T(8,128)(2,1)S(1)} %copy-done.1, bf16[256,640]{1,0:T(8,128)(2,1)S(1)} %collective-permute-done.4.v_near, ...), custom_call_target="tpu_custom_call" | custom-call | bytes 1024 | tf_op jit(solution)/shard_map/pallas_call | solution.py:53
  30.0 3.7 %collective-permute-done.6.near = bf16[656,256]{1,0:T(8,128)(2,1)S(1)} collective-permute-done((bf16[656,256]{1,0:T(8,128)(2,1)S(1)}, bf16[656,256]{1,0:T(8,128)(2,1)S(1)}, u32[]{:S(2)}, u32[]{:S(2)}) %collective-permute-start.6) | collective-permute-done | bytes 335904 | tf_op jit(solution)/shard_map/ppermute | solution.py:32
  33.7 0.1 shard_map.63
  33.8 0.0 collective-permute-done.7.other
  33.8 0.9 %shard_map.64 = bf16[256,640]{1,0:T(8,128)(2,1)} custom-call(f32[640,256]{1,0:T(8,128)S(1)} %get-tuple-element.37.merged, f32[8,256]{1,0:T(8,128)S(1)} %get-tuple-element.38.level, bf16[656,256]{1,0:T(8,128)(2,1)S(1)} %collective-permute-done.7.other), custom_call_target="tpu_custom_call" | custom-call | bytes 1024 | tf_op jit(solution)/shard_map/pallas_call | solution.py:285
  (8 shorter events, 0.1 us)
Async XLA Ops:
  0.0 13.8 %copy-start = (bf16[256,640]{1,0:T(8,128)(2,1)S(1)}, bf16[256,640]{1,0:T(8,128)(2,1)}, u32[]{:S(2)}) copy-start(bf16[256,640]{1,0:T(8,128)(2,1)} %key.3) | copy-start | bytes 983044
  0.0 11.5 %collective-permute-start.1 = (bf16[256,640]{1,0:T(8,128)(2,1)}, bf16[256,640]{1,0:T(8,128)(2,1)S(1)}, u32[]{:S(2)}, u32[]{:S(2)}) collective-permute-start(bf16[256,640]{1,0:T(8,128)(2,1)} %key.3), channel_id=1, source_target_pairs={{0,1},{1,0},{2,3},{3,2},{4,5},{5,4},{6,7},{7,6},{8,9},{9,8},{10,11... | collective-permute-start | bytes 983048 | tf_op jit(solution)/shard_map/ppermute | solution.py:27
  0.8 10.7 %collective-permute-start = (bf16[256,640]{1,0:T(8,128)(2,1)}, bf16[256,640]{1,0:T(8,128)(2,1)S(1)}, u32[]{:S(2)}, u32[]{:S(2)}) collective-permute-start(bf16[256,640]{1,0:T(8,128)(2,1)} %key.3), channel_id=1, source_target_pairs={{0,64},{1,2},{2,1},{3,67},{64,0},{65,66},{66,65},{67,3},{128,192},... | collective-permute-start | bytes 983048 | tf_op jit(solution)/shard_map/ppermute | solution.py:45
  0.8 12.9 %collective-permute-start.2 = (bf16[256,640]{1,0:T(8,128)(2,1)}, bf16[256,640]{1,0:T(8,128)(2,1)S(1)}, u32[]{:S(2)}, u32[]{:S(2)}) collective-permute-start(bf16[256,640]{1,0:T(8,128)(2,1)} %q.1), channel_id=1, source_target_pairs={{0,4},{4,0},{8,12},{12,8},{16,20},{20,16},{24,28},{28,24},{32,36},... | collective-permute-start | bytes 983048 | tf_op jit(solution)/shard_map/ppermute | solution.py:27
  2.8 15.9 %collective-permute-start.3 = (bf16[256,640]{1,0:T(8,128)(2,1)}, bf16[256,640]{1,0:T(8,128)(2,1)S(1)}, u32[]{:S(2)}, u32[]{:S(2)}) collective-permute-start(bf16[256,640]{1,0:T(8,128)(2,1)} %q.1), channel_id=1, source_target_pairs={{0,60},{4,8},{8,4},{12,16},{16,12},{20,24},{24,20},{28,32},{32,28}... | collective-permute-start | bytes 983048 | tf_op jit(solution)/shard_map/ppermute | solution.py:27
  10.3 9.8 %collective-permute-start.4 = (bf16[256,640]{1,0:T(8,128)(2,1)}, bf16[256,640]{1,0:T(8,128)(2,1)S(1)}, u32[]{:S(2)}, u32[]{:S(2)}) collective-permute-start(bf16[256,640]{1,0:T(8,128)(2,1)} %v.5), channel_id=1, source_target_pairs={{0,1},{1,0},{2,3},{3,2},{4,5},{5,4},{6,7},{7,6},{8,9},{9,8},{10,11... | collective-permute-start | bytes 983048 | tf_op jit(solution)/shard_map/ppermute | solution.py:27
  11.5 9.0 %collective-permute-start.5 = (bf16[256,640]{1,0:T(8,128)(2,1)}, bf16[256,640]{1,0:T(8,128)(2,1)S(1)}, u32[]{:S(2)}, u32[]{:S(2)}) collective-permute-start(bf16[256,640]{1,0:T(8,128)(2,1)} %v.5), channel_id=1, source_target_pairs={{0,64},{1,2},{2,1},{3,67},{64,0},{65,66},{66,65},{67,3},{128,192},... | collective-permute-start | bytes 983048 | tf_op jit(solution)/shard_map/ppermute | solution.py:45
  13.7 6.4 %copy-start.1 = (bf16[256,640]{1,0:T(8,128)(2,1)S(1)}, bf16[256,640]{1,0:T(8,128)(2,1)}, u32[]{:S(2)}) copy-start(bf16[256,640]{1,0:T(8,128)(2,1)} %v.5) | copy-start | bytes 983044
  20.9 12.8 %collective-permute-start.6 = (bf16[656,256]{1,0:T(8,128)(2,1)S(1)}, bf16[656,256]{1,0:T(8,128)(2,1)S(1)}, u32[]{:S(2)}, u32[]{:S(2)}) collective-permute-start(bf16[656,256]{1,0:T(8,128)(2,1)S(1)} %shard_map.58), channel_id=1, source_target_pairs={{0,4},{4,8},{8,12},{12,16},{16,20},{20,24},{24,28},{28,32},{32,36}... | collective-permute-start | bytes 1007624 | tf_op jit(solution)/shard_map/ppermute | solution.py:32
  22.8 11.0 %collective-permute-start.7 = (bf16[656,256]{1,0:T(8,128)(2,1)S(1)}, bf16[656,256]{1,0:T(8,128)(2,1)S(1)}, u32[]{:S(2)}, u32[]{:S(2)}) collective-permute-start(bf16[656,256]{1,0:T(8,128)(2,1)S(1)} %shard_map.60), channel_id=1, source_target_pairs={{0,60},{4,0},{8,4},{12,8},{16,12},{20,16},{24,20},{28,24},{32,28},... | collective-permute-start | bytes 1007624 | tf_op jit(solution)/shard_map/ppermute | solution.py:32
  27.2 1.0 %copy-start.2 = (bf16[256,640]{1,0:T(8,128)(2,1)S(1)}, bf16[256,640]{1,0:T(8,128)(2,1)}, u32[]{:S(2)}) copy-start(bf16[256,640]{1,0:T(8,128)(2,1)} %q.1) | copy-start | bytes 983044

commit v9 on v7

--- a/solution.py
+++ b/solution.py
@@ -168,22 +168,8 @@
     return [part * scale for part in parts]
 
 
-def merge_kernel(heads, own, stats, near, out, level_out):
-    levels = [stats[8 : 8 + heads, :], level_of(near, heads)]
-    top = jnp.maximum(levels[0], levels[1])
-    parts = [jnp.exp2(level - top) for level in levels]
-    scale = 1.0 / (parts[0] + parts[1])
-    level_out[...] = jnp.zeros(level_out.shape, jnp.float32)
-    level_out[0:heads, :] = top + jnp.log2(parts[0] + parts[1])
-    parts = [part * scale for part in parts]
-    for h in range(heads):
-        rows = slice(h * HEAD, (h + 1) * HEAD)
-        result = own[rows, :] * parts[0][h : h + 1]
-        out[rows, :] = result + near[rows, :].astype(jnp.float32) * parts[1][h : h + 1]
-
-
-def combine_kernel(heads, merged, level, other, out, block, sems):
-    parts = shares([level[0:heads, :], level_of(other, heads)])
+def combine_kernel(heads, own, stats, last, other, out, block, sems):
+    parts = shares([stats[8 : 8 + heads, :], level_of(last, heads), level_of(other, heads)])
     rows = block.shape[0]
     half = rows // 2
     copies = []
@@ -191,8 +177,9 @@
         lanes = slice(i * half, (i + 1) * half)
         for h in range(heads):
             features = slice(h * HEAD, (h + 1) * HEAD)
-            result = merged[features, lanes] * parts[0][h : h + 1, lanes]
-            result = result + other[features, lanes].astype(jnp.float32) * parts[1][h : h + 1, lanes]
+            result = own[features, lanes] * parts[0][h : h + 1, lanes]
+            for part, ref in zip(parts[1:], (last, other)):
+                result = result + ref[features, lanes].astype(jnp.float32) * part[h : h + 1, lanes]
             block[lanes, features] = result.astype(jnp.bfloat16).T
         copy = pltpu.make_async_copy(block.at[lanes], out.at[lanes], sems.at[i])
         copy.start()
@@ -277,11 +264,6 @@
         functools.partial(home_kernel, heads), jax.ShapeDtypeStruct((width, rows), f32),
         heads * 3 * pair, own_weights, own_stats, value, v_near, v_far,
     )
-    merged, level = call(
-        functools.partial(merge_kernel, heads),
-        (jax.ShapeDtypeStruct((width, rows), f32), jax.ShapeDtypeStruct((8, rows), f32)), 0,
-        own, own_stats, from_last,
-    )
     return pl.pallas_call(
         functools.partial(combine_kernel, heads),
         out_shape=jax.ShapeDtypeStruct((rows, width), bf16),
@@ -289,7 +271,7 @@
         scratch_shapes=[pltpu.VMEM((rows, width), bf16), pltpu.SemaphoreType.DMA((2,))],
         compiler_params=pltpu.CompilerParams(vmem_limit_bytes=40 * 1024 * 1024),
         cost_estimate=pl.CostEstimate(flops=0, bytes_accessed=1024, transcendentals=0),
-    )(merged, level, from_next)
+    )(own, own_stats, from_last, from_next)
 
 
 def solution(mesh):

time: 34.9 us -> 34.8 us (level)
    pallas_call x9 -> x8, Pallas kernels: 5.86 us -> 5.75 us  [call(): pl.pallas_call(kernel, out_shape=out_shape, compiler_params=pltpu.Compile...]
where the time goes in v9:
time: 34.8 us; the launch traced here: 34.6 us
  starting transfers between devices  18.6 us (53%)
  Pallas kernels  6.71 us (19%)
  waiting for transfers between devices  5.99 us (17%)
  local copies, waits for them, and re-layouts  2.09 us (6%)
  other arithmetic  1.04 us (3%)
    ppermute x4, starting transfers between devices, exchange(): lax.ppermute(block, axis, [(i, partner(i, side, count)) for i in range(co...  13.5 us
    pallas_call x8, Pallas kernels, call(): pl.pallas_call(kernel, out_shape=out_shape, compiler_params=pltpu.Compile...  5.75 us
    ppermute x2, starting transfers between devices, shift(): lax.ppermute(block, axis, [(i, (i + distance) % count) for i in range(cou...  5.09 us
    ppermute x4, waiting for transfers between devices, exchange(): lax.ppermute(block, axis, [(i, partner(i, side, count)) for i in range(co...  3.12 us
    ppermute x2, waiting for transfers between devices, shift(): lax.ppermute(block, axis, [(i, (i + distance) % count) for i in range(cou...  2.87 us
    unnamed x6, local copies, waits for them, and re-layouts  0.98 us
    pallas_call x1, Pallas kernels, shards(): pl.pallas_call(functools.partial(combine_kernel, heads), out_shape=jax.Sh...  0.96 us
    another operation x1, local copies, waits for them, and re-layouts, tile_bias(): queries = jnp.stack([tiles(column, t) for column in columns], axis=1)  0.9 us
  transfers between devices with their start and end apart: 8, of which 3 were waited for; matrix products, arithmetic and copies ran while one was open for 6% of the time, Pallas kernels for 16%

profile of v9, /device:TPU:6, one launch (start us, length us, event | category | flops | bytes accessed | tf_op | source)
XLA Modules:
  0.0 34.6 jit_solution(15208011728140035457)
XLA Ops:
  0.0 0.0 copy-start
  0.0 0.8 %collective-permute-start.1 = (bf16[256,640]{1,0:T(8,128)(2,1)}, bf16[256,640]{1,0:T(8,128)(2,1)S(1)}, u32[]{:S(2)}, u32[]{:S(2)}) collective-permute-start(bf16[256,640]{1,0:T(8,128)(2,1)} %key.3), channel_id=1, source_target_pairs={{0,1},{1,0},{2,3},{3,2},{4,5},{5,4},{6,7},{7,6},{8,9},{9,8},{10,11... | collective-permute-start | bytes 983048 | tf_op jit(solution)/shard_map/ppermute | solution.py:27
  0.8 0.0 collective-permute-start
  0.8 1.9 %collective-permute-start.2 = (bf16[256,640]{1,0:T(8,128)(2,1)}, bf16[256,640]{1,0:T(8,128)(2,1)S(1)}, u32[]{:S(2)}, u32[]{:S(2)}) collective-permute-start(bf16[256,640]{1,0:T(8,128)(2,1)} %q.1), channel_id=1, source_target_pairs={{0,4},{4,0},{8,12},{12,8},{16,20},{20,16},{24,28},{28,24},{32,36},... | collective-permute-start | bytes 983048 | tf_op jit(solution)/shard_map/ppermute | solution.py:27
  2.8 7.6 %collective-permute-start.3 = (bf16[256,640]{1,0:T(8,128)(2,1)}, bf16[256,640]{1,0:T(8,128)(2,1)S(1)}, u32[]{:S(2)}, u32[]{:S(2)}) collective-permute-start(bf16[256,640]{1,0:T(8,128)(2,1)} %q.1), channel_id=1, source_target_pairs={{0,60},{4,8},{8,4},{12,16},{16,12},{20,24},{24,20},{28,32},{32,28}... | collective-permute-start | bytes 983048 | tf_op jit(solution)/shard_map/ppermute | solution.py:27
  10.3 0.0 collective-permute-start.4
  10.3 0.0 collective-permute-done.1.key_near.refs_1_
  10.3 3.2 %collective-permute-start.5 = (bf16[256,640]{1,0:T(8,128)(2,1)}, bf16[256,640]{1,0:T(8,128)(2,1)S(1)}, u32[]{:S(2)}, u32[]{:S(2)}) collective-permute-start(bf16[256,640]{1,0:T(8,128)(2,1)} %v.5), channel_id=1, source_target_pairs={{0,1},{1,0},{2,3},{3,2},{4,5},{5,4},{6,7},{7,6},{8,9},{9,8},{10,11... | collective-permute-start | bytes 983048 | tf_op jit(solution)/shard_map/ppermute | solution.py:27
  13.6 0.0 collective-permute-done.key_far.refs_0_
  13.6 0.9 %dynamic-slice_bitcast_fusion.1 = (s32[3,1,4]{2,0,1:T(4,128)S(1)}, s32[3,1,4]{2,0,1:T(4,128)S(1)}, s32[3,4]{1,0:T(4,128)S(1)}, s32[3,4]{1,0:T(4,128)S(1)}, s32[3,4]{1,0:T(4,128)S(1)}) fusion(s32[3,256]{1,0:T(4,128)} %param.8, s32[]{:T(128)S(6)} %select_n.59, s32[]{:T(128)S(6)} %select_n.61, s32[]{:T(128)S(6)} %select_n.56, s32[]{:T(128)S(6)} %select_n.54, ...), kind=kLoop, calls=%fused_computation.6 | loop fusion | bytes 500 | tf_op jit(solution)/shard_map/stack | solution.py:202
  14.5 0.1 pad_add_fusion.1
  14.6 0.1 broadcast_in_dim.14
  14.6 0.1 sub.30
  14.7 0.1 subtract_abs_fusion
  14.8 0.8 %compare_reduce_fusion = pred[3,5,12,256]{3,2,1,0:T(8,128)(4,1)S(1)} fusion(s32[3,5]{1,0:T(4,128)} %param.9, s32[3,3,12,256]{3,2,1,0:T(8,128)S(1)} %subtract_abs_fusion), kind=kLoop, calls=%fused_computation | loop fusion | flops 230400 | bytes 156732 | tf_op jit(solution)/shard_map/reduce_and | solution.py:206
  15.7 0.0 copy-start.1
  15.8 0.0 collective-permute-done.2.q
  15.8 0.0 copy-done
  15.8 1.3 %shard_map.55 = (bf16[5,768,256]{2,1,0:T(8,128)(2,1)S(1)}, f32[16,256]{1,0:T(8,128)S(1)}) custom-call(bf16[256,640]{1,0:T(8,128)(2,1)S(1)} %collective-permute-done.key_far.refs_0_, bf16[256,640]{1,0:T(8,128)(2,1)S(1)} %collective-permute-done.1.key_near.refs_1_, bf16[256,640]{1,0:T(8,128)(2,1)S(1)} %collective-permute-done.2.q, ...), custom_call_target="tpu_custom_call" | custom-call | bytes 1024 | tf_op jit(solution)/shard_map/pallas_call | solution.py:53
  17.1 1.5 %collective-permute-done.3.refs_2_ = bf16[256,640]{1,0:T(8,128)(2,1)S(1)} collective-permute-done((bf16[256,640]{1,0:T(8,128)(2,1)}, bf16[256,640]{1,0:T(8,128)(2,1)S(1)}, u32[]{:S(2)}, u32[]{:S(2)}) %collective-permute-start.3) | collective-permute-done | bytes 327712 | tf_op jit(solution)/shard_map/ppermute | solution.py:27
  18.7 0.0 collective-permute-done.4.v_far
  18.7 0.0 copy-done.1
  18.7 0.4 %shard_map.57.early = f32[640,256]{1,0:T(8,128)S(1)} custom-call(bf16[5,768,256]{2,1,0:T(8,128)(2,1)S(1)} %get-tuple-element.23.near_weights, bf16[5,768,256]{2,1,0:T(8,128)(2,1)S(1)} %get-tuple-element.26.far_weights, bf16[256,640]{1,0:T(8,128)(2,1)S(1)} %copy-done.1, bf16[256,640]{1,0:T(8,128)(2,1)S(1)} %collective-permute-done.4.v_far), custom_call_target="tpu_custom_call" | custom-call | bytes 1024 | tf_op jit(solution)/shard_map/pallas_call | solution.py:53
  19.1 1.6 %collective-permute-done.5.v_near = bf16[256,640]{1,0:T(8,128)(2,1)S(1)} collective-permute-done((bf16[256,640]{1,0:T(8,128)(2,1)}, bf16[256,640]{1,0:T(8,128)(2,1)S(1)}, u32[]{:S(2)}, u32[]{:S(2)}) %collective-permute-start.5) | collective-permute-done | bytes 327712 | tf_op jit(solution)/shard_map/ppermute | solution.py:27
  20.7 0.3 shard_map.58
  21.0 0.1 collective-permute-start.6
  21.1 1.3 %shard_map.59 = (bf16[5,768,256]{2,1,0:T(8,128)(2,1)S(1)}, f32[16,256]{1,0:T(8,128)S(1)}) custom-call(bf16[256,640]{1,0:T(8,128)(2,1)S(1)} %collective-permute-done.key_far.refs_0_, bf16[256,640]{1,0:T(8,128)(2,1)S(1)} %collective-permute-done.1.key_near.refs_1_, bf16[256,640]{1,0:T(8,128)(2,1)S(1)} %collective-permute-done.3.refs_2_, ...), custom_call_target="tpu_custom_call" | custom-call | bytes 1024 | tf_op jit(solution)/shard_map/pallas_call | solution.py:53
  22.4 0.5 %shard_map.60 = bf16[656,256]{1,0:T(8,128)(2,1)S(1)} custom-call(bf16[5,768,256]{2,1,0:T(8,128)(2,1)S(1)} %get-tuple-element.23.near_weights, f32[16,256]{1,0:T(8,128)S(1)} %get-tuple-element.24.near_stats, bf16[5,768,256]{2,1,0:T(8,128)(2,1)S(1)} %get-tuple-element.30.far_weights, f32[16,256]{1,0:T(8,128)S(1)} %get-tuple-element.31.far_stats, ...), custom_call_target="tpu_custom_call" | custom-call | bytes 1024 | tf_op jit(solution)/shard_map/pallas_call | solution.py:53
  23.0 5.0 %collective-permute-start.7 = (bf16[656,256]{1,0:T(8,128)(2,1)S(1)}, bf16[656,256]{1,0:T(8,128)(2,1)S(1)}, u32[]{:S(2)}, u32[]{:S(2)}) collective-permute-start(bf16[656,256]{1,0:T(8,128)(2,1)S(1)} %shard_map.60), channel_id=1, source_target_pairs={{0,60},{4,0},{8,4},{12,8},{16,12},{20,16},{24,20},{28,24},{32,28},... | collective-permute-start | bytes 1007624 | tf_op jit(solution)/shard_map/ppermute | solution.py:32
  28.0 0.0 copy-start.2
  28.0 1.0 %copy-done.2 = bf16[256,640]{1,0:T(8,128)(2,1)S(1)} copy-done((bf16[256,640]{1,0:T(8,128)(2,1)S(1)}, bf16[256,640]{1,0:T(8,128)(2,1)}, u32[]{:S(2)}) %copy-start.2) | copy-done | bytes 327704
  29.0 1.3 %shard_map.61 = (bf16[5,768,256]{2,1,0:T(8,128)(2,1)S(1)}, f32[16,256]{1,0:T(8,128)S(1)}) custom-call(bf16[256,640]{1,0:T(8,128)(2,1)S(1)} %collective-permute-done.key_far.refs_0_, bf16[256,640]{1,0:T(8,128)(2,1)S(1)} %collective-permute-done.1.key_near.refs_1_, bf16[256,640]{1,0:T(8,128)(2,1)S(1)} %copy-done.2, bf16[256,640]{1,0:T(8,128)(2,1)S(1)} %copy-done, ...), custom_call_target="tpu_custom_call" | custom-call | bytes 1024 | tf_op jit(solution)/shard_map/pallas_call | solution.py:53
  30.3 0.5 %shard_map.62.own = f32[640,256]{1,0:T(8,128)S(1)} custom-call(bf16[5,768,256]{2,1,0:T(8,128)(2,1)S(1)} %get-tuple-element.33.weights, f32[16,256]{1,0:T(8,128)S(1)} %get-tuple-element.34.stats, bf16[256,640]{1,0:T(8,128)(2,1)S(1)} %copy-done.1, bf16[256,640]{1,0:T(8,128)(2,1)S(1)} %collective-permute-done.5.v_near, ...), custom_call_target="tpu_custom_call" | custom-call | bytes 1024 | tf_op jit(solution)/shard_map/pallas_call | solution.py:53
  30.8 2.9 %collective-permute-done.6.last = bf16[656,256]{1,0:T(8,128)(2,1)S(1)} collective-permute-done((bf16[656,256]{1,0:T(8,128)(2,1)S(1)}, bf16[656,256]{1,0:T(8,128)(2,1)S(1)}, u32[]{:S(2)}, u32[]{:S(2)}) %collective-permute-start.6) | collective-permute-done | bytes 335904 | tf_op jit(solution)/shard_map/ppermute | solution.py:32
  33.7 0.0 collective-permute-done.7.other
  33.7 1.0 %shard_map.63 = bf16[256,640]{1,0:T(8,128)(2,1)} custom-call(f32[640,256]{1,0:T(8,128)S(1)} %shard_map.62.own, f32[16,256]{1,0:T(8,128)S(1)} %get-tuple-element.34.stats, bf16[656,256]{1,0:T(8,128)(2,1)S(1)} %collective-permute-done.6.last, bf16[656,256]{1,0:T(8,128)(2,1)S(1)} %collective-permute-done.7.other), custom_call_target="tpu_custom_call" | custom-call | bytes 1024 | tf_op jit(solution)/shard_map/pallas_call | solution.py:267
  (8 shorter events, 0.1 us)
Async XLA Ops:
  0.0 15.8 %copy-start = (bf16[256,640]{1,0:T(8,128)(2,1)S(1)}, bf16[256,640]{1,0:T(8,128)(2,1)}, u32[]{:S(2)}) copy-start(bf16[256,640]{1,0:T(8,128)(2,1)} %key.3) | copy-start | bytes 983044
  0.0 10.3 %collective-permute-start.1 = (bf16[256,640]{1,0:T(8,128)(2,1)}, bf16[256,640]{1,0:T(8,128)(2,1)S(1)}, u32[]{:S(2)}, u32[]{:S(2)}) collective-permute-start(bf16[256,640]{1,0:T(8,128)(2,1)} %key.3), channel_id=1, source_target_pairs={{0,1},{1,0},{2,3},{3,2},{4,5},{5,4},{6,7},{7,6},{8,9},{9,8},{10,11... | collective-permute-start | bytes 983048 | tf_op jit(solution)/shard_map/ppermute | solution.py:27
  0.8 12.7 %collective-permute-start = (bf16[256,640]{1,0:T(8,128)(2,1)}, bf16[256,640]{1,0:T(8,128)(2,1)S(1)}, u32[]{:S(2)}, u32[]{:S(2)}) collective-permute-start(bf16[256,640]{1,0:T(8,128)(2,1)} %key.3), channel_id=1, source_target_pairs={{0,64},{1,2},{2,1},{3,67},{64,0},{65,66},{66,65},{67,3},{128,192},... | collective-permute-start | bytes 983048 | tf_op jit(solution)/shard_map/ppermute | solution.py:45
  0.8 14.9 %collective-permute-start.2 = (bf16[256,640]{1,0:T(8,128)(2,1)}, bf16[256,640]{1,0:T(8,128)(2,1)S(1)}, u32[]{:S(2)}, u32[]{:S(2)}) collective-permute-start(bf16[256,640]{1,0:T(8,128)(2,1)} %q.1), channel_id=1, source_target_pairs={{0,4},{4,0},{8,12},{12,8},{16,20},{20,16},{24,28},{28,24},{32,36},... | collective-permute-start | bytes 983048 | tf_op jit(solution)/shard_map/ppermute | solution.py:27
  2.8 15.9 %collective-permute-start.3 = (bf16[256,640]{1,0:T(8,128)(2,1)}, bf16[256,640]{1,0:T(8,128)(2,1)S(1)}, u32[]{:S(2)}, u32[]{:S(2)}) collective-permute-start(bf16[256,640]{1,0:T(8,128)(2,1)} %q.1), channel_id=1, source_target_pairs={{0,60},{4,8},{8,4},{12,16},{16,12},{20,24},{24,20},{28,32},{32,28}... | collective-permute-start | bytes 983048 | tf_op jit(solution)/shard_map/ppermute | solution.py:27
  10.3 8.3 %collective-permute-start.4 = (bf16[256,640]{1,0:T(8,128)(2,1)}, bf16[256,640]{1,0:T(8,128)(2,1)S(1)}, u32[]{:S(2)}, u32[]{:S(2)}) collective-permute-start(bf16[256,640]{1,0:T(8,128)(2,1)} %v.5), channel_id=1, source_target_pairs={{0,64},{1,2},{2,1},{3,67},{64,0},{65,66},{66,65},{67,3},{128,192},... | collective-permute-start | bytes 983048 | tf_op jit(solution)/shard_map/ppermute | solution.py:45
  10.3 10.3 %collective-permute-start.5 = (bf16[256,640]{1,0:T(8,128)(2,1)}, bf16[256,640]{1,0:T(8,128)(2,1)S(1)}, u32[]{:S(2)}, u32[]{:S(2)}) collective-permute-start(bf16[256,640]{1,0:T(8,128)(2,1)} %v.5), channel_id=1, source_target_pairs={{0,1},{1,0},{2,3},{3,2},{4,5},{5,4},{6,7},{7,6},{8,9},{9,8},{10,11... | collective-permute-start | bytes 983048 | tf_op jit(solution)/shard_map/ppermute | solution.py:27
  15.7 3.0 %copy-start.1 = (bf16[256,640]{1,0:T(8,128)(2,1)S(1)}, bf16[256,640]{1,0:T(8,128)(2,1)}, u32[]{:S(2)}) copy-start(bf16[256,640]{1,0:T(8,128)(2,1)} %v.5) | copy-start | bytes 983044
  21.0 12.7 %collective-permute-start.6 = (bf16[656,256]{1,0:T(8,128)(2,1)S(1)}, bf16[656,256]{1,0:T(8,128)(2,1)S(1)}, u32[]{:S(2)}, u32[]{:S(2)}) collective-permute-start(bf16[656,256]{1,0:T(8,128)(2,1)S(1)} %shard_map.58), channel_id=1, source_target_pairs={{0,4},{4,8},{8,12},{12,16},{16,20},{20,24},{24,28},{28,32},{32,36}... | collective-permute-start | bytes 1007624 | tf_op jit(solution)/shard_map/ppermute | solution.py:32
  23.0 10.7 %collective-permute-start.7 = (bf16[656,256]{1,0:T(8,128)(2,1)S(1)}, bf16[656,256]{1,0:T(8,128)(2,1)S(1)}, u32[]{:S(2)}, u32[]{:S(2)}) collective-permute-start(bf16[656,256]{1,0:T(8,128)(2,1)S(1)} %shard_map.60), channel_id=1, source_target_pairs={{0,60},{4,0},{8,4},{12,8},{16,12},{20,16},{24,20},{28,24},{32,28},... | collective-permute-start | bytes 1007624 | tf_op jit(solution)/shard_map/ppermute | solution.py:32
  28.0 1.0 %copy-start.2 = (bf16[256,640]{1,0:T(8,128)(2,1)S(1)}, bf16[256,640]{1,0:T(8,128)(2,1)}, u32[]{:S(2)}) copy-start(bf16[256,640]{1,0:T(8,128)(2,1)} %q.1) | copy-start | bytes 983044

commit v10 on v9

--- a/solution.py
+++ b/solution.py
@@ -123,17 +123,17 @@
     out[end : end + SPARE, :] = jnp.concatenate(pieces, axis=0).astype(jnp.bfloat16)
 
 
-def early_kernel(heads, side, near_weights, far_weights, v, v_far, out):
+def early_kernel(heads, side, near_weights, far_weights, v, v_near, out):
     def body(weights):
         for h in range(heads):
-            out[h * HEAD : (h + 1) * HEAD, :] = weighted(h, weights, v, 0) + weighted(h, weights, v_far, 2)
+            out[h * HEAD : (h + 1) * HEAD, :] = weighted(h, weights, v, 0) + weighted(h, weights, v_near, 1)
 
     by_side(side, body, (near_weights,), (far_weights,))
 
 
-def finish_kernel(heads, side, near_weights, near_stats, far_weights, far_stats, early, v_near, out):
+def finish_kernel(heads, side, near_weights, near_stats, far_weights, far_stats, early, v_far, out):
     def body(weights, stats):
-        store(heads, out, stats, lambda h, rows: early[rows, :] + weighted(h, weights, v_near, 1))
+        store(heads, out, stats, lambda h, rows: early[rows, :] + weighted(h, weights, v_far, 2))
 
     by_side(side, body, (near_weights, near_stats), (far_weights, far_stats))
 
@@ -221,8 +221,8 @@
     sent = after(query, mark)
     q_near = exchange(query, "space", NEAR)
     q_far = exchange(sent, "space", FAR)
-    v_far = swap_slabs(value)
-    v_near = exchange(after(value, k_near), "tm", NEAR)
+    v_near = exchange(value, "tm", NEAR)
+    v_far = swap_slabs(after(value, k_near))
     bias = tile_bias(after(tile_coords, k_far), windows, rows // TILE, k_near)
 
     def weigh(kernel, q, table):
@@ -244,11 +244,11 @@
     back = jax.ShapeDtypeStruct((width + SPARE, rows), bf16)
     early = call(
         functools.partial(early_kernel, heads, 0), jax.ShapeDtypeStruct((width, rows), f32), 0,
-        near_weights, odd_weights, value, v_far,
+        near_weights, odd_weights, value, v_near,
     )
     to_next = call(
         functools.partial(finish_kernel, heads, 0), back, 0,
-        near_weights, near_stats, odd_weights, odd_stats, early, v_near,
+        near_weights, near_stats, odd_weights, odd_stats, early, v_far,
     )
     even_weights, even_stats = weigh(
         functools.partial(weigh_if_kernel, heads, 0), q_far, after(bias[2], to_next)

time: 34.8 us -> 34.8 us (level)
  starting transfers between devices: 18.6 us -> 15.9 us
  waiting for transfers between devices: 5.99 us -> 8.67 us
    ppermute x4, starting transfers between devices: 13.5 us -> 11.5 us  [exchange(): lax.ppermute(block, axis, [(i, partner(i, side, count)) for i in range(co...]
    ppermute x4, waiting for transfers between devices: 3.12 us -> 4.98 us  [exchange(): lax.ppermute(block, axis, [(i, partner(i, side, count)) for i in range(co...]
    ppermute x2, waiting for transfers between devices: 2.87 us -> 3.69 us  [shift(): lax.ppermute(block, axis, [(i, (i + distance) % count) for i in range(cou...]
    ppermute x2, starting transfers between devices: 5.09 us -> 4.41 us  [shift(): lax.ppermute(block, axis, [(i, (i + distance) % count) for i in range(cou...]
where the time goes in v10:
time: 34.8 us; the launch traced here: 34.6 us
  starting transfers between devices  15.9 us (46%)
  waiting for transfers between devices  8.67 us (25%)
  Pallas kernels  6.72 us (19%)
  local copies, waits for them, and re-layouts  2.11 us (6%)
  other arithmetic  1.04 us (3%)
    ppermute x4, starting transfers between devices, exchange(): lax.ppermute(block, axis, [(i, partner(i, side, count)) for i in range(co...  11.5 us
    pallas_call x8, Pallas kernels, call(): pl.pallas_call(kernel, out_shape=out_shape, compiler_params=pltpu.Compile...  5.77 us
    ppermute x4, waiting for transfers between devices, exchange(): lax.ppermute(block, axis, [(i, partner(i, side, count)) for i in range(co...  4.98 us
    ppermute x2, starting transfers between devices, shift(): lax.ppermute(block, axis, [(i, (i + distance) % count) for i in range(cou...  4.41 us
    ppermute x2, waiting for transfers between devices, shift(): lax.ppermute(block, axis, [(i, (i + distance) % count) for i in range(cou...  3.69 us
    unnamed x6, local copies, waits for them, and re-layouts  0.98 us
    pallas_call x1, Pallas kernels, shards(): pl.pallas_call(functools.partial(combine_kernel, heads), out_shape=jax.Sh...  0.96 us
    another operation x1, local copies, waits for them, and re-layouts, tile_bias(): queries = jnp.stack([tiles(column, t) for column in columns], axis=1)  0.92 us
  transfers between devices with their start and end apart: 8, of which 3 were waited for; matrix products, arithmetic and copies ran while one was open for 6% of the time, Pallas kernels for 16%

profile of v10, /device:TPU:6, one launch (start us, length us, event | category | flops | bytes accessed | tf_op | source)
XLA Modules:
  0.0 34.6 jit_solution(7346838436947908417)
XLA Ops:
  0.0 0.0 copy-start
  0.0 0.8 %collective-permute-start.1 = (bf16[256,640]{1,0:T(8,128)(2,1)}, bf16[256,640]{1,0:T(8,128)(2,1)S(1)}, u32[]{:S(2)}, u32[]{:S(2)}) collective-permute-start(bf16[256,640]{1,0:T(8,128)(2,1)} %key.3), channel_id=1, source_target_pairs={{0,1},{1,0},{2,3},{3,2},{4,5},{5,4},{6,7},{7,6},{8,9},{9,8},{10,11... | collective-permute-start | bytes 983048 | tf_op jit(solution)/shard_map/ppermute | solution.py:27
  0.8 0.0 collective-permute-start
  0.8 1.9 %collective-permute-start.2 = (bf16[256,640]{1,0:T(8,128)(2,1)}, bf16[256,640]{1,0:T(8,128)(2,1)S(1)}, u32[]{:S(2)}, u32[]{:S(2)}) collective-permute-start(bf16[256,640]{1,0:T(8,128)(2,1)} %q.1), channel_id=1, source_target_pairs={{0,4},{4,0},{8,12},{12,8},{16,20},{20,16},{24,28},{28,24},{32,36},... | collective-permute-start | bytes 983048 | tf_op jit(solution)/shard_map/ppermute | solution.py:27
  2.8 7.6 %collective-permute-start.3 = (bf16[256,640]{1,0:T(8,128)(2,1)}, bf16[256,640]{1,0:T(8,128)(2,1)S(1)}, u32[]{:S(2)}, u32[]{:S(2)}) collective-permute-start(bf16[256,640]{1,0:T(8,128)(2,1)} %q.1), channel_id=1, source_target_pairs={{0,60},{4,8},{8,4},{12,16},{16,12},{20,24},{24,20},{28,32},{32,28}... | collective-permute-start | bytes 983048 | tf_op jit(solution)/shard_map/ppermute | solution.py:27
  10.3 1.2 %collective-permute-start.4 = (bf16[256,640]{1,0:T(8,128)(2,1)}, bf16[256,640]{1,0:T(8,128)(2,1)S(1)}, u32[]{:S(2)}, u32[]{:S(2)}) collective-permute-start(bf16[256,640]{1,0:T(8,128)(2,1)} %v.5), channel_id=1, source_target_pairs={{0,1},{1,0},{2,3},{3,2},{4,5},{5,4},{6,7},{7,6},{8,9},{9,8},{10,11... | collective-permute-start | bytes 983048 | tf_op jit(solution)/shard_map/ppermute | solution.py:27
  11.5 0.0 collective-permute-done.1.key_near.refs_1_
  11.5 0.0 collective-permute-start.5
  11.5 0.0 collective-permute-done.key_far.refs_0_
  11.5 0.9 %dynamic-slice_bitcast_fusion.1 = (s32[3,1,4]{2,0,1:T(4,128)S(1)}, s32[3,1,4]{2,0,1:T(4,128)S(1)}, s32[3,4]{1,0:T(4,128)S(1)}, s32[3,4]{1,0:T(4,128)S(1)}, s32[3,4]{1,0:T(4,128)S(1)}) fusion(s32[3,256]{1,0:T(4,128)} %param.8, s32[]{:T(128)S(6)} %select_n.59, s32[]{:T(128)S(6)} %select_n.61, s32[]{:T(128)S(6)} %select_n.56, s32[]{:T(128)S(6)} %select_n.54, ...), kind=kLoop, calls=%fused_computation.6 | loop fusion | bytes 500 | tf_op jit(solution)/shard_map/stack | solution.py:202
  12.5 0.1 pad_add_fusion.1
  12.5 0.1 broadcast_in_dim.14
  12.6 0.1 sub.30
  12.7 0.1 subtract_abs_fusion
  12.8 0.8 %compare_reduce_fusion = pred[3,5,12,256]{3,2,1,0:T(8,128)(4,1)S(1)} fusion(s32[3,5]{1,0:T(4,128)} %param.9, s32[3,3,12,256]{3,2,1,0:T(8,128)S(1)} %subtract_abs_fusion), kind=kLoop, calls=%fused_computation | loop fusion | flops 230400 | bytes 156732 | tf_op jit(solution)/shard_map/reduce_and | solution.py:206
  13.7 0.0 copy-start.1
  13.8 0.0 collective-permute-done.2.q
  13.8 0.0 copy-done
  13.8 1.3 %shard_map.55 = (bf16[5,768,256]{2,1,0:T(8,128)(2,1)S(1)}, f32[16,256]{1,0:T(8,128)S(1)}) custom-call(bf16[256,640]{1,0:T(8,128)(2,1)S(1)} %collective-permute-done.key_far.refs_0_, bf16[256,640]{1,0:T(8,128)(2,1)S(1)} %collective-permute-done.1.key_near.refs_1_, bf16[256,640]{1,0:T(8,128)(2,1)S(1)} %collective-permute-done.2.q, ...), custom_call_target="tpu_custom_call" | custom-call | bytes 1024 | tf_op jit(solution)/shard_map/pallas_call | solution.py:53
  15.1 3.5 %collective-permute-done.3.refs_2_ = bf16[256,640]{1,0:T(8,128)(2,1)S(1)} collective-permute-done((bf16[256,640]{1,0:T(8,128)(2,1)}, bf16[256,640]{1,0:T(8,128)(2,1)S(1)}, u32[]{:S(2)}, u32[]{:S(2)}) %collective-permute-start.3) | collective-permute-done | bytes 327712 | tf_op jit(solution)/shard_map/ppermute | solution.py:27
  18.7 1.4 %collective-permute-done.4.v_near = bf16[256,640]{1,0:T(8,128)(2,1)S(1)} collective-permute-done((bf16[256,640]{1,0:T(8,128)(2,1)}, bf16[256,640]{1,0:T(8,128)(2,1)S(1)}, u32[]{:S(2)}, u32[]{:S(2)}) %collective-permute-start.4) | collective-permute-done | bytes 327712 | tf_op jit(solution)/shard_map/ppermute | solution.py:27
  20.1 0.0 copy-done.1
  20.1 0.4 %shard_map.57.early = f32[640,256]{1,0:T(8,128)S(1)} custom-call(bf16[5,768,256]{2,1,0:T(8,128)(2,1)S(1)} %get-tuple-element.23.near_weights, bf16[5,768,256]{2,1,0:T(8,128)(2,1)S(1)} %get-tuple-element.26.far_weights, bf16[256,640]{1,0:T(8,128)(2,1)S(1)} %copy-done.1, bf16[256,640]{1,0:T(8,128)(2,1)S(1)} %collective-permute-done.4.v_near), custom_call_target="tpu_custom_call" | custom-call | bytes 1024 | tf_op jit(solution)/shard_map/pallas_call | solution.py:53
  20.5 0.0 collective-permute-done.5.v_far
  20.5 0.3 shard_map.58
  20.9 0.1 collective-permute-start.6
  20.9 1.4 %shard_map.59 = (bf16[5,768,256]{2,1,0:T(8,128)(2,1)S(1)}, f32[16,256]{1,0:T(8,128)S(1)}) custom-call(bf16[256,640]{1,0:T(8,128)(2,1)S(1)} %collective-permute-done.key_far.refs_0_, bf16[256,640]{1,0:T(8,128)(2,1)S(1)} %collective-permute-done.1.key_near.refs_1_, bf16[256,640]{1,0:T(8,128)(2,1)S(1)} %collective-permute-done.3.refs_2_, ...), custom_call_target="tpu_custom_call" | custom-call | bytes 1024 | tf_op jit(solution)/shard_map/pallas_call | solution.py:53
  22.3 0.5 %shard_map.60 = bf16[656,256]{1,0:T(8,128)(2,1)S(1)} custom-call(bf16[5,768,256]{2,1,0:T(8,128)(2,1)S(1)} %get-tuple-element.23.near_weights, f32[16,256]{1,0:T(8,128)S(1)} %get-tuple-element.24.near_stats, bf16[5,768,256]{2,1,0:T(8,128)(2,1)S(1)} %get-tuple-element.30.far_weights, f32[16,256]{1,0:T(8,128)S(1)} %get-tuple-element.31.far_stats, ...), custom_call_target="tpu_custom_call" | custom-call | bytes 1024 | tf_op jit(solution)/shard_map/pallas_call | solution.py:53
  22.8 4.3 %collective-permute-start.7 = (bf16[656,256]{1,0:T(8,128)(2,1)S(1)}, bf16[656,256]{1,0:T(8,128)(2,1)S(1)}, u32[]{:S(2)}, u32[]{:S(2)}) collective-permute-start(bf16[656,256]{1,0:T(8,128)(2,1)S(1)} %shard_map.60), channel_id=1, source_target_pairs={{0,60},{4,0},{8,4},{12,8},{16,12},{20,16},{24,20},{28,24},{32,28},... | collective-permute-start | bytes 1007624 | tf_op jit(solution)/shard_map/ppermute | solution.py:32
  27.2 0.0 copy-start.2
  27.2 1.0 %copy-done.2 = bf16[256,640]{1,0:T(8,128)(2,1)S(1)} copy-done((bf16[256,640]{1,0:T(8,128)(2,1)S(1)}, bf16[256,640]{1,0:T(8,128)(2,1)}, u32[]{:S(2)}) %copy-start.2) | copy-done | bytes 327704
  28.2 1.3 %shard_map.61 = (bf16[5,768,256]{2,1,0:T(8,128)(2,1)S(1)}, f32[16,256]{1,0:T(8,128)S(1)}) custom-call(bf16[256,640]{1,0:T(8,128)(2,1)S(1)} %collective-permute-done.key_far.refs_0_, bf16[256,640]{1,0:T(8,128)(2,1)S(1)} %collective-permute-done.1.key_near.refs_1_, bf16[256,640]{1,0:T(8,128)(2,1)S(1)} %copy-done.2, bf16[256,640]{1,0:T(8,128)(2,1)S(1)} %copy-done, ...), custom_call_target="tpu_custom_call" | custom-call | bytes 1024 | tf_op jit(solution)/shard_map/pallas_call | solution.py:53
  29.5 0.5 %shard_map.62.own = f32[640,256]{1,0:T(8,128)S(1)} custom-call(bf16[5,768,256]{2,1,0:T(8,128)(2,1)S(1)} %get-tuple-element.33.weights, f32[16,256]{1,0:T(8,128)S(1)} %get-tuple-element.34.stats, bf16[256,640]{1,0:T(8,128)(2,1)S(1)} %copy-done.1, bf16[256,640]{1,0:T(8,128)(2,1)S(1)} %collective-permute-done.4.v_near, ...), custom_call_target="tpu_custom_call" | custom-call | bytes 1024 | tf_op jit(solution)/shard_map/pallas_call | solution.py:53
  30.0 3.7 %collective-permute-done.6.last = bf16[656,256]{1,0:T(8,128)(2,1)S(1)} collective-permute-done((bf16[656,256]{1,0:T(8,128)(2,1)S(1)}, bf16[656,256]{1,0:T(8,128)(2,1)S(1)}, u32[]{:S(2)}, u32[]{:S(2)}) %collective-permute-start.6) | collective-permute-done | bytes 335904 | tf_op jit(solution)/shard_map/ppermute | solution.py:32
  33.7 0.0 collective-permute-done.7.other
  33.7 1.0 %shard_map.63 = bf16[256,640]{1,0:T(8,128)(2,1)} custom-call(f32[640,256]{1,0:T(8,128)S(1)} %shard_map.62.own, f32[16,256]{1,0:T(8,128)S(1)} %get-tuple-element.34.stats, bf16[656,256]{1,0:T(8,128)(2,1)S(1)} %collective-permute-done.6.last, bf16[656,256]{1,0:T(8,128)(2,1)S(1)} %collective-permute-done.7.other), custom_call_target="tpu_custom_call" | custom-call | bytes 1024 | tf_op jit(solution)/shard_map/pallas_call | solution.py:267
  (8 shorter events, 0.1 us)
Async XLA Ops:
  0.0 13.8 %copy-start = (bf16[256,640]{1,0:T(8,128)(2,1)S(1)}, bf16[256,640]{1,0:T(8,128)(2,1)}, u32[]{:S(2)}) copy-start(bf16[256,640]{1,0:T(8,128)(2,1)} %key.3) | copy-start | bytes 983044
  0.0 11.5 %collective-permute-start.1 = (bf16[256,640]{1,0:T(8,128)(2,1)}, bf16[256,640]{1,0:T(8,128)(2,1)S(1)}, u32[]{:S(2)}, u32[]{:S(2)}) collective-permute-start(bf16[256,640]{1,0:T(8,128)(2,1)} %key.3), channel_id=1, source_target_pairs={{0,1},{1,0},{2,3},{3,2},{4,5},{5,4},{6,7},{7,6},{8,9},{9,8},{10,11... | collective-permute-start | bytes 983048 | tf_op jit(solution)/shard_map/ppermute | solution.py:27
  0.8 10.7 %collective-permute-start = (bf16[256,640]{1,0:T(8,128)(2,1)}, bf16[256,640]{1,0:T(8,128)(2,1)S(1)}, u32[]{:S(2)}, u32[]{:S(2)}) collective-permute-start(bf16[256,640]{1,0:T(8,128)(2,1)} %key.3), channel_id=1, source_target_pairs={{0,64},{1,2},{2,1},{3,67},{64,0},{65,66},{66,65},{67,3},{128,192},... | collective-permute-start | bytes 983048 | tf_op jit(solution)/shard_map/ppermute | solution.py:45
  0.8 12.9 %collective-permute-start.2 = (bf16[256,640]{1,0:T(8,128)(2,1)}, bf16[256,640]{1,0:T(8,128)(2,1)S(1)}, u32[]{:S(2)}, u32[]{:S(2)}) collective-permute-start(bf16[256,640]{1,0:T(8,128)(2,1)} %q.1), channel_id=1, source_target_pairs={{0,4},{4,0},{8,12},{12,8},{16,20},{20,16},{24,28},{28,24},{32,36},... | collective-permute-start | bytes 983048 | tf_op jit(solution)/shard_map/ppermute | solution.py:27
  2.8 15.9 %collective-permute-start.3 = (bf16[256,640]{1,0:T(8,128)(2,1)}, bf16[256,640]{1,0:T(8,128)(2,1)S(1)}, u32[]{:S(2)}, u32[]{:S(2)}) collective-permute-start(bf16[256,640]{1,0:T(8,128)(2,1)} %q.1), channel_id=1, source_target_pairs={{0,60},{4,8},{8,4},{12,16},{16,12},{20,24},{24,20},{28,32},{32,28}... | collective-permute-start | bytes 983048 | tf_op jit(solution)/shard_map/ppermute | solution.py:27
  10.3 9.8 %collective-permute-start.4 = (bf16[256,640]{1,0:T(8,128)(2,1)}, bf16[256,640]{1,0:T(8,128)(2,1)S(1)}, u32[]{:S(2)}, u32[]{:S(2)}) collective-permute-start(bf16[256,640]{1,0:T(8,128)(2,1)} %v.5), channel_id=1, source_target_pairs={{0,1},{1,0},{2,3},{3,2},{4,5},{5,4},{6,7},{7,6},{8,9},{9,8},{10,11... | collective-permute-start | bytes 983048 | tf_op jit(solution)/shard_map/ppermute | solution.py:27
  11.5 9.0 %collective-permute-start.5 = (bf16[256,640]{1,0:T(8,128)(2,1)}, bf16[256,640]{1,0:T(8,128)(2,1)S(1)}, u32[]{:S(2)}, u32[]{:S(2)}) collective-permute-start(bf16[256,640]{1,0:T(8,128)(2,1)} %v.5), channel_id=1, source_target_pairs={{0,64},{1,2},{2,1},{3,67},{64,0},{65,66},{66,65},{67,3},{128,192},... | collective-permute-start | bytes 983048 | tf_op jit(solution)/shard_map/ppermute | solution.py:45
  13.7 6.4 %copy-start.1 = (bf16[256,640]{1,0:T(8,128)(2,1)S(1)}, bf16[256,640]{1,0:T(8,128)(2,1)}, u32[]{:S(2)}) copy-start(bf16[256,640]{1,0:T(8,128)(2,1)} %v.5) | copy-start | bytes 983044
  20.9 12.8 %collective-permute-start.6 = (bf16[656,256]{1,0:T(8,128)(2,1)S(1)}, bf16[656,256]{1,0:T(8,128)(2,1)S(1)}, u32[]{:S(2)}, u32[]{:S(2)}) collective-permute-start(bf16[656,256]{1,0:T(8,128)(2,1)S(1)} %shard_map.58), channel_id=1, source_target_pairs={{0,4},{4,8},{8,12},{12,16},{16,20},{20,24},{24,28},{28,32},{32,36}... | collective-permute-start | bytes 1007624 | tf_op jit(solution)/shard_map/ppermute | solution.py:32
  22.8 10.8 %collective-permute-start.7 = (bf16[656,256]{1,0:T(8,128)(2,1)S(1)}, bf16[656,256]{1,0:T(8,128)(2,1)S(1)}, u32[]{:S(2)}, u32[]{:S(2)}) collective-permute-start(bf16[656,256]{1,0:T(8,128)(2,1)S(1)} %shard_map.60), channel_id=1, source_target_pairs={{0,60},{4,0},{8,4},{12,8},{16,12},{20,16},{24,20},{28,24},{32,28},... | collective-permute-start | bytes 1007624 | tf_op jit(solution)/shard_map/ppermute | solution.py:32
  27.2 1.0 %copy-start.2 = (bf16[256,640]{1,0:T(8,128)(2,1)S(1)}, bf16[256,640]{1,0:T(8,128)(2,1)}, u32[]{:S(2)}) copy-start(bf16[256,640]{1,0:T(8,128)(2,1)} %q.1) | copy-start | bytes 983044
